TPU v7x, 512 devices: a whole 4x4x16 slice. The times are simulated.
512 devices in a mesh: seqhi: 32 (over z, core), seqlo: 16 (over x, y).
Axes of the slice: x: 4, y: 4, z: 16, core: 2. Of those that a mesh axis runs over, the one named last changes fastest.
Arguments:
- queries: bfloat16 [65536, 1024], P(('seqhi', 'seqlo')), may hold values from -8 to 8
- key_rows: bfloat16 [65536, 1024], P(('seqhi', 'seqlo')), may hold values from -8 to 8
- value_rows: bfloat16 [65536, 1024], P(('seqhi', 'seqlo')), may hold values from -10 to 10
Outputs:
- attended: bfloat16 [65536, 1024], P(('seqhi', 'seqlo'))
All inputs are finite; a program needn't handle non-finite values.
Results may differ from a plain program's by a relative error of at most 0.012.
Values may be sent and summed in bfloat16 or wider, within the bound.
No kernel may reach another device: no remote copies, remote signals or barrier semaphores. Data moves between devices by JAX's collectives and lax.ppermute only.
A program may use at most 64 MiB of HBM per device.

v0:
```python
import math

import jax
import jax.numpy as jnp
from jax import lax
from jax.sharding import PartitionSpec as P

HEADS = 16
HEAD = 64
BLOCK = 128


floor_score = -1e30


def extended(cells, sides, width):
    for axis, dim in sides:
        count = lax.axis_size(axis)
        ends = count - 1
        head = lax.slice_in_dim(cells, 0, width, axis=dim)
        tail = lax.slice_in_dim(cells, cells.shape[dim] - width, cells.shape[dim], axis=dim)
        cells = jnp.concatenate(
            [
                lax.ppermute(tail, axis, [(i, (i + 1) % count) for i in range(ends)]),
                cells,
                lax.ppermute(head, axis, [((i + 1) % count, i) for i in range(ends)]),
            ],
            axis=dim,
        )
    return cells


def from_partner(block, axis, apart):
    count = lax.axis_size(axis)
    route = []
    for low in range(count):
        high = low | 1 << apart
        if high != low and high < count:
            route += [(low, high), (high, low)]
    return lax.ppermute(block, axis, route)


def shifted(value, axis, by):
    devices = lax.axis_size(axis)
    pairs = [(i, i + by) for i in range(devices) if 0 <= i + by < devices]
    return lax.ppermute(value, axis, pairs)


def coarsen(member):
    dims_in = member.shape
    paired = member.reshape(dims_in[:-2] + (dims_in[-2] // 2, 2, dims_in[-1])).astype(jnp.float32)
    return (0.5 * (paired[..., 0, :] + paired[..., 1, :])).astype(jnp.bfloat16)


def admit(row_ids, col_ids, height, row_count):
    allowed = (
        (col_ids >= 0) & (col_ids < row_count) & (jnp.abs(row_ids // BLOCK - col_ids // BLOCK) <= 1)
    )
    if height > 0:
        allowed = allowed & (jnp.abs(2 * row_ids // BLOCK - 2 * col_ids // BLOCK) > 1)
    return allowed


def attend(level_rows, key_block, value_block, allowed, weight):
    row_count = level_rows.shape[0]
    col_count = key_block.shape[0]
    q_heads = level_rows.reshape(row_count, HEADS, -1)
    k_heads = key_block.reshape(col_count, HEADS, -1)
    v_heads = value_block.reshape(col_count, HEADS, -1)
    scores = jnp.einsum("qhd,khd->hqk", q_heads, k_heads, preferred_element_type=jnp.float32) * (
        1.0 / math.sqrt(q_heads.shape[2])
    )
    scores = jnp.where(allowed[None], scores, floor_score)
    maxima = jnp.max(scores, axis=2)
    exp_terms = jnp.where(allowed[None], jnp.exp(scores - maxima[:, :, None]), 0.0)
    totals = weight * jnp.sum(exp_terms, axis=2)
    low_terms = exp_terms.astype(jnp.bfloat16)
    weighted = weight * jnp.einsum(
        "hqk,khd->qhd", low_terms, v_heads, preferred_element_type=jnp.float32
    )
    return (maxima, totals, weighted.reshape(row_count, -1))


def widen(scale_rows):
    return jnp.repeat(scale_rows.T, HEAD, axis=1)


def combine(left_terms, right_terms):
    maxima = jnp.maximum(left_terms[0], right_terms[0])
    scale_one = jnp.exp(left_terms[0] - maxima)
    scale_two = jnp.exp(right_terms[0] - maxima)
    return (
        maxima,
        left_terms[1] * scale_one + right_terms[1] * scale_two,
        left_terms[2] * widen(scale_one) + right_terms[2] * widen(scale_two),
    )


def spread(pieces, repeats):
    if repeats == 1:
        return pieces
    return (
        jnp.repeat(pieces[0], repeats, axis=1),
        jnp.repeat(pieces[1], repeats, axis=1),
        jnp.repeat(pieces[2], repeats, axis=0),
    )


def local_level(level_queries, padded, height, device_index, row_count):
    rows_here, row_width = level_queries.shape
    block_count = rows_here // BLOCK
    blocks_all = padded.reshape(2, block_count + 2, BLOCK, row_width)
    nearby = jnp.concatenate([blocks_all[:, :-2], blocks_all[:, 1:-1], blocks_all[:, 2:]], 2)
    anchor = device_index * rows_here
    row_ids = anchor + jnp.arange(rows_here, dtype=jnp.int32).reshape(block_count, BLOCK)
    col_ids = (
        anchor
        + BLOCK * (jnp.arange(block_count, dtype=jnp.int32)[:, None] - 1)
        + jnp.arange(3 * BLOCK, dtype=jnp.int32)[None, :]
    )
    allowed = admit(row_ids[:, :, None], col_ids[:, None, :], height, row_count)
    maxima, totals, weighted = jax.vmap(attend, in_axes=(0, 0, 0, 0, None))(
        level_queries.reshape(block_count, BLOCK, row_width),
        nearby[0],
        nearby[1],
        allowed,
        2.0**height,
    )
    head_count = maxima.shape[1]
    return (
        maxima.transpose(1, 0, 2).reshape(head_count, rows_here),
        totals.transpose(1, 0, 2).reshape(head_count, rows_here),
        weighted.reshape(rows_here, row_width),
    )


def body(queries, key_rows, value_rows):
    tok_here = queries.shape[0]
    devices_all = lax.axis_size(("seqhi", "seqlo"))
    device_index = lax.axis_index(("seqhi", "seqlo"))
    all_tokens = tok_here * devices_all
    height_count = (all_tokens // BLOCK).bit_length() - 1
    local_count = min((tok_here // BLOCK).bit_length(), height_count)
    level_pairs = jnp.stack([key_rows, value_rows])
    collected = []
    height = 0
    padded = extended(level_pairs, ((("seqhi", "seqlo"), 1),), BLOCK)
    pieces = local_level(queries, padded, height, device_index, all_tokens >> height)
    collected.append((pieces, tok_here >> height))
    block_queries = queries
    block_pairs = level_pairs
    for height in range(local_count, height_count):
        bit_number = height - local_count
        group_size = 2 << bit_number
        halves = coarsen(jnp.concatenate([block_queries[None], block_pairs], 0))
        partner = from_partner(halves, ("seqhi", "seqlo"), bit_number)
        upper_half = device_index >> bit_number & 1 == 1
        joined = jnp.where(
            upper_half, jnp.concatenate([partner, halves], 1), jnp.concatenate([halves, partner], 1)
        )
        block_queries = joined[0]
        block_pairs = joined[1:]
        row_count = all_tokens >> height
        own_count = max(tok_here >> height, 1)
        place_in = device_index % group_size * tok_here >> height
        own_queries = lax.dynamic_slice_in_dim(block_queries, place_in, own_count, 0)
        first_row = device_index * tok_here >> height
        own_ids = first_row + jnp.arange(own_count, dtype=jnp.int32)
        block_start = first_row // BLOCK * BLOCK
        offsets = jnp.arange(BLOCK, dtype=jnp.int32)
        weight = 2.0**height
        prior_pairs = shifted(block_pairs, ("seqhi", "seqlo"), group_size)
        later_pairs = shifted(block_pairs, ("seqhi", "seqlo"), -group_size)
        nearby = jnp.concatenate([prior_pairs, later_pairs], 1)
        col_ids = jnp.concatenate([block_start - BLOCK + offsets, block_start + BLOCK + offsets])
        allowed = admit(own_ids[:, None], col_ids[None, :], height, row_count)
        pieces = attend(own_queries, nearby[0], nearby[1], allowed, weight)
        collected.append((pieces, own_count))
    merged, merged_rows = collected[-1]
    for position in range(len(collected) - 2, -1, -1):
        pieces, finer_rows = collected[position]
        merged = combine(spread(merged, finer_rows // merged_rows), pieces)
        merged_rows = finer_rows
    maxima, totals, weighted = merged
    return (weighted / widen(totals)).astype(jnp.bfloat16)


def solution(mesh):
    placed = (P(("seqhi", "seqlo"), None), P(("seqhi", "seqlo"), None), P(("seqhi", "seqlo"), None))
    return jax.shard_map(
        body, mesh=mesh, in_specs=placed, out_specs=P(("seqhi", "seqlo"), None), check_vma=False
    )
```

profile of v0, /device:TPU:4, one launch (start us, length us, event | category | flops | bytes accessed | tf_op | source)
XLA Modules:
  0.0 408.9 jit_solution(9731880493703378985)
XLA Ops:
  1.9 3.5 collective-permute-start.24
  5.4 4.5 %collective-permute-start.25 = (bf16[2,128,1024]{2,1,0:T(8,128)(2,1)}, bf16[2,128,1024]{2,1,0:T(8,128)(2,1)}, u32[]{:S(2)}, u32[]{:S(2)}) collective-permute-start(bf16[2,128,1024]{2,1,0:T(8,128)(2,1)} %pad_maximum_fusion.2), channel_id=1, source_target_pairs={{1,0},{2,1},{3,2},{4,3},{5,4},{6,5},{7,6},{8,7},{9,8},{10,9},{11,1... | collective-permute-start | bytes 1572872 | tf_op jit(solution)/shard_map/ppermute | solution.py:26
  21.9 7.4 %collective-permute-done = bf16[3,64,1024]{2,1,0:T(8,128)(2,1)S(1)} collective-permute-done((bf16[3,64,1024]{2,1,0:T(8,128)(2,1)S(1)}, bf16[3,64,1024]{2,1,0:T(8,128)(2,1)S(1)}, u32[]{:S(2)}, u32[]{:S(2)}) %collective-permute-start) | collective-permute-done | bytes 393248 | tf_op jit(solution)/shard_map/ppermute | solution.py:40
  31.5 4.9 %collective-permute-start.22 = (bf16[2,128,1024]{2,1,0:T(8,128)(2,1)}, bf16[2,128,1024]{2,1,0:T(8,128)(2,1)}, u32[]{:S(2)}, u32[]{:S(2)}) collective-permute-start(bf16[2,128,1024]{2,1,0:T(8,128)(2,1)} %slice.264), channel_id=1, source_target_pairs={{0,2},{1,3},{2,4},{3,5},{4,6},{5,7},{6,8},{7,9},{8,10},{9,11},{10,... | collective-permute-start | bytes 1572872 | tf_op jit(solution)/shard_map/ppermute | solution.py:46
  36.4 3.6 collective-permute-start.23
  41.3 4.1 collective-permute-start.1
  56.5 11.8 %collective-permute-done.1 = bf16[3,64,1024]{2,1,0:T(8,128)(2,1)} collective-permute-done((bf16[3,64,1024]{2,1,0:T(8,128)(2,1)S(1)}, bf16[3,64,1024]{2,1,0:T(8,128)(2,1)}, u32[]{:S(2)}, u32[]{:S(2)}) %collective-permute-start.1) | collective-permute-done | bytes 393248 | tf_op jit(solution)/shard_map/ppermute | solution.py:40
  78.9 3.1 collective-permute-start.2
  87.0 10.5 %collective-permute-done.2 = bf16[3,64,1024]{2,1,0:T(8,128)(2,1)S(1)} collective-permute-done((bf16[3,64,1024]{2,1,0:T(8,128)(2,1)S(1)}, bf16[3,64,1024]{2,1,0:T(8,128)(2,1)S(1)}, u32[]{:S(2)}, u32[]{:S(2)}) %collective-permute-start.2) | collective-permute-done | bytes 393248 | tf_op jit(solution)/shard_map/ppermute | solution.py:40
  101.6 6.3 %collective-permute-start.19 = (bf16[2,128,1024]{2,1,0:T(8,128)(2,1)}, bf16[2,128,1024]{2,1,0:T(8,128)(2,1)}, u32[]{:S(2)}, u32[]{:S(2)}) collective-permute-start(bf16[2,128,1024]{2,1,0:T(8,128)(2,1)} %slice.256), channel_id=1, source_target_pairs={{8,0},{9,1},{10,2},{11,3},{12,4},{13,5},{14,6},{15,7},{16,8},{17,9... | collective-permute-start | bytes 1572872 | tf_op jit(solution)/shard_map/ppermute | solution.py:46
  117.5 13.1 %collective-permute-done.3 = bf16[3,64,1024]{2,1,0:T(8,128)(2,1)S(1)} collective-permute-done((bf16[3,64,1024]{2,1,0:T(8,128)(2,1)S(1)}, bf16[3,64,1024]{2,1,0:T(8,128)(2,1)S(1)}, u32[]{:S(2)}, u32[]{:S(2)}) %collective-permute-start.3) | collective-permute-done | bytes 393248 | tf_op jit(solution)/shard_map/ppermute | solution.py:40
  132.7 9.7 %collective-permute-start.16 = (bf16[2,128,1024]{2,1,0:T(8,128)(2,1)}, bf16[2,128,1024]{2,1,0:T(8,128)(2,1)}, u32[]{:S(2)}, u32[]{:S(2)}) collective-permute-start(bf16[2,128,1024]{2,1,0:T(8,128)(2,1)} %slice.252), channel_id=1, source_target_pairs={{0,16},{1,17},{2,18},{3,19},{4,20},{5,21},{6,22},{7,23},{8,24},{9,... | collective-permute-start | bytes 1572872 | tf_op jit(solution)/shard_map/ppermute | solution.py:46
  155.6 6.6 %collective-permute-start.14 = (bf16[2,128,1024]{2,1,0:T(8,128)(2,1)}, bf16[2,128,1024]{2,1,0:T(8,128)(2,1)}, u32[]{:S(2)}, u32[]{:S(2)}) collective-permute-start(bf16[2,128,1024]{2,1,0:T(8,128)(2,1)} %slice.248), channel_id=1, source_target_pairs={{0,32},{1,33},{2,34},{3,35},{4,36},{5,37},{6,38},{7,39},{8,40},{9,... | collective-permute-start | bytes 1572872 | tf_op jit(solution)/shard_map/ppermute | solution.py:46
  164.8 4.6 %collective-permute-start.5 = (bf16[3,64,1024]{2,1,0:T(8,128)(2,1)S(1)}, bf16[3,64,1024]{2,1,0:T(8,128)(2,1)S(1)}, u32[]{:S(2)}, u32[]{:S(2)}) collective-permute-start(bf16[3,64,1024]{2,1,0:T(8,128)(2,1)S(1)} %bitcast.216), channel_id=1, source_target_pairs={{0,32},{32,0},{1,33},{33,1},{2,34},{34,2},{3,35},{35,3},{4,36},{36... | collective-permute-start | bytes 1179656 | tf_op jit(solution)/shard_map/ppermute | solution.py:40
  176.8 9.6 %collective-permute-done.5 = bf16[3,64,1024]{2,1,0:T(8,128)(2,1)S(1)} collective-permute-done((bf16[3,64,1024]{2,1,0:T(8,128)(2,1)S(1)}, bf16[3,64,1024]{2,1,0:T(8,128)(2,1)S(1)}, u32[]{:S(2)}, u32[]{:S(2)}) %collective-permute-start.5) | collective-permute-done | bytes 393248 | tf_op jit(solution)/shard_map/ppermute | solution.py:40
  188.5 6.6 %collective-permute-start.12 = (bf16[2,128,1024]{2,1,0:T(8,128)(2,1)}, bf16[2,128,1024]{2,1,0:T(8,128)(2,1)}, u32[]{:S(2)}, u32[]{:S(2)}) collective-permute-start(bf16[2,128,1024]{2,1,0:T(8,128)(2,1)} %slice.244), channel_id=1, source_target_pairs={{0,64},{1,65},{2,66},{3,67},{4,68},{5,69},{6,70},{7,71},{8,72},{9,... | collective-permute-start | bytes 1572872 | tf_op jit(solution)/shard_map/ppermute | solution.py:46
  197.6 5.7 %collective-permute-start.6 = (bf16[3,64,1024]{2,1,0:T(8,128)(2,1)S(1)}, bf16[3,64,1024]{2,1,0:T(8,128)(2,1)S(1)}, u32[]{:S(2)}, u32[]{:S(2)}) collective-permute-start(bf16[3,64,1024]{2,1,0:T(8,128)(2,1)S(1)} %bitcast.218), channel_id=1, source_target_pairs={{0,64},{64,0},{1,65},{65,1},{2,66},{66,2},{3,67},{67,3},{4,68},{68... | collective-permute-start | bytes 1179656 | tf_op jit(solution)/shard_map/ppermute | solution.py:40
  210.7 27.1 %collective-permute-done.6 = bf16[3,64,1024]{2,1,0:T(8,128)(2,1)S(1)} collective-permute-done((bf16[3,64,1024]{2,1,0:T(8,128)(2,1)S(1)}, bf16[3,64,1024]{2,1,0:T(8,128)(2,1)S(1)}, u32[]{:S(2)}, u32[]{:S(2)}) %collective-permute-start.6) | collective-permute-done | bytes 393248 | tf_op jit(solution)/shard_map/ppermute | solution.py:40
  239.0 9.3 %collective-permute-start.10 = (bf16[2,128,1024]{2,1,0:T(8,128)(2,1)}, bf16[2,128,1024]{2,1,0:T(8,128)(2,1)}, u32[]{:S(2)}, u32[]{:S(2)}) collective-permute-start(bf16[2,128,1024]{2,1,0:T(8,128)(2,1)} %slice.240), channel_id=1, source_target_pairs={{0,128},{1,129},{2,130},{3,131},{4,132},{5,133},{6,134},{7,135},{8... | collective-permute-start | bytes 1572872 | tf_op jit(solution)/shard_map/ppermute | solution.py:46
  253.9 8.5 %collective-permute-start.7 = (bf16[3,64,1024]{2,1,0:T(8,128)(2,1)S(1)}, bf16[3,64,1024]{2,1,0:T(8,128)(2,1)S(1)}, u32[]{:S(2)}, u32[]{:S(2)}) collective-permute-start(bf16[3,64,1024]{2,1,0:T(8,128)(2,1)S(1)} %bitcast.226), channel_id=1, source_target_pairs={{0,128},{128,0},{1,129},{129,1},{2,130},{130,2},{3,131},{131,3},{4... | collective-permute-start | bytes 1179656 | tf_op jit(solution)/shard_map/ppermute | solution.py:40
  268.4 71.3 %collective-permute-done.7 = bf16[3,64,1024]{2,1,0:T(8,128)(2,1)S(1)} collective-permute-done((bf16[3,64,1024]{2,1,0:T(8,128)(2,1)S(1)}, bf16[3,64,1024]{2,1,0:T(8,128)(2,1)S(1)}, u32[]{:S(2)}, u32[]{:S(2)}) %collective-permute-start.7) | collective-permute-done | bytes 393248 | tf_op jit(solution)/shard_map/ppermute | solution.py:40
  340.1 8.1 %collective-permute-start.8 = (bf16[2,128,1024]{2,1,0:T(8,128)(2,1)S(1)}, bf16[2,128,1024]{2,1,0:T(8,128)(2,1)}, u32[]{:S(2)}, u32[]{:S(2)}) collective-permute-start(bf16[2,128,1024]{2,1,0:T(8,128)(2,1)S(1)} %slice.235), channel_id=1, source_target_pairs={{0,256},{1,257},{2,258},{3,259},{4,260},{5,261},{6,262},{7,263},{8... | collective-permute-start | bytes 1572872 | tf_op jit(solution)/shard_map/ppermute | solution.py:46
  355.1 20.8 %collective-permute-done.8 = bf16[2,128,1024]{2,1,0:T(8,128)(2,1)} collective-permute-done((bf16[2,128,1024]{2,1,0:T(8,128)(2,1)S(1)}, bf16[2,128,1024]{2,1,0:T(8,128)(2,1)}, u32[]{:S(2)}, u32[]{:S(2)}) %collective-permute-start.8) | collective-permute-done | bytes 524320 | tf_op jit(solution)/shard_map/ppermute | solution.py:46
  376.9 6.6 %collective-permute-done.9 = bf16[2,128,1024]{2,1,0:T(8,128)(2,1)} collective-permute-done((bf16[2,128,1024]{2,1,0:T(8,128)(2,1)S(1)}, bf16[2,128,1024]{2,1,0:T(8,128)(2,1)}, u32[]{:S(2)}, u32[]{:S(2)}) %collective-permute-start.9) | collective-permute-done | bytes 524320 | tf_op jit(solution)/shard_map/ppermute | solution.py:46
  (436 shorter events, 139.0 us)
Async XLA Ops:
  1.9 44.4 %collective-permute-start.24 = (bf16[2,128,1024]{2,1,0:T(8,128)(2,1)}, bf16[2,128,1024]{2,1,0:T(8,128)(2,1)}, u32[]{:S(2)}, u32[]{:S(2)}) collective-permute-start(bf16[2,128,1024]{2,1,0:T(8,128)(2,1)} %pad_maximum_fusion.2), channel_id=1, source_target_pairs={{0,1},{1,2},{2,3},{3,4},{4,5},{5,6},{6,7},{7,8},{8,9},{9,10},{10,1... | collective-permute-start | bytes 1572872 | tf_op jit(solution)/shard_map/ppermute | solution.py:24
  5.4 40.9 %collective-permute-start.25 = (bf16[2,128,1024]{2,1,0:T(8,128)(2,1)}, bf16[2,128,1024]{2,1,0:T(8,128)(2,1)}, u32[]{:S(2)}, u32[]{:S(2)}) collective-permute-start(bf16[2,128,1024]{2,1,0:T(8,128)(2,1)} %pad_maximum_fusion.2), channel_id=1, source_target_pairs={{1,0},{2,1},{3,2},{4,3},{5,4},{6,5},{7,6},{8,7},{9,8},{10,9},{11,1... | collective-permute-start | bytes 1572872 | tf_op jit(solution)/shard_map/ppermute | solution.py:26
  31.5 50.7 %collective-permute-start.22 = (bf16[2,128,1024]{2,1,0:T(8,128)(2,1)}, bf16[2,128,1024]{2,1,0:T(8,128)(2,1)}, u32[]{:S(2)}, u32[]{:S(2)}) collective-permute-start(bf16[2,128,1024]{2,1,0:T(8,128)(2,1)} %slice.264), channel_id=1, source_target_pairs={{0,2},{1,3},{2,4},{3,5},{4,6},{5,7},{6,8},{7,9},{8,10},{9,11},{10,... | collective-permute-start | bytes 1572872 | tf_op jit(solution)/shard_map/ppermute | solution.py:46
  36.4 46.8 %collective-permute-start.23 = (bf16[2,128,1024]{2,1,0:T(8,128)(2,1)}, bf16[2,128,1024]{2,1,0:T(8,128)(2,1)}, u32[]{:S(2)}, u32[]{:S(2)}) collective-permute-start(bf16[2,128,1024]{2,1,0:T(8,128)(2,1)} %slice.264), channel_id=1, source_target_pairs={{2,0},{3,1},{4,2},{5,3},{6,4},{7,5},{8,6},{9,7},{10,8},{11,9},{12,... | collective-permute-start | bytes 1572872 | tf_op jit(solution)/shard_map/ppermute | solution.py:46
  41.3 27.1 %collective-permute-start.1 = (bf16[3,64,1024]{2,1,0:T(8,128)(2,1)S(1)}, bf16[3,64,1024]{2,1,0:T(8,128)(2,1)}, u32[]{:S(2)}, u32[]{:S(2)}) collective-permute-start(bf16[3,64,1024]{2,1,0:T(8,128)(2,1)S(1)} %bitcast.214), channel_id=1, source_target_pairs={{0,2},{2,0},{1,3},{3,1},{4,6},{6,4},{5,7},{7,5},{8,10},{10,8},{9,1... | collective-permute-start | bytes 1179656 | tf_op jit(solution)/shard_map/ppermute | solution.py:40
  71.6 40.5 %collective-permute-start.20 = (bf16[2,128,1024]{2,1,0:T(8,128)(2,1)}, bf16[2,128,1024]{2,1,0:T(8,128)(2,1)}, u32[]{:S(2)}, u32[]{:S(2)}) collective-permute-start(bf16[2,128,1024]{2,1,0:T(8,128)(2,1)} %slice.260), channel_id=1, source_target_pairs={{0,4},{1,5},{2,6},{3,7},{4,8},{5,9},{6,10},{7,11},{8,12},{9,13},{1... | collective-permute-start | bytes 1572872 | tf_op jit(solution)/shard_map/ppermute | solution.py:46
  74.7 38.5 %collective-permute-start.21 = (bf16[2,128,1024]{2,1,0:T(8,128)(2,1)}, bf16[2,128,1024]{2,1,0:T(8,128)(2,1)}, u32[]{:S(2)}, u32[]{:S(2)}) collective-permute-start(bf16[2,128,1024]{2,1,0:T(8,128)(2,1)} %slice.260), channel_id=1, source_target_pairs={{4,0},{5,1},{6,2},{7,3},{8,4},{9,5},{10,6},{11,7},{12,8},{13,9},{1... | collective-permute-start | bytes 1572872 | tf_op jit(solution)/shard_map/ppermute | solution.py:46
  78.9 18.7 %collective-permute-start.2 = (bf16[3,64,1024]{2,1,0:T(8,128)(2,1)S(1)}, bf16[3,64,1024]{2,1,0:T(8,128)(2,1)S(1)}, u32[]{:S(2)}, u32[]{:S(2)}) collective-permute-start(bf16[3,64,1024]{2,1,0:T(8,128)(2,1)S(1)} %bitcast.220), channel_id=1, source_target_pairs={{0,4},{4,0},{1,5},{5,1},{2,6},{6,2},{3,7},{7,3},{8,12},{12,8},{9,1... | collective-permute-start | bytes 1179656 | tf_op jit(solution)/shard_map/ppermute | solution.py:40
  99.7 49.2 %collective-permute-start.18 = (bf16[2,128,1024]{2,1,0:T(8,128)(2,1)}, bf16[2,128,1024]{2,1,0:T(8,128)(2,1)}, u32[]{:S(2)}, u32[]{:S(2)}) collective-permute-start(bf16[2,128,1024]{2,1,0:T(8,128)(2,1)} %slice.256), channel_id=1, source_target_pairs={{0,8},{1,9},{2,10},{3,11},{4,12},{5,13},{6,14},{7,15},{8,16},{9,17... | collective-permute-start | bytes 1572872 | tf_op jit(solution)/shard_map/ppermute | solution.py:46
  101.6 48.4 %collective-permute-start.19 = (bf16[2,128,1024]{2,1,0:T(8,128)(2,1)}, bf16[2,128,1024]{2,1,0:T(8,128)(2,1)}, u32[]{:S(2)}, u32[]{:S(2)}) collective-permute-start(bf16[2,128,1024]{2,1,0:T(8,128)(2,1)} %slice.256), channel_id=1, source_target_pairs={{8,0},{9,1},{10,2},{11,3},{12,4},{13,5},{14,6},{15,7},{16,8},{17,9... | collective-permute-start | bytes 1572872 | tf_op jit(solution)/shard_map/ppermute | solution.py:46
  109.2 21.4 %collective-permute-start.3 = (bf16[3,64,1024]{2,1,0:T(8,128)(2,1)S(1)}, bf16[3,64,1024]{2,1,0:T(8,128)(2,1)S(1)}, u32[]{:S(2)}, u32[]{:S(2)}) collective-permute-start(bf16[3,64,1024]{2,1,0:T(8,128)(2,1)S(1)} %bitcast.222), channel_id=1, source_target_pairs={{0,8},{8,0},{1,9},{9,1},{2,10},{10,2},{3,11},{11,3},{4,12},{12,4},... | collective-permute-start | bytes 1179656 | tf_op jit(solution)/shard_map/ppermute | solution.py:40
  132.7 37.4 %collective-permute-start.16 = (bf16[2,128,1024]{2,1,0:T(8,128)(2,1)}, bf16[2,128,1024]{2,1,0:T(8,128)(2,1)}, u32[]{:S(2)}, u32[]{:S(2)}) collective-permute-start(bf16[2,128,1024]{2,1,0:T(8,128)(2,1)} %slice.252), channel_id=1, source_target_pairs={{0,16},{1,17},{2,18},{3,19},{4,20},{5,21},{6,22},{7,23},{8,24},{9,... | collective-permute-start | bytes 1572872 | tf_op jit(solution)/shard_map/ppermute | solution.py:46
  142.4 28.8 %collective-permute-start.17 = (bf16[2,128,1024]{2,1,0:T(8,128)(2,1)}, bf16[2,128,1024]{2,1,0:T(8,128)(2,1)}, u32[]{:S(2)}, u32[]{:S(2)}) collective-permute-start(bf16[2,128,1024]{2,1,0:T(8,128)(2,1)} %slice.252), channel_id=1, source_target_pairs={{16,0},{17,1},{18,2},{19,3},{20,4},{21,5},{22,6},{23,7},{24,8},{25... | collective-permute-start | bytes 1572872 | tf_op jit(solution)/shard_map/ppermute | solution.py:46
  155.6 48.4 %collective-permute-start.14 = (bf16[2,128,1024]{2,1,0:T(8,128)(2,1)}, bf16[2,128,1024]{2,1,0:T(8,128)(2,1)}, u32[]{:S(2)}, u32[]{:S(2)}) collective-permute-start(bf16[2,128,1024]{2,1,0:T(8,128)(2,1)} %slice.248), channel_id=1, source_target_pairs={{0,32},{1,33},{2,34},{3,35},{4,36},{5,37},{6,38},{7,39},{8,40},{9,... | collective-permute-start | bytes 1572872 | tf_op jit(solution)/shard_map/ppermute | solution.py:46
  162.3 42.9 %collective-permute-start.15 = (bf16[2,128,1024]{2,1,0:T(8,128)(2,1)}, bf16[2,128,1024]{2,1,0:T(8,128)(2,1)}, u32[]{:S(2)}, u32[]{:S(2)}) collective-permute-start(bf16[2,128,1024]{2,1,0:T(8,128)(2,1)} %slice.248), channel_id=1, source_target_pairs={{32,0},{33,1},{34,2},{35,3},{36,4},{37,5},{38,6},{39,7},{40,8},{41... | collective-permute-start | bytes 1572872 | tf_op jit(solution)/shard_map/ppermute | solution.py:46
  164.8 21.5 %collective-permute-start.5 = (bf16[3,64,1024]{2,1,0:T(8,128)(2,1)S(1)}, bf16[3,64,1024]{2,1,0:T(8,128)(2,1)S(1)}, u32[]{:S(2)}, u32[]{:S(2)}) collective-permute-start(bf16[3,64,1024]{2,1,0:T(8,128)(2,1)S(1)} %bitcast.216), channel_id=1, source_target_pairs={{0,32},{32,0},{1,33},{33,1},{2,34},{34,2},{3,35},{35,3},{4,36},{36... | collective-permute-start | bytes 1179656 | tf_op jit(solution)/shard_map/ppermute | solution.py:40
  188.5 73.9 %collective-permute-start.12 = (bf16[2,128,1024]{2,1,0:T(8,128)(2,1)}, bf16[2,128,1024]{2,1,0:T(8,128)(2,1)}, u32[]{:S(2)}, u32[]{:S(2)}) collective-permute-start(bf16[2,128,1024]{2,1,0:T(8,128)(2,1)} %slice.244), channel_id=1, source_target_pairs={{0,64},{1,65},{2,66},{3,67},{4,68},{5,69},{6,70},{7,71},{8,72},{9,... | collective-permute-start | bytes 1572872 | tf_op jit(solution)/shard_map/ppermute | solution.py:46
  195.1 68.4 %collective-permute-start.13 = (bf16[2,128,1024]{2,1,0:T(8,128)(2,1)}, bf16[2,128,1024]{2,1,0:T(8,128)(2,1)}, u32[]{:S(2)}, u32[]{:S(2)}) collective-permute-start(bf16[2,128,1024]{2,1,0:T(8,128)(2,1)} %slice.244), channel_id=1, source_target_pairs={{64,0},{65,1},{66,2},{67,3},{68,4},{69,5},{70,6},{71,7},{72,8},{73... | collective-permute-start | bytes 1572872 | tf_op jit(solution)/shard_map/ppermute | solution.py:46
  197.6 40.2 %collective-permute-start.6 = (bf16[3,64,1024]{2,1,0:T(8,128)(2,1)S(1)}, bf16[3,64,1024]{2,1,0:T(8,128)(2,1)S(1)}, u32[]{:S(2)}, u32[]{:S(2)}) collective-permute-start(bf16[3,64,1024]{2,1,0:T(8,128)(2,1)S(1)} %bitcast.218), channel_id=1, source_target_pairs={{0,64},{64,0},{1,65},{65,1},{2,66},{66,2},{3,67},{67,3},{4,68},{68... | collective-permute-start | bytes 1179656 | tf_op jit(solution)/shard_map/ppermute | solution.py:40
  239.0 111.3 %collective-permute-start.10 = (bf16[2,128,1024]{2,1,0:T(8,128)(2,1)}, bf16[2,128,1024]{2,1,0:T(8,128)(2,1)}, u32[]{:S(2)}, u32[]{:S(2)}) collective-permute-start(bf16[2,128,1024]{2,1,0:T(8,128)(2,1)} %slice.240), channel_id=1, source_target_pairs={{0,128},{1,129},{2,130},{3,131},{4,132},{5,133},{6,134},{7,135},{8... | collective-permute-start | bytes 1572872 | tf_op jit(solution)/shard_map/ppermute | solution.py:46
  248.3 103.0 %collective-permute-start.11 = (bf16[2,128,1024]{2,1,0:T(8,128)(2,1)}, bf16[2,128,1024]{2,1,0:T(8,128)(2,1)}, u32[]{:S(2)}, u32[]{:S(2)}) collective-permute-start(bf16[2,128,1024]{2,1,0:T(8,128)(2,1)} %slice.240), channel_id=1, source_target_pairs={{128,0},{129,1},{130,2},{131,3},{132,4},{133,5},{134,6},{135,7},{1... | collective-permute-start | bytes 1572872 | tf_op jit(solution)/shard_map/ppermute | solution.py:46
  253.9 85.8 %collective-permute-start.7 = (bf16[3,64,1024]{2,1,0:T(8,128)(2,1)S(1)}, bf16[3,64,1024]{2,1,0:T(8,128)(2,1)S(1)}, u32[]{:S(2)}, u32[]{:S(2)}) collective-permute-start(bf16[3,64,1024]{2,1,0:T(8,128)(2,1)S(1)} %bitcast.226), channel_id=1, source_target_pairs={{0,128},{128,0},{1,129},{129,1},{2,130},{130,2},{3,131},{131,3},{4... | collective-permute-start | bytes 1179656 | tf_op jit(solution)/shard_map/ppermute | solution.py:40
  340.1 35.8 %collective-permute-start.8 = (bf16[2,128,1024]{2,1,0:T(8,128)(2,1)S(1)}, bf16[2,128,1024]{2,1,0:T(8,128)(2,1)}, u32[]{:S(2)}, u32[]{:S(2)}) collective-permute-start(bf16[2,128,1024]{2,1,0:T(8,128)(2,1)S(1)} %slice.235), channel_id=1, source_target_pairs={{0,256},{1,257},{2,258},{3,259},{4,260},{5,261},{6,262},{7,263},{8... | collective-permute-start | bytes 1572872 | tf_op jit(solution)/shard_map/ppermute | solution.py:46
  348.2 35.3 %collective-permute-start.9 = (bf16[2,128,1024]{2,1,0:T(8,128)(2,1)S(1)}, bf16[2,128,1024]{2,1,0:T(8,128)(2,1)}, u32[]{:S(2)}, u32[]{:S(2)}) collective-permute-start(bf16[2,128,1024]{2,1,0:T(8,128)(2,1)S(1)} %slice.235), channel_id=1, source_target_pairs={{256,0},{257,1},{258,2},{259,3},{260,4},{261,5},{262,6},{263,7},{2... | collective-permute-start | bytes 1572872 | tf_op jit(solution)/shard_map/ppermute | solution.py:46
  (65 other events, 556.3 us)
where the time goes:
time: 417 us; the launch traced here: 409 us
  waiting for transfers between devices  178 us (43%)
  starting transfers between devices  111 us (27%)
  local copies, waits for them, and re-layouts  65.2 us (16%)
  other arithmetic  38.4 us (9%)
  matrix products  13.9 us (3%)
    ppermute x8, waiting for transfers between devices, from_partner(): return lax.ppermute(block, axis, route)  151 us
    ppermute x16, starting transfers between devices, shifted(): return lax.ppermute(value, axis, pairs)  69.6 us
    ppermute x8, starting transfers between devices, from_partner(): return lax.ppermute(block, axis, route)  33 us
    ppermute x16, waiting for transfers between devices, shifted(): return lax.ppermute(value, axis, pairs)  27.4 us
    unnamed x134, local copies, waits for them, and re-layouts  13.1 us
    slice x24, local copies, waits for them, and re-layouts, body(): pieces = attend(own_queries, nearby[0], nearby[1], allowed, weight)  9.47 us
    convert_element_type x8, other arithmetic, coarsen(): return (0.5 * (paired[..., 0, :] + paired[..., 1, :])).astype(jnp.bfloat16)  8.93 us
    concatenate x8, local copies, waits for them, and re-layouts, body(): nearby = jnp.concatenate([prior_pairs, later_pairs], 1)  8.62 us
  transfers between devices with their start and end apart: 26, of which 9 were waited for; matrix products, arithmetic and copies ran while one was open for 22% of the time, Pallas kernels for 0%

commit v1 on v0

v1 whole, which is shorter than its diff:
```python
import math

import jax
import jax.numpy as jnp
from jax import lax
from jax.experimental import pallas as pl
from jax.experimental.pallas import tpu as pltpu
from jax.sharding import PartitionSpec as P

HEADS = 16
HEAD = 64
BLOCK = 128
NEVER = -1e30
SCALE = math.log2(math.e) / math.sqrt(HEAD)
TILES = 16
OFFSET = {1: 0, 2: 8, 3: 12, 4: 14}
COUNT = {0: 16, 1: 8, 2: 4, 3: 2, 4: 1}
ROWS = 72
PACKED = {5: 0, 6: 64, 7: 96, 8: 112}

VMEM = pl.BlockSpec(memory_space=pltpu.VMEM)
SMEM = pl.BlockSpec(memory_space=pltpu.SMEM)
PARAMS = pltpu.CompilerParams(vmem_limit_bytes=48 * 1024 * 1024)


def iota(shape, dim):
    return lax.broadcasted_iota(jnp.int32, shape, dim)


def mm(a, b):
    return jnp.dot(a, b, preferred_element_type=jnp.float32)


def split_kernel(q_ref, k_ref, v_ref, out_ref):
    for pair in range(HEADS // 2):
        for place, ref in enumerate((q_ref, k_ref, v_ref)):
            turned = ref[:, 128 * pair : 128 * pair + 128].T
            out_ref[2 * pair, 64 * place : 64 * place + 64, :] = turned[:64]
            out_ref[2 * pair + 1, 64 * place : 64 * place + 64, :] = turned[64:]


def join_kernel(in_ref, out_ref):
    for pair in range(HEADS // 2):
        both = jnp.concatenate([in_ref[2 * pair], in_ref[2 * pair + 1]], axis=0)
        out_ref[:, 128 * pair : 128 * pair + 128] = both.T


def coarse_kernel(plane_ref, x_ref, tiles_ref, queries_ref, left_ref, right_ref, far_ref):
    plane = plane_ref[0]
    halve = jnp.where(iota((256, 128), 0) // 2 == iota((256, 128), 1), 0.5, 0.0).astype(jnp.bfloat16)
    finer = [x_ref[i] for i in range(TILES)]
    for level in range(1, 5):
        coarser = []
        for i in range(COUNT[level]):
            pair = jnp.concatenate([finer[2 * i], finer[2 * i + 1]], axis=1)
            tile = mm(pair, halve).astype(jnp.bfloat16)
            tiles_ref[OFFSET[level] + i] = tile
            coarser.append(tile)
        left_ref[level] = coarser[0][64:]
        right_ref[level] = coarser[-1][64:]
        finer = coarser
    left_ref[0] = x_ref[0, 64:]
    right_ref[0] = x_ref[TILES - 1, 64:]
    tile = finer[0]
    small = []
    for level in range(5, 9):
        tile = mm(tile, halve[:128]).astype(jnp.bfloat16)
        small.append(tile)
    lanes = iota((64, 128), 1)
    packed = small[0][:64].astype(jnp.float32)
    for level in range(6, 9):
        moved = pltpu.roll(small[level - 5][:64].astype(jnp.float32), PACKED[level], 1)
        packed = jnp.where(lanes >= PACKED[level], moved, packed)
    queries_ref[...] = packed.astype(jnp.bfloat16)
    ready = []
    for tile in small:
        keys = tile[64:128].astype(jnp.float32)
        values = pltpu.roll(tile[128:].astype(jnp.float32), 64, 1)
        ready.append(jnp.where(lanes < 64, keys, values).astype(jnp.bfloat16))
    for there in range(16):
        level = needed_level(plane, there)
        for at in range(5, 9):

            @pl.when(level == at)
            def _(there=there, at=at):
                far_ref[there] = ready[at - 5]


def needed_level(plane, there):
    level = jnp.int32(8)
    for at in (7, 6, 5):
        near = jnp.abs((plane >> (at - 5)) - (there >> (at - 5))) <= 1
        level = jnp.where(near, jnp.int32(at), level)
    return level


def softmax_parts(parts):
    top = parts[0].max(axis=0, keepdims=True)
    for part in parts[1:]:
        top = jnp.maximum(top, part.max(axis=0, keepdims=True))
    top = top * SCALE
    weights, total = [], None
    for part in parts:
        grown = jnp.exp2(part * SCALE - top)
        added = grown.sum(axis=0, keepdims=True)
        total = added if total is None else total + added
        weights.append(grown.astype(jnp.bfloat16))
    return top, total, weights


def near_tile(query, keys, values, bias=(None, None, None)):
    parts = []
    for key, add in zip(keys, bias):
        scores = mm(key, query)
        parts.append(scores if add is None else scores + add)
    top, total, weights = softmax_parts(parts)
    numer = mm(jnp.concatenate(values, axis=1), jnp.concatenate(weights, axis=0))
    return numer, top, total


def far_tile(query, keys, values, level, bias=(None, None)):
    scores = []
    for key, add in zip(keys, bias):
        part = mm(key, query)
        scores.append(part if add is None else part + add)
    lower = iota((64, 128), 1) < 64
    middle = jnp.where(lower, scores[1][:64], scores[0][64:])
    top, total, weights = softmax_parts([scores[0][:64], middle, scores[1][64:]])
    none = jnp.zeros_like(weights[1])
    spread = [weights[0], jnp.where(lower, none, weights[1]), jnp.where(lower, weights[1], none), weights[2]]
    numer = mm(jnp.concatenate(values, axis=1), jnp.concatenate(spread, axis=0))
    times = 2.0**level
    return numer * times, top, total * times


def put(ref, place, state):
    numer, top, total = state
    ref[place, :64] = numer
    ref[place, 64:65] = top
    ref[place, 65:66] = total


def get(ref, place):
    return ref[place, :64], ref[place, 64:65], ref[place, 65:66]


def merge(one, two):
    top = jnp.maximum(one[1], two[1])
    scale_one = jnp.exp2(one[1] - top)
    scale_two = jnp.exp2(two[1] - top)
    return one[0] * scale_one + two[0] * scale_two, top, one[2] * scale_one + two[2] * scale_two


def lanes_from(state, picks):
    wide = jnp.concatenate([picks] * 8, axis=0)
    both = jnp.concatenate([state[1], state[2], jnp.zeros((6, 128), jnp.float32)], axis=0)
    both = jnp.take_along_axis(both, picks, axis=1)
    return jnp.take_along_axis(state[0], wide, axis=1), both[0:1], both[1:2]


STATE_TILES = TILES + 8 + 4
STATE_AT = {0: 0, 1: 16, 2: 24}


def interior_kernel(x_ref, tiles_ref, state_ref):
    def tile(level, i):
        return x_ref.at[i] if level == 0 else tiles_ref.at[OFFSET[level] + i]

    for level in range(3):
        count = COUNT[level]
        turned = {}
        for i in range(count):
            if level == 0 or 1 <= i + 1 < count or 1 <= i - 1:
                turned[i] = tile(level, i)[64:128].T
        for i in range(1, count - 1):
            query = tile(level, i)[:64]
            at = (i - 1, i, i + 1) if level == 0 else (i - 1, i + 1)
            keys = [turned[n] for n in at]
            values = [tile(level, n)[128:] for n in at]
            state = near_tile(query, keys, values) if level == 0 else far_tile(query, keys, values, level)
            put(state_ref, STATE_AT[level] + i, state)


def edges_kernel(place_ref, x_ref, tiles_ref, before_ref, after_ref, inner_ref, state_ref):
    place = place_ref[0]
    last_place = place_ref[1]
    no_before = jnp.where(place == 0, jnp.float32(NEVER), jnp.float32(0.0))
    no_after = jnp.where(place == last_place, jnp.float32(NEVER), jnp.float32(0.0))
    lanes = iota((8, 128), 1)

    def tile(level, i):
        return x_ref.at[i] if level == 0 else tiles_ref.at[OFFSET[level] + i]

    def side(level, i):
        if i < 0:
            return before_ref[level, :64].T, before_ref[level, 64:], no_before
        if i >= COUNT[level]:
            return after_ref[level, :64].T, after_ref[level, 64:], no_after
        return tile(level, i)[64:128].T, tile(level, i)[128:], None

    coarser = None
    for level in (4, 3, 2, 1, 0):
        merged = []
        for i in range(COUNT[level]):
            if level < 3 and 0 < i < COUNT[level] - 1:
                state = get(inner_ref, STATE_AT[level] + i)
            else:
                at = (i - 1, i, i + 1) if level == 0 else (i - 1, i + 1)
                keys, values, bias = zip(*(side(level, n) for n in at))
                query = tile(level, i)[:64]
                if level == 0:
                    state = near_tile(query, keys, values, bias)
                else:
                    state = far_tile(query, keys, values, level, bias)
            if coarser is not None:
                picks = 64 * (i % 2) + lanes // 2
                state = merge(state, lanes_from(coarser[i // 2], picks))
            merged.append(state)
        coarser = merged
    for i in range(TILES):
        put(state_ref, i, coarser[i])


def final_kernel(place_ref, queries_ref, own_ref, other_ref, state_ref, out_ref, bias_ref):
    plane = place_ref[0] >> 1
    core = place_ref[0] & 1
    query = queries_ref[...]
    lane = iota((32, 128), 1)
    slot = iota((32, 128), 0)
    lane_level = jnp.where(lane < 64, 5, jnp.where(lane < 96, 6, jnp.where(lane < 112, 7, 8)))
    bias_ref[0] = jnp.full((32, 128), NEVER, jnp.float32)
    for level in (6, 7, 8):
        held = (lane_level == level) & (slot < (64 >> (level - 5)))
        bias_ref[level - 5] = jnp.where(held, 0.0, NEVER)

    pick = (iota((128, 512), 0) // 32 == iota((128, 512), 1) // 128) & (
        iota((128, 512), 0) % 32 == iota((128, 512), 1) % 128
    )
    pick = jnp.where(pick, 1.0, 0.0).astype(jnp.bfloat16)
    place_value = (iota((512, 128), 1) // 32 == iota((512, 128), 0) // 128) & (
        iota((512, 128), 1) % 32 + 64 == iota((512, 128), 0) % 128
    )
    place_value = jnp.where(place_value, 1.0, 0.0).astype(jnp.bfloat16)
    parts, values = [], []
    for ref in (own_ref, other_ref):
        for four in range(4):
            chunks = jnp.concatenate([ref[4 * four + n] for n in range(4)], axis=1)
            key = lax.dot_general(
                pick, chunks, (((1,), (1,)), ((), ())), preferred_element_type=jnp.float32
            ).astype(jnp.bfloat16)
            values.append(mm(chunks, place_value).astype(jnp.bfloat16))
            bias = [bias_ref[needed_level(plane, 4 * four + n) - 5] for n in range(4)]
            parts.append(mm(key, query) + jnp.concatenate(bias, axis=0))
    first_lanes = jnp.where(iota((1, 128), 1) < 64, 0.0, NEVER)
    for step in (-1, 1):
        there = plane + step
        held = (there >= 0) & (there < 16)
        at = jnp.clip(there, 0, 15)
        for mine, ref in ((True, own_ref), (False, other_ref)):
            source = core if mine else 1 - core
            apart = 2 * step + source - core
            keep = held & (jnp.abs(apart) >= 2)
            chunk = ref[at]
            turned = chunk.T
            parts.append(mm(turned[:64], query) + (first_lanes + jnp.where(keep, 0.0, NEVER)))
            values.append(chunk[:, 64:])
    top, total, weights = softmax_parts(parts)
    numer = mm(jnp.concatenate(values, axis=1), jnp.concatenate(weights, axis=0))
    row = lane_level[:1]
    times = jnp.where(row == 5, 32.0, jnp.where(row == 6, 64.0, jnp.where(row == 7, 128.0, 256.0)))
    packed = (numer * times, top, total * times)
    lanes = iota((8, 128), 1)
    state = packed
    for level in (6, 7, 8):
        picks = jnp.minimum(PACKED[level] + lanes // (1 << (level - 5)), 127)
        state = merge(state, lanes_from(packed, picks))
    for i in range(TILES):
        spread = lanes_from(state, 4 * i + lanes // 32)
        numer, _, total = merge(get(state_ref, i), spread)
        out_ref[i] = (numer / total).astype(jnp.bfloat16)


def cost(flops, moved, exps=0):
    return pl.CostEstimate(flops=flops, bytes_accessed=moved, transcendentals=exps)


def body(queries, key_rows, value_rows):
    bf16, f32 = jnp.bfloat16, jnp.float32
    outer = lax.axis_size("seqhi")
    place = lax.axis_index("seqhi").astype(jnp.int32)
    place_info = jnp.stack([place, jnp.int32(outer - 1)])
    shape = jax.ShapeDtypeStruct

    split = pl.pallas_call(
        split_kernel,
        out_shape=shape((HEADS, 192, 128), bf16),
        in_specs=[VMEM] * 3,
        out_specs=VMEM,
        compiler_params=PARAMS,
        cost_estimate=cost(1 << 22, 3 << 19),
    )(queries, key_rows, value_rows)
    tokens = lax.all_to_all(split, "seqlo", 0, 0)

    tiles, packed, to_left, to_right, far = pl.pallas_call(
        coarse_kernel,
        out_shape=(
            shape((15, 192, 128), bf16),
            shape((64, 128), bf16),
            shape((5, 128, 128), bf16),
            shape((5, 128, 128), bf16),
            shape((16, 64, 128), bf16),
        ),
        in_specs=[SMEM, VMEM],
        out_specs=(VMEM,) * 5,
        compiler_params=PARAMS,
        cost_estimate=cost(1 << 28, 2 << 20),
    )(place_info[:1] >> 1, tokens)

    planes = [[2 * z + core for z in range(outer // 2)] for core in range(2)]
    own = lax.all_to_all(far, "seqhi", 0, 0, axis_index_groups=planes)
    before = lax.ppermute(to_right, "seqhi", [(i, i + 1) for i in range(outer - 1)])
    after = lax.ppermute(to_left, "seqhi", [(i + 1, i) for i in range(outer - 1)])
    other = lax.ppermute(own, "seqhi", [(i, i ^ 1) for i in range(outer)])

    inner = pl.pallas_call(
        interior_kernel,
        out_shape=shape((STATE_TILES, ROWS, 128), f32),
        in_specs=[VMEM] * 2,
        out_specs=VMEM,
        compiler_params=PARAMS,
        cost_estimate=cost(1 << 32, 2 << 20, 1 << 20),
    )(tokens, tiles)
    local = pl.pallas_call(
        edges_kernel,
        out_shape=shape((TILES, ROWS, 128), f32),
        in_specs=[SMEM] + [VMEM] * 5,
        out_specs=VMEM,
        compiler_params=PARAMS,
        cost_estimate=cost(1 << 31, 2 << 20, 1 << 19),
    )(place_info, tokens, tiles, before, after, inner)
    out = pl.pallas_call(
        final_kernel,
        out_shape=shape((TILES, HEAD, 128), bf16),
        in_specs=[SMEM] + [VMEM] * 4,
        out_specs=VMEM,
        scratch_shapes=[pltpu.VMEM((4, 32, 128), f32)],
        compiler_params=PARAMS,
        cost_estimate=cost(1 << 30, 2 << 20, 1 << 18),
    )(place_info, packed, own, other, local)

    heads = lax.all_to_all(out, "seqlo", 0, 0)
    return pl.pallas_call(
        join_kernel,
        out_shape=shape((128, HEADS * HEAD), bf16),
        in_specs=[VMEM],
        out_specs=VMEM,
        compiler_params=PARAMS,
        cost_estimate=cost(1 << 22, 1 << 19),
    )(heads)


def solution(mesh):
    placed = P(("seqhi", "seqlo"), None)
    return jax.shard_map(body, mesh=mesh, in_specs=(placed,) * 3, out_specs=placed, check_vma=False)
```

time: 417 us -> 86.9 us (0.21)
  the two profiles are of different devices: /device:TPU:4 before, /device:TPU:1 now
where the time goes in v1:
time: 86.9 us; the launch traced here: 86.5 us
  starting transfers between devices  42.9 us (49%)
  waiting for transfers between devices  15.2 us (17%)
  Pallas kernels  13.9 us (16%)
  blocking collectives  11.4 us (13%)
  local copies, waits for them, and re-layouts  2.85 us (3%)
    all_to_all x1, starting transfers between devices, body(): own = lax.all_to_all(far, 'seqhi', 0, 0, axis_index_groups=planes)  17 us
    all_to_all x1, blocking collectives, body(): heads = lax.all_to_all(out, 'seqlo', 0, 0)  11.4 us
    all_to_all x1, waiting for transfers between devices, body(): tokens = lax.all_to_all(split, 'seqlo', 0, 0)  10.7 us
    ppermute x1, starting transfers between devices, body(): other = lax.ppermute(own, 'seqhi', [(i, i ^ 1) for i in range(outer)])  10.2 us
    all_to_all x1, starting transfers between devices, body(): tokens = lax.all_to_all(split, 'seqlo', 0, 0)  7.58 us
    ppermute x1, starting transfers between devices, body(): lax.ppermute(to_right, 'seqhi', [(i, i + 1) for i in range(outer - 1)])  6.24 us
    pallas_call x1, Pallas kernels, body(): pl.pallas_call(interior_kernel, out_shape=shape((STATE_TILES, ROWS, 128),...  4.78 us
    all_to_all x1, waiting for transfers between devices, body(): own = lax.all_to_all(far, 'seqhi', 0, 0, axis_index_groups=planes)  4.52 us
  transfers between devices with their start and end apart: 5, of which 2 were waited for; matrix products, arithmetic and copies ran while one was open for 0% of the time, Pallas kernels for 8%

profile of v1, /device:TPU:1, one launch (start us, length us, event | category | flops | bytes accessed | tf_op | source)
XLA Modules:
  0.0 86.5 jit_solution(18435060340581839775)
XLA Ops:
  0.0 0.0 copy-start
  0.0 0.9 %copy-done = bf16[128,1024]{1,0:T(8,128)(2,1)S(1)} copy-done((bf16[128,1024]{1,0:T(8,128)(2,1)S(1)}, bf16[128,1024]{1,0:T(8,128)(2,1)}, u32[]{:S(2)}) %copy-start) | copy-done | bytes 262168
  1.0 0.0 copy-start.1
  1.0 0.9 %copy-done.1 = bf16[128,1024]{1,0:T(8,128)(2,1)S(1)} copy-done((bf16[128,1024]{1,0:T(8,128)(2,1)S(1)}, bf16[128,1024]{1,0:T(8,128)(2,1)}, u32[]{:S(2)}) %copy-start.1) | copy-done | bytes 262168
  1.9 0.0 copy-start.2
  1.9 0.9 %copy-done.2 = bf16[128,1024]{1,0:T(8,128)(2,1)S(1)} copy-done((bf16[128,1024]{1,0:T(8,128)(2,1)S(1)}, bf16[128,1024]{1,0:T(8,128)(2,1)}, u32[]{:S(2)}) %copy-start.2) | copy-done | bytes 262168
  2.9 1.1 %shard_map.37 = bf16[16,192,128]{2,1,0:T(8,128)(2,1)} custom-call(bf16[128,1024]{1,0:T(8,128)(2,1)S(1)} %copy-done, bf16[128,1024]{1,0:T(8,128)(2,1)S(1)} %copy-done.1, bf16[128,1024]{1,0:T(8,128)(2,1)S(1)} %copy-done.2), custom_call_target="tpu_custom_call" | custom-call | flops 4194304 | bytes 1572864 | tf_op jit(solution)/shard_map/pallas_call | solution.py:294
  4.0 7.6 %all-to-all-start = ((bf16[16,192,128]{2,1,0:T(8,128)(2,1)}), bf16[16,192,128]{2,1,0:T(8,128)(2,1)S(1)}, u32[]{:S(2)}, u32[]{:S(2)}) async-start(bf16[16,192,128]{2,1,0:T(8,128)(2,1)} %shard_map.37), calls=%async_computation | async-start | bytes 1572864 | tf_op jit(solution)/shard_map/all_to_all | solution.py:302
  11.6 10.7 %all-to-all-done.x_ref = bf16[16,192,128]{2,1,0:T(8,128)(2,1)S(1)} async-done(((bf16[16,192,128]{2,1,0:T(8,128)(2,1)}), bf16[16,192,128]{2,1,0:T(8,128)(2,1)S(1)}, u32[]{:S(2)}, u32[]{:S(2)}) %all-to-all-start) | async-done | bytes 786464 | tf_op jit(solution)/shard_map/all_to_all | solution.py:302
  22.3 2.3 %shard_map.38 = (bf16[15,192,128]{2,1,0:T(8,128)(2,1)S(1)}, bf16[64,128]{1,0:T(8,128)(2,1)S(1)}, bf16[5,128,128]{2,1,0:T(8,128)(2,1)S(1)}, bf16[5,128,128]{2,1,0:T(8,128)(2,1)S(1)}, bf16[16,64,128]{2,1,0:T(8,128)(2,1)}) custom-call(s32[1]{0:T(128)S(6)} %shift_right_arithmetic.3.plane_ref, bf16[16,192,128]{2,1,0:T(8,128)(2,1)S(1)} %all-to-all-done.x_ref), custom_call_target="tpu_custom_call" | custom-call | flops 268435456 | bytes 2097152 | tf_op jit(solution)/shard_map/pallas_call | solution.py:304
  24.5 17.0 %all-to-all-start.1 = ((bf16[16,64,128]{2,1,0:T(8,128)(2,1)}), bf16[16,64,128]{2,1,0:T(8,128)(2,1)S(1)}, u32[]{:S(2)}, u32[]{:S(2)}) async-start(bf16[16,64,128]{2,1,0:T(8,128)(2,1)} %get-tuple-element.11), calls=%async_computation.1 | async-start | bytes 524288 | tf_op jit(solution)/shard_map/all_to_all | solution.py:320
  41.5 0.1 pad_add_fusion.place_ref
  41.6 6.2 %collective-permute-start.1 = (bf16[5,128,128]{2,1,0:T(8,128)(2,1)S(1)}, bf16[5,128,128]{2,1,0:T(8,128)(2,1)S(1)}, u32[]{:S(2)}, u32[]{:S(2)}) collective-permute-start(bf16[5,128,128]{2,1,0:T(8,128)(2,1)S(1)} %get-tuple-element.13), channel_id=1, source_target_pairs={{0,16},{16,32},{32,48},{48,64},{64,80},{80,96},{96,112},{112,128},... | collective-permute-start | bytes 491528 | tf_op jit(solution)/shard_map/ppermute | solution.py:321
  47.9 1.9 %collective-permute-start.2 = (bf16[5,128,128]{2,1,0:T(8,128)(2,1)S(1)}, bf16[5,128,128]{2,1,0:T(8,128)(2,1)S(1)}, u32[]{:S(2)}, u32[]{:S(2)}) collective-permute-start(bf16[5,128,128]{2,1,0:T(8,128)(2,1)S(1)} %get-tuple-element.14), channel_id=1, source_target_pairs={{16,0},{32,16},{48,32},{64,48},{80,64},{96,80},{112,96},{128,112},... | collective-permute-start | bytes 491528 | tf_op jit(solution)/shard_map/ppermute | solution.py:322
  49.8 4.5 %all-to-all-done.1.own_ref = bf16[16,64,128]{2,1,0:T(8,128)(2,1)S(1)} async-done(((bf16[16,64,128]{2,1,0:T(8,128)(2,1)}), bf16[16,64,128]{2,1,0:T(8,128)(2,1)S(1)}, u32[]{:S(2)}, u32[]{:S(2)}) %all-to-all-start.1) | async-done | bytes 262176 | tf_op jit(solution)/shard_map/all_to_all | solution.py:320
  54.3 10.2 %collective-permute-start = (bf16[16,64,128]{2,1,0:T(8,128)(2,1)S(1)}, bf16[16,64,128]{2,1,0:T(8,128)(2,1)S(1)}, u32[]{:S(2)}, u32[]{:S(2)}) collective-permute-start(bf16[16,64,128]{2,1,0:T(8,128)(2,1)S(1)} %all-to-all-done.1.own_ref), channel_id=1, source_target_pairs={{0,16},{16,0},{32,48},{48,32},{64,80},{80,64},{96,112},{112,96},{1... | collective-permute-start | bytes 786440 | tf_op jit(solution)/shard_map/ppermute | solution.py:323
  64.5 4.8 %shard_map.39.inner_ref = f32[28,72,128]{2,1,0:T(8,128)S(1)} custom-call(bf16[16,192,128]{2,1,0:T(8,128)(2,1)S(1)} %all-to-all-done.x_ref, bf16[15,192,128]{2,1,0:T(8,128)(2,1)S(1)} %get-tuple-element.12.tiles_ref), custom_call_target="tpu_custom_call" | custom-call | flops 4294967296 | bytes 2097152 | tf_op jit(solution)/shard_map/pallas_call | solution.py:325
  69.3 0.0 collective-permute-done.1.before_ref
  69.3 0.0 collective-permute-done.2.after_ref
  69.3 2.5 %shard_map.40.state_ref = f32[16,72,128]{2,1,0:T(8,128)S(1)} custom-call(s32[2]{0:T(128)S(1)} %pad_add_fusion.place_ref, bf16[16,192,128]{2,1,0:T(8,128)(2,1)S(1)} %all-to-all-done.x_ref, bf16[15,192,128]{2,1,0:T(8,128)(2,1)S(1)} %get-tuple-element.12.tiles_ref, bf16[5,128,128]{2,1,0:T(8,128)(2,1)S(1)} %collective-permute-done.1.before_ref, ...), custom_call_target="tpu_custom_call" | custom-call | flops 2147483648 | bytes 2097152 | tf_op jit(solution)/shard_map/pallas_call | solution.py:333
  71.8 0.0 collective-permute-done.other_ref
  71.8 2.4 %shard_map.41 = bf16[16,64,128]{2,1,0:T(8,128)(2,1)S(1)} custom-call(s32[2]{0:T(128)S(1)} %pad_add_fusion.place_ref, bf16[64,128]{1,0:T(8,128)(2,1)S(1)} %get-tuple-element.10.queries_ref, bf16[16,64,128]{2,1,0:T(8,128)(2,1)S(1)} %all-to-all-done.1.own_ref, bf16[16,64,128]{2,1,0:T(8,128)(2,1)S(1)} %collective-permute-done.other_ref, ...), custom_call_target="tpu_custom_call" | custom-call | flops 1073741824 | bytes 2097152 | tf_op jit(solution)/shard_map/pallas_call | solution.py:341
  74.3 11.4 %all_to_all.15.in_ref = bf16[16,64,128]{2,1,0:T(8,128)(2,1)S(1)} all-to-all(bf16[16,64,128]{2,1,0:T(8,128)(2,1)S(1)} %shard_map.41), channel_id=1, replica_groups=mesh['seqhi'=32,'seqlo'=16] {'seqlo'}, dimensions={0} | all-to-all | bytes 524288 | tf_op jit(solution)/shard_map/all_to_all | solution.py:351
  85.7 0.8 shard_map.42
Async XLA Ops:
  0.0 0.9 %copy-start = (bf16[128,1024]{1,0:T(8,128)(2,1)S(1)}, bf16[128,1024]{1,0:T(8,128)(2,1)}, u32[]{:S(2)}) copy-start(bf16[128,1024]{1,0:T(8,128)(2,1)} %q_ref.1) | copy-start | bytes 786436
  1.0 0.9 %copy-start.1 = (bf16[128,1024]{1,0:T(8,128)(2,1)S(1)}, bf16[128,1024]{1,0:T(8,128)(2,1)}, u32[]{:S(2)}) copy-start(bf16[128,1024]{1,0:T(8,128)(2,1)} %k_ref.1) | copy-start | bytes 786436
  1.9 0.9 %copy-start.2 = (bf16[128,1024]{1,0:T(8,128)(2,1)S(1)}, bf16[128,1024]{1,0:T(8,128)(2,1)}, u32[]{:S(2)}) copy-start(bf16[128,1024]{1,0:T(8,128)(2,1)} %v_ref.1) | copy-start | bytes 786436
  4.0 18.3 %all-to-all-start = ((bf16[16,192,128]{2,1,0:T(8,128)(2,1)}), bf16[16,192,128]{2,1,0:T(8,128)(2,1)S(1)}, u32[]{:S(2)}, u32[]{:S(2)}) async-start(bf16[16,192,128]{2,1,0:T(8,128)(2,1)} %shard_map.37), calls=%async_computation | async-start | bytes 1572864 | tf_op jit(solution)/shard_map/all_to_all | solution.py:302
  24.5 29.8 %all-to-all-start.1 = ((bf16[16,64,128]{2,1,0:T(8,128)(2,1)}), bf16[16,64,128]{2,1,0:T(8,128)(2,1)S(1)}, u32[]{:S(2)}, u32[]{:S(2)}) async-start(bf16[16,64,128]{2,1,0:T(8,128)(2,1)} %get-tuple-element.11), calls=%async_computation.1 | async-start | bytes 524288 | tf_op jit(solution)/shard_map/all_to_all | solution.py:320
  41.6 27.7 %collective-permute-start.1 = (bf16[5,128,128]{2,1,0:T(8,128)(2,1)S(1)}, bf16[5,128,128]{2,1,0:T(8,128)(2,1)S(1)}, u32[]{:S(2)}, u32[]{:S(2)}) collective-permute-start(bf16[5,128,128]{2,1,0:T(8,128)(2,1)S(1)} %get-tuple-element.13), channel_id=1, source_target_pairs={{0,16},{16,32},{32,48},{48,64},{64,80},{80,96},{96,112},{112,128},... | collective-permute-start | bytes 491528 | tf_op jit(solution)/shard_map/ppermute | solution.py:321
  47.9 21.5 %collective-permute-start.2 = (bf16[5,128,128]{2,1,0:T(8,128)(2,1)S(1)}, bf16[5,128,128]{2,1,0:T(8,128)(2,1)S(1)}, u32[]{:S(2)}, u32[]{:S(2)}) collective-permute-start(bf16[5,128,128]{2,1,0:T(8,128)(2,1)S(1)} %get-tuple-element.14), channel_id=1, source_target_pairs={{16,0},{32,16},{48,32},{64,48},{80,64},{96,80},{112,96},{128,112},... | collective-permute-start | bytes 491528 | tf_op jit(solution)/shard_map/ppermute | solution.py:322
  54.3 17.5 %collective-permute-start = (bf16[16,64,128]{2,1,0:T(8,128)(2,1)S(1)}, bf16[16,64,128]{2,1,0:T(8,128)(2,1)S(1)}, u32[]{:S(2)}, u32[]{:S(2)}) collective-permute-start(bf16[16,64,128]{2,1,0:T(8,128)(2,1)S(1)} %all-to-all-done.1.own_ref), channel_id=1, source_target_pairs={{0,16},{16,0},{32,48},{48,32},{64,80},{80,64},{96,112},{112,96},{1... | collective-permute-start | bytes 786440 | tf_op jit(solution)/shard_map/ppermute | solution.py:323

commit v2 on v1

v2 whole, which is shorter than its diff:
```python
import functools
import math

import jax
import jax.numpy as jnp
from jax import lax
from jax.experimental import pallas as pl
from jax.experimental.pallas import tpu as pltpu
from jax.sharding import PartitionSpec as P

HEADS = 16
HEAD = 64
BLOCK = 128
NEVER = -1e30
SCALE = math.log2(math.e) / math.sqrt(HEAD)
TILES = 16
OFFSET = {1: 0, 2: 8, 3: 12, 4: 14}
COUNT = {0: 16, 1: 8, 2: 4, 3: 2, 4: 1}
ROWS = 72
PACKED = {5: 0, 6: 64, 7: 96, 8: 112}

VMEM = pl.BlockSpec(memory_space=pltpu.VMEM)
SMEM = pl.BlockSpec(memory_space=pltpu.SMEM)


def iota(shape, dim):
    return lax.broadcasted_iota(jnp.int32, shape, dim)


def mm(a, b):
    return jnp.dot(a, b, preferred_element_type=jnp.float32)


def split_kernel(count, *refs):
    sources, out_ref, held, sems = refs[:count], refs[count], refs[count + 1], refs[count + 2]
    copies = []
    for place in range(count):
        for part in range(2):
            columns = pl.ds(512 * part, 512)
            copy = pltpu.make_async_copy(
                sources[place].at[:, columns], held.at[place, :, columns], sems.at[place, part]
            )
            copy.start()
            copies.append((place, part, copy))
    for place, part, copy in copies:
        copy.wait()
        for pair in range(4 * part, 4 * part + 4):
            turned = held[place, :, 128 * pair : 128 * pair + 128].T
            out_ref[2 * pair, 64 * place : 64 * place + 64, :] = turned[:64]
            out_ref[2 * pair + 1, 64 * place : 64 * place + 64, :] = turned[64:]


def join_kernel(in_ref, out_ref):
    for pair in range(HEADS // 2):
        both = jnp.concatenate([in_ref[2 * pair], in_ref[2 * pair + 1]], axis=0)
        out_ref[:, 128 * pair : 128 * pair + 128] = both.T


def halving():
    wanted = iota((256, 128), 0) // 2 == iota((256, 128), 1)
    return jnp.where(wanted, 0.5, 0.0).astype(jnp.bfloat16)


def coarser_tiles(finer, halve):
    out = []
    for i in range(len(finer) // 2):
        pair = jnp.concatenate([finer[2 * i], finer[2 * i + 1]], axis=1)
        out.append(mm(pair, halve).astype(jnp.bfloat16))
    return out


def coarse_kernel(place_ref, x_ref, tiles_ref, inside_ref, outside_ref, far_ref, ready_ref):
    plane = place_ref[0] >> 1
    first_core = (place_ref[0] & 1) == 0
    halve = halving()
    finer = [x_ref[i, :128] for i in range(TILES)]
    ends = [(finer[0], finer[-1])]
    for level in range(1, 5):
        finer = coarser_tiles(finer, halve)
        for i, tile in enumerate(finer):
            tiles_ref[OFFSET[level] + i] = tile
        ends.append((finer[0], finer[-1]))
    tile = finer[0]
    lanes = iota((64, 128), 1)
    for level in range(5, 9):
        tile = mm(tile, halve[:128]).astype(jnp.bfloat16)
        values = pltpu.roll(tile[64:].astype(jnp.float32), 64, 1)
        ready_ref[level - 5] = jnp.where(lanes < 64, tile[:64].astype(jnp.float32), values).astype(jnp.bfloat16)
    for there in range(16):
        far_ref[there] = ready_ref[needed_level(plane, there) - 5]
    for level, (first, last) in enumerate(ends):
        inside_ref[level] = jnp.where(first_core, last, first)
        outside_ref[level] = jnp.where(first_core, first, last)


def needed_level(plane, there):
    level = jnp.int32(8)
    for at in (7, 6, 5):
        near = jnp.abs((plane >> (at - 5)) - (there >> (at - 5))) <= 1
        level = jnp.where(near, jnp.int32(at), level)
    return level


def softmax_parts(parts):
    top = parts[0].max(axis=0, keepdims=True)
    for part in parts[1:]:
        top = jnp.maximum(top, part.max(axis=0, keepdims=True))
    top = top * SCALE
    weights, total = [], None
    for part in parts:
        grown = jnp.exp2(part * SCALE - top)
        added = grown.sum(axis=0, keepdims=True)
        total = added if total is None else total + added
        weights.append(grown.astype(jnp.bfloat16))
    return top, total, weights


def near_tile(query, keys, values, bias=(None, None, None)):
    parts = []
    for key, add in zip(keys, bias):
        scores = mm(key, query)
        parts.append(scores if add is None else scores + add)
    top, total, weights = softmax_parts(parts)
    numer = mm(jnp.concatenate(values, axis=1), jnp.concatenate(weights, axis=0))
    return numer, top, total


def far_tile(query, keys, values, level, bias=(None, None)):
    scores = []
    for key, add in zip(keys, bias):
        part = mm(key, query)
        scores.append(part if add is None else part + add)
    lower = iota((64, 128), 1) < 64
    middle = jnp.where(lower, scores[1][:64], scores[0][64:])
    top, total, weights = softmax_parts([scores[0][:64], middle, scores[1][64:]])
    none = jnp.zeros_like(weights[1])
    spread = [weights[0], jnp.where(lower, none, weights[1]), jnp.where(lower, weights[1], none), weights[2]]
    numer = mm(jnp.concatenate(values, axis=1), jnp.concatenate(spread, axis=0))
    times = 2.0**level
    return numer * times, top, total * times


def put(ref, place, state):
    numer, top, total = state
    ref[place, :64] = numer
    ref[place, 64:65] = top
    ref[place, 65:66] = total


def get(ref, place):
    return ref[place, :64], ref[place, 64:65], ref[place, 65:66]


def merge(one, two):
    top = jnp.maximum(one[1], two[1])
    scale_one = jnp.exp2(one[1] - top)
    scale_two = jnp.exp2(two[1] - top)
    return one[0] * scale_one + two[0] * scale_two, top, one[2] * scale_one + two[2] * scale_two


def lanes_from(state, picks):
    wide = jnp.concatenate([picks] * 8, axis=0)
    both = jnp.concatenate([state[1], state[2], jnp.zeros((6, 128), jnp.float32)], axis=0)
    both = jnp.take_along_axis(both, picks, axis=1)
    return jnp.take_along_axis(state[0], wide, axis=1), both[0:1], both[1:2]


STATE_TILES = TILES + 8 + 4
STATE_AT = {0: 0, 1: 16, 2: 24}


def level_tile(level_zero, coarse, level, i):
    return level_zero.at[i] if level == 0 else coarse.at[OFFSET[level] + i]


def query_tile(level_zero, coarse, level, i):
    return level_zero[i, 128:] if level == 0 else coarse[OFFSET[level] + i]


def interior_kernel(x_ref, tiles_ref, state_ref, coarse_q_ref, packed_ref):
    halve = halving()
    finer = [x_ref[i, 128:] for i in range(TILES)]
    for level in range(1, 5):
        finer = coarser_tiles(finer, halve)
        for i, tile in enumerate(finer):
            coarse_q_ref[OFFSET[level] + i] = tile
    tile, packed = finer[0], None
    lanes = iota((64, 128), 1)
    for level in range(5, 9):
        tile = mm(tile, halve[:128]).astype(jnp.bfloat16)
        wide = tile.astype(jnp.float32)
        if level == 5:
            packed = wide
        else:
            packed = jnp.where(lanes >= PACKED[level], pltpu.roll(wide, PACKED[level], 1), packed)
    packed_ref[...] = packed.astype(jnp.bfloat16)

    for level in range(3):
        count = COUNT[level]
        turned = {}
        for i in range(1, count - 1):
            query = query_tile(x_ref, coarse_q_ref, level, i)
            at = (i - 1, i, i + 1) if level == 0 else (i - 1, i + 1)
            for n in at:
                if n not in turned:
                    turned[n] = level_tile(x_ref, tiles_ref, level, n)[:64].T
            keys = [turned[n] for n in at]
            values = [level_tile(x_ref, tiles_ref, level, n)[64:128] for n in at]
            state = near_tile(query, keys, values) if level == 0 else far_tile(query, keys, values, level)
            put(state_ref, STATE_AT[level] + i, state)


def edges_kernel(place_ref, coarse_q_ref, x_ref, tiles_ref, inside_ref, outside_ref, inner_ref, state_ref):
    place = place_ref[0]
    last_place = place_ref[1]
    first_core = (place & 1) == 0
    no_before = jnp.where(place == 0, jnp.float32(NEVER), jnp.float32(0.0))
    no_after = jnp.where(place == last_place, jnp.float32(NEVER), jnp.float32(0.0))
    lanes = iota((8, 128), 1)

    def side(level, i):
        if 0 <= i < COUNT[level]:
            ref = level_tile(x_ref, tiles_ref, level, i)
            return ref[:64].T, ref[64:128], None
        came_inside = first_core if i >= 0 else jnp.logical_not(first_core)
        both = jnp.where(came_inside, inside_ref[level], outside_ref[level])
        return both[:64].T, both[64:], no_before if i < 0 else no_after

    coarser = None
    for level in (4, 3, 2, 1, 0):
        merged = []
        for i in range(COUNT[level]):
            if level < 3 and 0 < i < COUNT[level] - 1:
                state = get(inner_ref, STATE_AT[level] + i)
            else:
                at = (i - 1, i, i + 1) if level == 0 else (i - 1, i + 1)
                keys, values, bias = zip(*(side(level, n) for n in at))
                query = query_tile(x_ref, coarse_q_ref, level, i)
                if level == 0:
                    state = near_tile(query, keys, values, bias)
                else:
                    state = far_tile(query, keys, values, level, bias)
            if coarser is not None:
                picks = 64 * (i % 2) + lanes // 2
                state = merge(state, lanes_from(coarser[i // 2], picks))
            merged.append(state)
        coarser = merged
    for i in range(TILES):
        put(state_ref, i, coarser[i])


def lane_levels():
    lane = iota((32, 128), 1)
    return jnp.where(lane < 64, 5, jnp.where(lane < 96, 6, jnp.where(lane < 112, 7, 8)))


def far_state(plane, core, source, query, ref, bias_ref):
    slot = iota((32, 128), 0)
    lane_level = lane_levels()
    bias_ref[0] = jnp.full((32, 128), NEVER, jnp.float32)
    for level in (6, 7, 8):
        held = (lane_level == level) & (slot < (64 >> (level - 5)))
        bias_ref[level - 5] = jnp.where(held, 0.0, NEVER)

    rows, lanes = iota((128, 512), 0), iota((128, 512), 1)
    pick = jnp.where((rows // 32 == lanes // 128) & (rows % 32 == lanes % 128), 1.0, 0.0).astype(jnp.bfloat16)
    rows, lanes = iota((512, 128), 0), iota((512, 128), 1)
    place = (lanes // 32 == rows // 128) & (lanes % 32 + 64 == rows % 128)
    place = jnp.where(place, 1.0, 0.0).astype(jnp.bfloat16)
    parts, values = [], []
    for four in range(4):
        chunks = jnp.concatenate([ref[4 * four + n] for n in range(4)], axis=1)
        key = lax.dot_general(
            pick, chunks, (((1,), (1,)), ((), ())), preferred_element_type=jnp.float32
        ).astype(jnp.bfloat16)
        values.append(mm(chunks, place).astype(jnp.bfloat16))
        bias = [bias_ref[needed_level(plane, 4 * four + n) - 5] for n in range(4)]
        parts.append(mm(key, query) + jnp.concatenate(bias, axis=0))
    first_lanes = jnp.where(iota((1, 128), 1) < 64, 0.0, NEVER)
    for step in (-1, 1):
        there = plane + step
        held = (there >= 0) & (there < 16) & (jnp.abs(2 * step + source - core) >= 2)
        chunk = ref[jnp.clip(there, 0, 15)]
        turned = chunk.T
        parts.append(mm(turned[:64], query) + (first_lanes + jnp.where(held, 0.0, NEVER)))
        values.append(chunk[:, 64:])
    top, total, weights = softmax_parts(parts)
    return mm(jnp.concatenate(values, axis=1), jnp.concatenate(weights, axis=0)), top, total


def own_kernel(place_ref, packed_ref, chunks_ref, state_ref, bias_ref):
    plane, core = place_ref[0] >> 1, place_ref[0] & 1
    put(state_ref, 0, far_state(plane, core, core, packed_ref[...], chunks_ref, bias_ref))


def final_kernel(place_ref, packed_ref, chunks_ref, own_ref, local_ref, out_ref, bias_ref):
    plane, core = place_ref[0] >> 1, place_ref[0] & 1
    state = far_state(plane, core, 1 - core, packed_ref[...], chunks_ref, bias_ref)
    numer, top, total = merge(state, get(own_ref, 0))
    row = lane_levels()[:1]
    times = jnp.where(row == 5, 32.0, jnp.where(row == 6, 64.0, jnp.where(row == 7, 128.0, 256.0)))
    packed = (numer * times, top, total * times)
    lanes = iota((8, 128), 1)
    state = packed
    for level in (6, 7, 8):
        picks = jnp.minimum(PACKED[level] + lanes // (1 << (level - 5)), 127)
        state = merge(state, lanes_from(packed, picks))
    for i in range(TILES):
        spread = lanes_from(state, 4 * i + lanes // 32)
        numer, _, total = merge(get(local_ref, i), spread)
        out_ref[i] = (numer / total).astype(jnp.bfloat16)


def call(kernel, out_shape, in_specs, flops, moved, exps=0, scratch=(), limit=48):
    out_specs = (VMEM,) * len(out_shape) if isinstance(out_shape, tuple) else VMEM
    return pl.pallas_call(
        kernel,
        out_shape=out_shape,
        in_specs=in_specs,
        out_specs=out_specs,
        scratch_shapes=scratch,
        compiler_params=pltpu.CompilerParams(vmem_limit_bytes=limit << 20),
        cost_estimate=pl.CostEstimate(flops=flops, bytes_accessed=moved, transcendentals=exps),
    )


def split(*arrays):
    count = len(arrays)
    return call(
        functools.partial(split_kernel, count),
        jax.ShapeDtypeStruct((HEADS, 64 * count, 128), jnp.bfloat16),
        [pl.BlockSpec(memory_space=pltpu.HBM)] * count,
        1 << 22,
        count << 19,
        scratch=[pltpu.VMEM((count, 128, HEADS * HEAD), jnp.bfloat16), pltpu.SemaphoreType.DMA((count, 2))],
        limit=62,
    )(*arrays)


def body(queries, key_rows, value_rows):
    bf16, f32 = jnp.bfloat16, jnp.float32
    outer = lax.axis_size("seqhi")
    place = lax.axis_index("seqhi").astype(jnp.int32)
    place_info = jnp.stack([place, jnp.int32(outer - 1)])
    shape = jax.ShapeDtypeStruct

    tokens = lax.all_to_all(split(key_rows, value_rows, queries), "seqlo", 0, 0)

    tiles, inside, outside, far = call(
        coarse_kernel,
        (
            shape((15, 128, 128), bf16),
            shape((5, 128, 128), bf16),
            shape((5, 128, 128), bf16),
            shape((16, 64, 128), bf16),
        ),
        [SMEM, VMEM],
        1 << 27,
        2 << 20,
        scratch=[pltpu.VMEM((4, 64, 128), bf16)],
    )(place_info, tokens)

    planes = [[2 * z + core for z in range(outer // 2)] for core in range(2)]
    own = lax.all_to_all(far, "seqhi", 0, 0, axis_index_groups=planes)
    cores = [(i, i ^ 1) for i in range(outer)]
    inside = lax.ppermute(inside, "seqhi", cores)
    beside = [pair for i in range(1, outer - 1, 2) for pair in ((i, i + 1), (i + 1, i))]
    outside = lax.ppermute(outside, "seqhi", beside)

    inner, coarse_q, packed = call(
        interior_kernel,
        (shape((STATE_TILES, ROWS, 128), f32), shape((15, 64, 128), bf16), shape((64, 128), bf16)),
        [VMEM] * 2,
        1 << 32,
        2 << 20,
        1 << 20,
    )(tokens, tiles)
    local = call(
        edges_kernel, shape((TILES, ROWS, 128), f32), [SMEM] + [VMEM] * 6, 1 << 31, 2 << 20, 1 << 19
    )(place_info, coarse_q, tokens, tiles, inside, outside, inner)

    own, local = lax.optimization_barrier((own, local))
    other = lax.ppermute(own, "seqhi", cores)
    bias = pltpu.VMEM((4, 32, 128), f32)
    own_state = call(
        own_kernel, shape((1, ROWS, 128), f32), [SMEM] + [VMEM] * 2, 1 << 30, 1 << 20, 1 << 17, [bias]
    )(place_info, packed, own)
    out = call(
        final_kernel, shape((TILES, HEAD, 128), bf16), [SMEM] + [VMEM] * 4, 1 << 30, 2 << 20, 1 << 17, [bias]
    )(place_info, packed, other, own_state, local)

    heads = lax.all_to_all(out, "seqlo", 0, 0)
    return call(join_kernel, shape((128, HEADS * HEAD), bf16), [VMEM], 1 << 22, 1 << 19)(heads)


def solution(mesh):
    placed = P(("seqhi", "seqlo"), None)
    return jax.shard_map(body, mesh=mesh, in_specs=(placed,) * 3, out_specs=placed, check_vma=False)
```

time: 86.9 us -> 78.1 us (0.90)
  starting transfers between devices: 42.9 us -> 37.1 us
  Pallas kernels: 13.9 us -> 17.1 us
  local copies, waits for them, and re-layouts: 2.85 us -> 0 us
  waiting for transfers between devices: 15.2 us -> 12.4 us
    ppermute x3, starting transfers between devices: 18.4 us -> 12.5 us  [the longest x1 4.73 us: body(): inside = lax.ppermute(inside, 'seqhi', cores)]
    all_to_all x1, waiting for transfers between devices: 4.52 us -> 0.01 us  [body(): own = lax.all_to_all(far, 'seqhi', 0, 0, axis_index_groups=planes)]
    pallas_call x6 -> x7, Pallas kernels: 13.9 us -> 17.1 us  [the longest x1 5.64 us: body(): call(interior_kernel, (shape((STATE_TILES, ROWS, 128), f32), shape((15, 6...]
    unnamed x6 -> x0, local copies, waits for them, and re-layouts: 2.85 us -> none
    ppermute x3, waiting for transfers between devices: 0.01 us -> 1.79 us  [the longest x1 1.78 us: body(): outside = lax.ppermute(outside, 'seqhi', beside)]
  transfers between devices with their start and end apart: 5 -> 5, of which waited for: 2 -> 2; matrix products, arithmetic and copies ran while one was open for 0% -> 0% of each run, Pallas kernels for 8% -> 12%
where the time goes in v2:
time: 78.1 us; the launch traced here: 77.7 us
  starting transfers between devices  37.1 us (48%)
  Pallas kernels  17.1 us (22%)
  waiting for transfers between devices  12.4 us (16%)
  blocking collectives  11 us (14%)
    all_to_all x1, starting transfers between devices, body(): own = lax.all_to_all(far, 'seqhi', 0, 0, axis_index_groups=planes)  17 us
    all_to_all x1, blocking collectives, body(): heads = lax.all_to_all(out, 'seqlo', 0, 0)  11 us
    all_to_all x1, waiting for transfers between devices, body(): tokens = lax.all_to_all(split(key_rows, value_rows, queries), 'seqlo', 0, 0)  10.6 us
    all_to_all x1, starting transfers between devices, body(): tokens = lax.all_to_all(split(key_rows, value_rows, queries), 'seqlo', 0, 0)  7.6 us
    pallas_call x1, Pallas kernels, body(): call(interior_kernel, (shape((STATE_TILES, ROWS, 128), f32), shape((15, 6...  5.64 us
    ppermute x1, starting transfers between devices, body(): inside = lax.ppermute(inside, 'seqhi', cores)  4.73 us
    ppermute x1, starting transfers between devices, body(): other = lax.ppermute(own, 'seqhi', cores)  4.31 us
    ppermute x1, starting transfers between devices, body(): outside = lax.ppermute(outside, 'seqhi', beside)  3.44 us
  transfers between devices with their start and end apart: 5, of which 2 were waited for; matrix products, arithmetic and copies ran while one was open for 0% of the time, Pallas kernels for 12%

profile of v2, /device:TPU:1, one launch (start us, length us, event | category | flops | bytes accessed | tf_op | source)
XLA Modules:
  0.0 77.7 jit_solution(6879125642505660215)
XLA Ops:
  0.0 2.4 %shard_map.37 = bf16[16,192,128]{2,1,0:T(8,128)(2,1)} custom-call(bf16[128,1024]{1,0:T(8,128)(2,1)} %refs_0_.1, bf16[128,1024]{1,0:T(8,128)(2,1)} %refs_1_.1, bf16[128,1024]{1,0:T(8,128)(2,1)} %refs_2_.1), custom_call_target="tpu_custom_call" | custom-call | flops 4194304 | bytes 1572864 | tf_op jit(solution)/shard_map/pallas_call | solution.py:329
  2.4 7.6 %all-to-all-start = ((bf16[16,192,128]{2,1,0:T(8,128)(2,1)}), bf16[16,192,128]{2,1,0:T(8,128)(2,1)S(1)}, u32[]{:S(2)}, u32[]{:S(2)}) async-start(bf16[16,192,128]{2,1,0:T(8,128)(2,1)} %shard_map.37), calls=%async_computation | async-start | bytes 1572864 | tf_op jit(solution)/shard_map/all_to_all | solution.py:347
  10.0 0.1 pad_add_fusion.place_ref
  10.1 10.6 %all-to-all-done.x_ref = bf16[16,192,128]{2,1,0:T(8,128)(2,1)S(1)} async-done(((bf16[16,192,128]{2,1,0:T(8,128)(2,1)}), bf16[16,192,128]{2,1,0:T(8,128)(2,1)S(1)}, u32[]{:S(2)}, u32[]{:S(2)}) %all-to-all-start) | async-done | bytes 786464 | tf_op jit(solution)/shard_map/all_to_all | solution.py:347
  20.7 2.4 %shard_map.38 = (bf16[15,128,128]{2,1,0:T(8,128)(2,1)S(1)}, bf16[5,128,128]{2,1,0:T(8,128)(2,1)S(1)}, bf16[5,128,128]{2,1,0:T(8,128)(2,1)S(1)}, bf16[16,64,128]{2,1,0:T(8,128)(2,1)}) custom-call(s32[2]{0:T(128)S(1)} %pad_add_fusion.place_ref, bf16[16,192,128]{2,1,0:T(8,128)(2,1)S(1)} %all-to-all-done.x_ref), custom_call_target="tpu_custom_call" | custom-call | flops 134217728 | bytes 2097152 | tf_op jit(solution)/shard_map/pallas_call | solution.py:349
  23.1 17.0 %all-to-all-start.1 = ((bf16[16,64,128]{2,1,0:T(8,128)(2,1)}), bf16[16,64,128]{2,1,0:T(8,128)(2,1)S(1)}, u32[]{:S(2)}, u32[]{:S(2)}) async-start(bf16[16,64,128]{2,1,0:T(8,128)(2,1)} %get-tuple-element.16), calls=%async_computation.1 | async-start | bytes 524288 | tf_op jit(solution)/shard_map/all_to_all | solution.py:364
  40.1 4.7 %collective-permute-start = (bf16[5,128,128]{2,1,0:T(8,128)(2,1)S(1)}, bf16[5,128,128]{2,1,0:T(8,128)(2,1)S(1)}, u32[]{:S(2)}, u32[]{:S(2)}) collective-permute-start(bf16[5,128,128]{2,1,0:T(8,128)(2,1)S(1)} %get-tuple-element.18), channel_id=1, source_target_pairs={{0,16},{16,0},{32,48},{48,32},{64,80},{80,64},{96,112},{112,96},{1... | collective-permute-start | bytes 491528 | tf_op jit(solution)/shard_map/ppermute | solution.py:366
  44.9 3.4 %collective-permute-start.1 = (bf16[5,128,128]{2,1,0:T(8,128)(2,1)S(1)}, bf16[5,128,128]{2,1,0:T(8,128)(2,1)S(1)}, u32[]{:S(2)}, u32[]{:S(2)}) collective-permute-start(bf16[5,128,128]{2,1,0:T(8,128)(2,1)S(1)} %get-tuple-element.19), channel_id=1, source_target_pairs={{16,32},{32,16},{48,64},{64,48},{80,96},{96,80},{112,128},{128,112... | collective-permute-start | bytes 491528 | tf_op jit(solution)/shard_map/ppermute | solution.py:368
  48.3 5.6 %shard_map.39 = (f32[28,72,128]{2,1,0:T(8,128)S(1)}, bf16[15,64,128]{2,1,0:T(8,128)(2,1)S(1)}, bf16[64,128]{1,0:T(8,128)(2,1)S(1)}) custom-call(bf16[16,192,128]{2,1,0:T(8,128)(2,1)S(1)} %all-to-all-done.x_ref, bf16[15,128,128]{2,1,0:T(8,128)(2,1)S(1)} %get-tuple-element.14.tiles_ref), custom_call_target="tpu_custom_call" | custom-call | flops 4294967296 | bytes 2097152 | tf_op jit(solution)/shard_map/pallas_call | solution.py:370
  54.0 0.0 collective-permute-done.inside_ref
  54.0 1.8 %collective-permute-done.1.outside_ref = bf16[5,128,128]{2,1,0:T(8,128)(2,1)S(1)} collective-permute-done((bf16[5,128,128]{2,1,0:T(8,128)(2,1)S(1)}, bf16[5,128,128]{2,1,0:T(8,128)(2,1)S(1)}, u32[]{:S(2)}, u32[]{:S(2)}) %collective-permute-start.1) | collective-permute-done | bytes 163872 | tf_op jit(solution)/shard_map/ppermute | solution.py:368
  55.8 2.5 %shard_map.40.local_ref = f32[16,72,128]{2,1,0:T(8,128)S(1)} custom-call(s32[2]{0:T(128)S(1)} %pad_add_fusion.place_ref, bf16[15,64,128]{2,1,0:T(8,128)(2,1)S(1)} %get-tuple-element.17.coarse_q_ref, bf16[16,192,128]{2,1,0:T(8,128)(2,1)S(1)} %all-to-all-done.x_ref, bf16[15,128,128]{2,1,0:T(8,128)(2,1)S(1)} %get-tuple-element.14.tiles_ref, ...), custom_call_target="tpu_custom_call" | custom-call | flops 2147483648 | bytes 2097152 | tf_op jit(solution)/shard_map/pallas_call | solution.py:378
  58.3 0.0 all-to-all-done.1.chunks_ref
  58.3 4.3 %collective-permute-start.2 = (bf16[16,64,128]{2,1,0:T(8,128)(2,1)S(1)}, bf16[16,64,128]{2,1,0:T(8,128)(2,1)S(1)}, u32[]{:S(2)}, u32[]{:S(2)}) collective-permute-start(bf16[16,64,128]{2,1,0:T(8,128)(2,1)S(1)} %all-to-all-done.1.chunks_ref), channel_id=1, source_target_pairs={{0,16},{16,0},{32,48},{48,32},{64,80},{80,64},{96,112},{112,96},{1... | collective-permute-start | bytes 786440 | tf_op jit(solution)/shard_map/ppermute | solution.py:383
  62.6 1.4 %shard_map.41.own_ref = f32[1,72,128]{2,1,0:T(8,128)S(1)} custom-call(s32[2]{0:T(128)S(1)} %pad_add_fusion.place_ref, bf16[64,128]{1,0:T(8,128)(2,1)S(1)} %get-tuple-element.15.packed_ref, bf16[16,64,128]{2,1,0:T(8,128)(2,1)S(1)} %all-to-all-done.1.chunks_ref), custom_call_target="tpu_custom_call" | custom-call | flops 1073741824 | bytes 1048576 | tf_op jit(solution)/shard_map/pallas_call | solution.py:385
  64.0 0.0 collective-permute-done.2.chunks_ref
  64.0 1.9 %shard_map.42 = bf16[16,64,128]{2,1,0:T(8,128)(2,1)S(1)} custom-call(s32[2]{0:T(128)S(1)} %pad_add_fusion.place_ref, bf16[64,128]{1,0:T(8,128)(2,1)S(1)} %get-tuple-element.15.packed_ref, bf16[16,64,128]{2,1,0:T(8,128)(2,1)S(1)} %collective-permute-done.2.chunks_ref, f32[1,72,128]{2,1,0:T(8,128)S(1)} %shard_map.41.own_ref, ...), custom_call_target="tpu_custom_call" | custom-call | flops 1073741824 | bytes 2097152 | tf_op jit(solution)/shard_map/pallas_call | solution.py:388
  65.9 11.0 %all_to_all.15.in_ref = bf16[16,64,128]{2,1,0:T(8,128)(2,1)S(1)} all-to-all(bf16[16,64,128]{2,1,0:T(8,128)(2,1)S(1)} %shard_map.42), channel_id=1, replica_groups=mesh['seqhi'=32,'seqlo'=16] {'seqlo'}, dimensions={0} | all-to-all | bytes 524288 | tf_op jit(solution)/shard_map/all_to_all | solution.py:392
  76.9 0.8 %shard_map.43 = bf16[128,1024]{1,0:T(8,128)(2,1)} custom-call(bf16[16,64,128]{2,1,0:T(8,128)(2,1)S(1)} %all_to_all.15.in_ref), custom_call_target="tpu_custom_call" | custom-call | flops 4194304 | bytes 524288 | tf_op jit(solution)/shard_map/pallas_call | solution.py:393
Async XLA Ops:
  2.4 18.3 %all-to-all-start = ((bf16[16,192,128]{2,1,0:T(8,128)(2,1)}), bf16[16,192,128]{2,1,0:T(8,128)(2,1)S(1)}, u32[]{:S(2)}, u32[]{:S(2)}) async-start(bf16[16,192,128]{2,1,0:T(8,128)(2,1)} %shard_map.37), calls=%async_computation | async-start | bytes 1572864 | tf_op jit(solution)/shard_map/all_to_all | solution.py:347
  23.1 35.1 %all-to-all-start.1 = ((bf16[16,64,128]{2,1,0:T(8,128)(2,1)}), bf16[16,64,128]{2,1,0:T(8,128)(2,1)S(1)}, u32[]{:S(2)}, u32[]{:S(2)}) async-start(bf16[16,64,128]{2,1,0:T(8,128)(2,1)} %get-tuple-element.16), calls=%async_computation.1 | async-start | bytes 524288 | tf_op jit(solution)/shard_map/all_to_all | solution.py:364
  40.1 13.8 %collective-permute-start = (bf16[5,128,128]{2,1,0:T(8,128)(2,1)S(1)}, bf16[5,128,128]{2,1,0:T(8,128)(2,1)S(1)}, u32[]{:S(2)}, u32[]{:S(2)}) collective-permute-start(bf16[5,128,128]{2,1,0:T(8,128)(2,1)S(1)} %get-tuple-element.18), channel_id=1, source_target_pairs={{0,16},{16,0},{32,48},{48,32},{64,80},{80,64},{96,112},{112,96},{1... | collective-permute-start | bytes 491528 | tf_op jit(solution)/shard_map/ppermute | solution.py:366
  44.9 10.9 %collective-permute-start.1 = (bf16[5,128,128]{2,1,0:T(8,128)(2,1)S(1)}, bf16[5,128,128]{2,1,0:T(8,128)(2,1)S(1)}, u32[]{:S(2)}, u32[]{:S(2)}) collective-permute-start(bf16[5,128,128]{2,1,0:T(8,128)(2,1)S(1)} %get-tuple-element.19), channel_id=1, source_target_pairs={{16,32},{32,16},{48,64},{64,48},{80,96},{96,80},{112,128},{128,112... | collective-permute-start | bytes 491528 | tf_op jit(solution)/shard_map/ppermute | solution.py:368
  58.3 5.7 %collective-permute-start.2 = (bf16[16,64,128]{2,1,0:T(8,128)(2,1)S(1)}, bf16[16,64,128]{2,1,0:T(8,128)(2,1)S(1)}, u32[]{:S(2)}, u32[]{:S(2)}) collective-permute-start(bf16[16,64,128]{2,1,0:T(8,128)(2,1)S(1)} %all-to-all-done.1.chunks_ref), channel_id=1, source_target_pairs={{0,16},{16,0},{32,48},{48,32},{64,80},{80,64},{96,112},{112,96},{1... | collective-permute-start | bytes 786440 | tf_op jit(solution)/shard_map/ppermute | solution.py:383

commit v3 on v2

v3 whole, which is shorter than its diff:
```python
import functools
import math

import jax
import jax.numpy as jnp
from jax import lax
from jax.experimental import pallas as pl
from jax.experimental.pallas import tpu as pltpu
from jax.sharding import PartitionSpec as P

HEADS = 16
HEAD = 64
BLOCK = 128
NEVER = -1e30
SCALE = math.log2(math.e) / math.sqrt(HEAD)
TILES = 16
OFFSET = {1: 0, 2: 8, 3: 12, 4: 14}
COUNT = {0: 16, 1: 8, 2: 4, 3: 2, 4: 1}
ROWS = 72
PACKED = {5: 0, 6: 64, 7: 96, 8: 112}

VMEM = pl.BlockSpec(memory_space=pltpu.VMEM)


def iota(shape, dim):
    return lax.broadcasted_iota(jnp.int32, shape, dim)


def mm(a, b):
    return jnp.dot(a, b, preferred_element_type=jnp.float32)


def split_kernel(count, *refs):
    sources, out_ref, held, sems = refs[:count], refs[count], refs[count + 1], refs[count + 2]
    copies = []
    for place in range(count):
        for part in range(2):
            columns = pl.ds(512 * part, 512)
            copy = pltpu.make_async_copy(
                sources[place].at[:, columns], held.at[place, :, columns], sems.at[place, part]
            )
            copy.start()
            copies.append((place, part, copy))
    for place, part, copy in copies:
        copy.wait()
        for pair in range(4 * part, 4 * part + 4):
            turned = held[place, :, 128 * pair : 128 * pair + 128].T
            out_ref[2 * pair, 64 * place : 64 * place + 64, :] = turned[:64]
            out_ref[2 * pair + 1, 64 * place : 64 * place + 64, :] = turned[64:]


def join_kernel(in_ref, out_ref):
    for pair in range(HEADS // 2):
        both = jnp.concatenate([in_ref[2 * pair], in_ref[2 * pair + 1]], axis=0)
        out_ref[:, 128 * pair : 128 * pair + 128] = both.T


def halving():
    wanted = iota((256, 128), 0) // 2 == iota((256, 128), 1)
    return jnp.where(wanted, 0.5, 0.0).astype(jnp.bfloat16)


def halving_rows(rows, columns):
    return jnp.where(iota((rows, columns), 1) // 2 == iota((rows, columns), 0), 0.5, 0.0).astype(jnp.bfloat16)


def coarser_tiles(finer, halve):
    count, dims = len(finer) // 2, finer[0].shape[0]
    pairs = [jnp.concatenate([finer[2 * i], finer[2 * i + 1]], axis=1) for i in range(count)]
    joined = mm(jnp.concatenate(pairs, axis=0), halve).astype(jnp.bfloat16)
    return [joined[dims * i : dims * (i + 1)] for i in range(count)]


def coarse_kernel(x_ref, far_ref, fifth_ref, tiles_ref, ready_ref):
    place = lax.axis_index("seqhi")
    plane = place >> 1
    halve = halving()
    finer = [x_ref[i, :128] for i in range(TILES)]
    for level in range(1, 5):
        finer = coarser_tiles(finer, halve)
        for i, tile in enumerate(finer):
            tiles_ref[OFFSET[level] + i] = tile
    fifth = lax.dot_general(
        halving_rows(64, 128), finer[0], (((1,), (1,)), ((), ())), preferred_element_type=jnp.float32
    ).astype(jnp.bfloat16)
    fifth_ref[...] = fifth
    finer = fifth
    ready_ref[0] = jnp.zeros((32, 128), jnp.bfloat16)
    for level in (6, 7, 8):
        finer = mm(halving_rows(32, finer.shape[0]), finer).astype(jnp.bfloat16)
        ready_ref[level - 5] = finer
    for there in range(16):
        far_ref[there] = ready_ref[needed_level(plane, there) - 5]


def needed_level(plane, there):
    level = jnp.int32(8)
    for at in (7, 6, 5):
        near = jnp.abs((plane >> (at - 5)) - (there >> (at - 5))) <= 1
        level = jnp.where(near, jnp.int32(at), level)
    return level


class Task:
    def __init__(self, level, query, keys, values, bias=None):
        self.level, self.query, self.keys, self.values = level, query, keys, values
        self.bias = bias or [None] * len(keys)
        self.rows = 128 * len(keys)


def biased(scores, add):
    return scores if add is None else scores + add


def softmax_parts(parts):
    top = parts[0].max(axis=0, keepdims=True)
    for part in parts[1:]:
        top = jnp.maximum(top, part.max(axis=0, keepdims=True))
    top = top * SCALE
    weights, total = [], None
    for part in parts:
        grown = jnp.exp2(part * SCALE - top)
        added = grown.sum(axis=0, keepdims=True)
        total = added if total is None else total + added
        weights.append(grown.astype(jnp.bfloat16))
    return top, total, weights


def attend_all(tasks, score_ref, weight_ref):
    lower = iota((64, 128), 1) < 64
    none = jnp.zeros((64, 128), jnp.bfloat16)
    for n, task in enumerate(tasks):
        score_ref[n, : task.rows] = mm(jnp.concatenate(task.keys, axis=0), task.query)
    tops = []
    for n, task in enumerate(tasks):
        if task.level == 0:
            parts = [biased(score_ref[n, 128 * i : 128 * i + 128], add) for i, add in enumerate(task.bias)]
            top, total, weights = softmax_parts(parts)
            for i, weight in enumerate(weights):
                weight_ref[n, 128 * i : 128 * i + 128] = weight
        else:
            first, second, third, fourth = (
                biased(score_ref[n, 64 * i : 64 * i + 64], task.bias[i // 2]) for i in range(4)
            )
            top, total, weights = softmax_parts([first, jnp.where(lower, third, second), fourth])
            weight_ref[n, 0:64] = weights[0]
            weight_ref[n, 64:128] = jnp.where(lower, none, weights[1])
            weight_ref[n, 128:192] = jnp.where(lower, weights[1], none)
            weight_ref[n, 192:256] = weights[2]
        tops.append((top, total))
    states = []
    for n, task in enumerate(tasks):
        numer = mm(jnp.concatenate(task.values, axis=1), weight_ref[n, : task.rows])
        times = 2.0**task.level
        top, total = tops[n]
        states.append((numer * times, top, total * times) if task.level else (numer, top, total))
    return states


def put(ref, place, state):
    numer, top, total = state
    ref[place, :64] = numer
    ref[place, 64:65] = top
    ref[place, 65:66] = total


def get(ref, place):
    return ref[place, :64], ref[place, 64:65], ref[place, 65:66]


def merge(one, two):
    top = jnp.maximum(one[1], two[1])
    scale_one = jnp.exp2(one[1] - top)
    scale_two = jnp.exp2(two[1] - top)
    return one[0] * scale_one + two[0] * scale_two, top, one[2] * scale_one + two[2] * scale_two


def lanes_from(state, picks):
    wide = jnp.concatenate([picks] * 8, axis=0)
    both = jnp.concatenate([state[1], state[2], jnp.zeros((6, 128), jnp.float32)], axis=0)
    both = jnp.take_along_axis(both, picks, axis=1)
    return jnp.take_along_axis(state[0], wide, axis=1), both[0:1], both[1:2]


STATE_TILES = TILES + 8 + 4
STATE_AT = {0: 0, 1: 16, 2: 24}


def level_tile(level_zero, coarse, level, i):
    return level_zero.at[i] if level == 0 else coarse.at[OFFSET[level] + i]


def query_tile(level_zero, coarse, level, i):
    return level_zero[i, 128:] if level == 0 else coarse[OFFSET[level] + i]


def interior_kernel(
    x_ref, tiles_ref, fifth_ref, state_ref, coarse_q_ref, packed_ref, inside_ref, outside_ref, score_ref, weight_ref
):
    first_core = (lax.axis_index("seqhi") & 1) == 0
    for level in range(5):
        first = level_tile(x_ref, tiles_ref, level, 0)[:128]
        last = level_tile(x_ref, tiles_ref, level, COUNT[level] - 1)[:128]
        inside_ref[level] = jnp.where(first_core, last, first)
        sent = jnp.where(first_core, first, last)
        outside_ref[2 * level] = sent[:64]
        outside_ref[2 * level + 1] = sent[64:]
    outside_ref[10] = fifth_ref[...]
    halve = halving()
    finer = [x_ref[i, 128:] for i in range(TILES)]
    for level in range(1, 5):
        finer = coarser_tiles(finer, halve)
        for i, tile in enumerate(finer):
            coarse_q_ref[OFFSET[level] + i] = tile
    tile, packed = finer[0], None
    lanes = iota((64, 128), 1)
    for level in range(5, 9):
        tile = mm(tile, halve[:128]).astype(jnp.bfloat16)
        wide = tile.astype(jnp.float32)
        if level == 5:
            packed = wide
        else:
            packed = jnp.where(lanes >= PACKED[level], pltpu.roll(wide, PACKED[level], 1), packed)
    packed_ref[...] = packed.astype(jnp.bfloat16)

    tasks, places = [], []
    for level in range(3):
        turned = [level_tile(x_ref, tiles_ref, level, n)[:64].T for n in range(COUNT[level])]
        for i in range(1, COUNT[level] - 1):
            at = (i - 1, i, i + 1) if level == 0 else (i - 1, i + 1)
            values = [level_tile(x_ref, tiles_ref, level, n)[64:128] for n in at]
            tasks.append(Task(level, query_tile(x_ref, coarse_q_ref, level, i), [turned[n] for n in at], values))
            places.append(STATE_AT[level] + i)
    for place, state in zip(places, attend_all(tasks, score_ref, weight_ref)):
        put(state_ref, place, state)


def edges_kernel(
    coarse_q_ref, x_ref, tiles_ref, inside_ref, outside_ref, inner_ref, state_ref, score_ref, weight_ref
):
    place = lax.axis_index("seqhi")
    last_place = lax.axis_size("seqhi") - 1
    first_core = (place & 1) == 0
    no_before = jnp.where(place == 0, jnp.float32(NEVER), jnp.float32(0.0))
    no_after = jnp.where(place == last_place, jnp.float32(NEVER), jnp.float32(0.0))
    lanes = iota((8, 128), 1)

    def side(level, i):
        if 0 <= i < COUNT[level]:
            ref = level_tile(x_ref, tiles_ref, level, i)
            return ref[:64].T, ref[64:128], None
        came_inside = first_core if i >= 0 else jnp.logical_not(first_core)
        key = jnp.where(came_inside, inside_ref[level, :64], outside_ref[2 * level])
        value = jnp.where(came_inside, inside_ref[level, 64:], outside_ref[2 * level + 1])
        return key.T, value, no_before if i < 0 else no_after

    tasks, places = [], []
    for level in (4, 3, 2, 1, 0):
        for i in range(COUNT[level]):
            if level < 3 and 0 < i < COUNT[level] - 1:
                continue
            at = (i - 1, i, i + 1) if level == 0 else (i - 1, i + 1)
            keys, values, bias = zip(*(side(level, n) for n in at))
            tasks.append(Task(level, query_tile(x_ref, coarse_q_ref, level, i), keys, values, bias))
            places.append((level, i))
    done = dict(zip(places, attend_all(tasks, score_ref, weight_ref)))
    coarser = None
    for level in (4, 3, 2, 1, 0):
        merged = []
        for i in range(COUNT[level]):
            state = done[level, i] if (level, i) in done else get(inner_ref, STATE_AT[level] + i)
            if coarser is not None:
                state = merge(state, lanes_from(coarser[i // 2], 64 * (i % 2) + lanes // 2))
            merged.append(state)
        coarser = merged
    for i in range(TILES):
        put(state_ref, i, coarser[i])


def lane_levels():
    lane = iota((32, 128), 1)
    return jnp.where(lane < 64, 5, jnp.where(lane < 96, 6, jnp.where(lane < 112, 7, 8)))


def far_state(plane, query, chunks_ref, near, bias_ref, score_ref):
    slot = iota((32, 128), 0)
    lane_level = lane_levels()
    bias_ref[0] = jnp.full((32, 128), NEVER, jnp.float32)
    for level in (6, 7, 8):
        held = (lane_level == level) & (slot < (64 >> (level - 5)))
        bias_ref[level - 5] = jnp.where(held, 0.0, NEVER)
    first_lanes = jnp.where(iota((1, 128), 1) < 64, 0.0, NEVER)
    tall = jnp.concatenate([query, jnp.zeros((64, 128), jnp.bfloat16)], axis=0)
    rows = jnp.concatenate([chunks_ref[...]] + [tile for tile, _ in near], axis=0)
    count = rows.shape[0]
    score_ref[:count] = mm(rows, tall)
    top = None
    for n in range(16 + 2 * len(near)):
        if n < 16:
            bias = bias_ref[needed_level(plane, n) - 5]
        else:
            bias = first_lanes + jnp.where(near[(n - 16) // 2][1], 0.0, NEVER)
        part = score_ref[32 * n : 32 * n + 32] + bias
        score_ref[32 * n : 32 * n + 32] = part
        high = part.max(axis=0, keepdims=True)
        top = high if top is None else jnp.maximum(top, high)
    top = top * SCALE
    grown = jnp.exp2(score_ref[:count] * SCALE - top)
    total = grown.sum(axis=0, keepdims=True)
    both = lax.dot_general(
        rows, grown.astype(jnp.bfloat16), (((0,), (0,)), ((), ())), preferred_element_type=jnp.float32
    )
    return both[64:], top, total


def own_kernel(packed_ref, chunks_ref, beyond_ref, state_ref, bias_ref, score_ref):
    place = lax.axis_index("seqhi")
    toward = jnp.where((place & 1) == 0, place - 2, place + 2)
    near = [(beyond_ref[...], (toward >= 0) & (toward < lax.axis_size("seqhi")))]
    put(state_ref, 0, far_state(place >> 1, packed_ref[...], chunks_ref, near, bias_ref, score_ref))


def final_kernel(packed_ref, other_ref, own_ref, local_ref, out_ref, bias_ref, score_ref):
    place = lax.axis_index("seqhi")
    toward = jnp.where((place & 1) == 0, place + 2, place - 2)
    here = (toward >= 0) & (toward < lax.axis_size("seqhi"))
    near = [(other_ref[512:576], here), (other_ref[576:], here)]
    state = far_state(place >> 1, packed_ref[...], other_ref.at[:512], near, bias_ref, score_ref)
    numer, top, total = merge(state, get(own_ref, 0))
    row = lane_levels()[:1]
    times = jnp.where(row == 5, 32.0, jnp.where(row == 6, 64.0, jnp.where(row == 7, 128.0, 256.0)))
    packed = (numer * times, top, total * times)
    lanes = iota((8, 128), 1)
    state = packed
    for level in (6, 7, 8):
        picks = jnp.minimum(PACKED[level] + lanes // (1 << (level - 5)), 127)
        state = merge(state, lanes_from(packed, picks))
    for i in range(TILES):
        spread = lanes_from(state, 4 * i + lanes // 32)
        numer, _, total = merge(get(local_ref, i), spread)
        out_ref[i] = (numer / total).astype(jnp.bfloat16)


def call(kernel, out_shape, in_specs, flops, moved, exps=0, scratch=(), limit=24):
    out_specs = (VMEM,) * len(out_shape) if isinstance(out_shape, tuple) else VMEM
    return pl.pallas_call(
        kernel,
        out_shape=out_shape,
        in_specs=in_specs,
        out_specs=out_specs,
        scratch_shapes=scratch,
        compiler_params=pltpu.CompilerParams(vmem_limit_bytes=limit << 20),
        cost_estimate=pl.CostEstimate(flops=flops, bytes_accessed=moved, transcendentals=exps),
    )


def split(*arrays):
    count = len(arrays)
    return call(
        functools.partial(split_kernel, count),
        jax.ShapeDtypeStruct((HEADS, 64 * count, 128), jnp.bfloat16),
        [pl.BlockSpec(memory_space=pltpu.HBM)] * count,
        1 << 22,
        count << 19,
        scratch=[pltpu.VMEM((count, 128, HEADS * HEAD), jnp.bfloat16), pltpu.SemaphoreType.DMA((count, 2))],
        limit=62,
    )(*arrays)


def body(queries, key_rows, value_rows):
    bf16, f32 = jnp.bfloat16, jnp.float32
    outer = lax.axis_size("seqhi")
    shape = jax.ShapeDtypeStruct

    tokens = lax.all_to_all(split(key_rows, value_rows, queries), "seqlo", 0, 0)

    far, fifth, tiles = call(
        coarse_kernel,
        (shape((16, 32, 128), bf16), shape((64, 128), bf16), shape((15, 128, 128), bf16)),
        [VMEM],
        1 << 27,
        2 << 20,
        scratch=[pltpu.VMEM((4, 32, 128), bf16)],
    )(tokens)

    planes = [[2 * z + core for z in range(outer // 2)] for core in range(2)]
    own = lax.all_to_all(far, "seqhi", 0, 0, axis_index_groups=planes)
    inner, coarse_q, packed, inside, outside = call(
        interior_kernel,
        (
            shape((STATE_TILES, ROWS, 128), f32),
            shape((15, 64, 128), bf16),
            shape((64, 128), bf16),
            shape((5, 128, 128), bf16),
            shape((11, 64, 128), bf16),
        ),
        [VMEM] * 3,
        1 << 20,
        1 << 16,
        1 << 10,
        [pltpu.VMEM((22, 384, 128), f32), pltpu.VMEM((22, 384, 128), bf16)],
    )(tokens, tiles, fifth)
    beside = [pair for i in range(1, outer - 1, 2) for pair in ((i, i + 1), (i + 1, i))]
    outside = lax.ppermute(outside, "seqhi", beside)
    cores = [(i, i ^ 1) for i in range(outer)]
    inside = lax.ppermute(inside, "seqhi", cores)
    apart = [(i, i + 2) for i in range(0, outer - 2, 2)] + [(i, i - 2) for i in range(3, outer, 2)]
    fifth, inner = lax.optimization_barrier((fifth, inner))
    beyond = lax.ppermute(fifth, "seqhi", apart)
    local = call(
        edges_kernel,
        shape((TILES, ROWS, 128), f32),
        [VMEM] * 6,
        1 << 20,
        1 << 16,
        1 << 10,
        [pltpu.VMEM((9, 384, 128), f32), pltpu.VMEM((9, 384, 128), bf16)],
    )(coarse_q, tokens, tiles, inside, outside, inner)

    own, local = lax.optimization_barrier((own, local))
    own = own.reshape(512, 128)
    other = lax.ppermute(jnp.concatenate([own, outside[10], beyond], axis=0), "seqhi", cores)
    scratch = [pltpu.VMEM((4, 32, 128), f32), pltpu.VMEM((640, 128), f32)]
    own_state = call(
        own_kernel, shape((1, ROWS, 128), f32), [VMEM] * 3, 1 << 30, 1 << 20, 1 << 17, scratch
    )(packed, own, beyond)
    out = call(
        final_kernel, shape((TILES, HEAD, 128), bf16), [VMEM] * 4, 1 << 30, 2 << 20, 1 << 17, scratch
    )(packed, other, own_state, local)

    heads = lax.all_to_all(out, "seqlo", 0, 0)
    return call(join_kernel, shape((128, HEADS * HEAD), bf16), [VMEM], 1 << 22, 1 << 19)(heads)


def solution(mesh):
    placed = P(("seqhi", "seqlo"), None)
    return jax.shard_map(body, mesh=mesh, in_specs=(placed,) * 3, out_specs=placed, check_vma=False)
```

time: 78.1 us -> 72 us (0.922)
  blocking collectives: 11 us -> 29 us
  waiting for transfers between devices: 12.4 us -> 1.55 us
  Pallas kernels: 17.1 us -> 10.1 us
  starting transfers between devices: 37.1 us -> 30.9 us
    all_to_all x0 -> x1, blocking collectives: none -> 18.3 us  [body(): tokens = lax.all_to_all(split(key_rows, value_rows, queries), 'seqlo', 0, 0)]
    all_to_all x1 -> x0, waiting for transfers between devices: 10.6 us -> none  [body(): tokens = lax.all_to_all(split(key_rows, value_rows, queries), 'seqlo', 0, 0)]
    all_to_all x1 -> x0, starting transfers between devices: 7.6 us -> none  [body(): tokens = lax.all_to_all(split(key_rows, value_rows, queries), 'seqlo', 0, 0)]
    pallas_call x4, Pallas kernels: 8.22 us -> 4.56 us  [the longest x1 1.94 us: body(): call(coarse_kernel, (shape((16, 32, 128), bf16), shape((64, 128), bf16),...]
    pallas_call x1, Pallas kernels: 5.64 us -> 2.32 us  [body(): call(interior_kernel, (shape((STATE_TILES, ROWS, 128), f32), shape((15, 6...]
    ppermute x1, starting transfers between devices: 3.44 us -> 5.44 us  [body(): outside = lax.ppermute(outside, 'seqhi', beside)]
    ppermute x1, starting transfers between devices: 4.73 us -> 2.93 us  [body(): inside = lax.ppermute(inside, 'seqhi', cores)]
    ppermute x1, waiting for transfers between devices: 1.78 us -> 0.24 us  [body(): outside = lax.ppermute(outside, 'seqhi', beside)]
  transfers between devices with their start and end apart: 5 -> 5, of which waited for: 2 -> 3; matrix products, arithmetic and copies ran while one was open for 0% -> 0% of each run, Pallas kernels for 12% -> 6%
where the time goes in v3:
time: 72 us; the launch traced here: 71.6 us
  starting transfers between devices  30.9 us (43%)
  blocking collectives  29 us (40%)
  Pallas kernels  10.1 us (14%)
  waiting for transfers between devices  1.55 us (2%)
    all_to_all x1, blocking collectives, body(): tokens = lax.all_to_all(split(key_rows, value_rows, queries), 'seqlo', 0, 0)  18.3 us
    all_to_all x1, starting transfers between devices, body(): own = lax.all_to_all(far, 'seqhi', 0, 0, axis_index_groups=planes)  17.6 us
    all_to_all x1, blocking collectives, body(): heads = lax.all_to_all(out, 'seqlo', 0, 0)  10.7 us
    ppermute x1, starting transfers between devices, body(): outside = lax.ppermute(outside, 'seqhi', beside)  5.44 us
    ppermute x1, starting transfers between devices, body(): lax.ppermute(jnp.concatenate([own, outside[10], beyond], axis=0), 'seqhi'...  3.64 us
    ppermute x1, starting transfers between devices, body(): inside = lax.ppermute(inside, 'seqhi', cores)  2.93 us
    pallas_call x1, Pallas kernels, split(): call(functools.partial(split_kernel, count), jax.ShapeDtypeStruct((HEADS,...  2.38 us
    pallas_call x1, Pallas kernels, body(): call(interior_kernel, (shape((STATE_TILES, ROWS, 128), f32), shape((15, 6...  2.32 us
  transfers between devices with their start and end apart: 5, of which 3 were waited for; matrix products, arithmetic and copies ran while one was open for 0% of the time, Pallas kernels for 6%

profile of v3, /device:TPU:1, one launch (start us, length us, event | category | flops | bytes accessed | tf_op | source)
XLA Modules:
  0.0 71.6 jit_solution(8239693381672277195)
XLA Ops:
  0.0 2.4 %shard_map.37 = bf16[16,192,128]{2,1,0:T(8,128)(2,1)} custom-call(bf16[128,1024]{1,0:T(8,128)(2,1)} %refs_0_.1, bf16[128,1024]{1,0:T(8,128)(2,1)} %refs_1_.1, bf16[128,1024]{1,0:T(8,128)(2,1)} %refs_2_.1), custom_call_target="tpu_custom_call" | custom-call | flops 4194304 | bytes 1572864 | tf_op jit(solution)/shard_map/pallas_call | solution.py:359
  2.4 18.3 %all_to_all.15.x_ref = bf16[16,192,128]{2,1,0:T(8,128)(2,1)S(1)} all-to-all(bf16[16,192,128]{2,1,0:T(8,128)(2,1)} %shard_map.37), channel_id=1, replica_groups=mesh['seqhi'=32,'seqlo'=16] {'seqlo'}, dimensions={0} | all-to-all | bytes 1572864 | tf_op jit(solution)/shard_map/all_to_all | solution.py:375
  20.7 1.9 %shard_map.38 = (bf16[16,32,128]{2,1,0:T(8,128)(2,1)}, bf16[64,128]{1,0:T(8,128)(2,1)S(1)}, bf16[15,128,128]{2,1,0:T(8,128)(2,1)S(1)}) custom-call(bf16[16,192,128]{2,1,0:T(8,128)(2,1)S(1)} %all_to_all.15.x_ref), custom_call_target="tpu_custom_call" | custom-call | flops 134217728 | bytes 2097152 | tf_op jit(solution)/shard_map/pallas_call | solution.py:377
  22.6 17.6 %all-to-all-start.1 = ((bf16[16,32,128]{2,1,0:T(8,128)(2,1)}), bf16[16,32,128]{2,1,0:T(8,128)(2,1)S(1)}, u32[]{:S(2)}, u32[]{:S(2)}) async-start(bf16[16,32,128]{2,1,0:T(8,128)(2,1)} %get-tuple-element.20), calls=%async_computation.1 | async-start | bytes 262144 | tf_op jit(solution)/shard_map/all_to_all | solution.py:387
  40.2 2.3 %shard_map.39 = (f32[28,72,128]{2,1,0:T(8,128)S(1)}, bf16[15,64,128]{2,1,0:T(8,128)(2,1)S(1)}, bf16[64,128]{1,0:T(8,128)(2,1)S(1)}, bf16[5,128,128]{2,1,0:T(8,128)(2,1)S(1)}, bf16[11,64,128]{2,1,0:T(8,128)(2,1)S(1)}) custom-call(bf16[16,192,128]{2,1,0:T(8,128)(2,1)S(1)} %all_to_all.15.x_ref, bf16[15,128,128]{2,1,0:T(8,128)(2,1)S(1)} %get-tuple-element.17.tiles_ref, ...), custom_call_target="tpu_custom_call" | custom-call | flops 1048576 | bytes 65536 | tf_op jit(solution)/shard_map/pallas_call | solution.py:388
  42.5 5.4 %collective-permute-start.1 = (bf16[11,64,128]{2,1,0:T(8,128)(2,1)S(1)}, bf16[11,64,128]{2,1,0:T(8,128)(2,1)S(1)}, u32[]{:S(2)}, u32[]{:S(2)}) collective-permute-start(bf16[11,64,128]{2,1,0:T(8,128)(2,1)S(1)} %get-tuple-element.23), channel_id=1, source_target_pairs={{16,32},{32,16},{48,64},{64,48},{80,96},{96,80},{112,128},{128,112... | collective-permute-start | bytes 540680 | tf_op jit(solution)/shard_map/ppermute | solution.py:404
  48.0 1.3 %collective-permute-start.2 = (bf16[64,128]{1,0:T(8,128)(2,1)S(1)}, bf16[64,128]{1,0:T(8,128)(2,1)S(1)}, u32[]{:S(2)}, u32[]{:S(2)}) collective-permute-start(bf16[64,128]{1,0:T(8,128)(2,1)S(1)} %get-tuple-element.27.fifth_ref), channel_id=1, source_target_pairs={{0,32},{32,64},{64,96},{96,128},{128,160},{160,192},{192,224},{224... | collective-permute-start | bytes 49160 | tf_op jit(solution)/shard_map/ppermute | solution.py:409
  49.3 2.9 %collective-permute-start = (bf16[5,128,128]{2,1,0:T(8,128)(2,1)S(1)}, bf16[5,128,128]{2,1,0:T(8,128)(2,1)S(1)}, u32[]{:S(2)}, u32[]{:S(2)}) collective-permute-start(bf16[5,128,128]{2,1,0:T(8,128)(2,1)S(1)} %get-tuple-element.22), channel_id=1, source_target_pairs={{0,16},{16,0},{32,48},{48,32},{64,80},{80,64},{96,112},{112,96},{1... | collective-permute-start | bytes 491528 | tf_op jit(solution)/shard_map/ppermute | solution.py:406
  52.2 0.2 collective-permute-done.1.outside_ref
  52.5 0.8 %collective-permute-done.inside_ref = bf16[5,128,128]{2,1,0:T(8,128)(2,1)S(1)} collective-permute-done((bf16[5,128,128]{2,1,0:T(8,128)(2,1)S(1)}, bf16[5,128,128]{2,1,0:T(8,128)(2,1)S(1)}, u32[]{:S(2)}, u32[]{:S(2)}) %collective-permute-start) | collective-permute-done | bytes 163872 | tf_op jit(solution)/shard_map/ppermute | solution.py:406
  53.2 1.3 %shard_map.40.local_ref = f32[16,72,128]{2,1,0:T(8,128)S(1)} custom-call(bf16[15,64,128]{2,1,0:T(8,128)(2,1)S(1)} %get-tuple-element.21.coarse_q_ref, bf16[16,192,128]{2,1,0:T(8,128)(2,1)S(1)} %all_to_all.15.x_ref, bf16[15,128,128]{2,1,0:T(8,128)(2,1)S(1)} %get-tuple-element.17.tiles_ref, bf16[5,128,128]{2,1,0:T(8,128)(2,1)S(1)} %collective-permute-done.inside_ref, ...), custom_call_target="tpu_custom_call" | custom-call | flops 1048576 | bytes 65536 | tf_op jit(solution)/shard_map/pallas_call | solution.py:410
  54.5 0.0 all-to-all-done.1
  54.5 0.0 collective-permute-done.2.beyond_ref
  54.5 3.6 %collective-permute-start.3 = (bf16[640,128]{1,0:T(8,128)(2,1)S(1)}, bf16[640,128]{1,0:T(8,128)(2,1)S(1)}, u32[]{:S(2)}, u32[]{:S(2)}) collective-permute-start(bf16[640,128]{1,0:T(8,128)(2,1)S(1)} %pad_maximum_fusion), channel_id=1, source_target_pairs={{0,16},{16,0},{32,48},{48,32},{64,80},{80,64},{96,112},{112,96},{1... | collective-permute-start | bytes 491528 | tf_op jit(solution)/shard_map/ppermute | solution.py:422
  58.2 0.5 shard_map.41.own_ref
  58.6 0.5 collective-permute-done.3.other_ref
  59.2 0.9 %shard_map.42 = bf16[16,64,128]{2,1,0:T(8,128)(2,1)S(1)} custom-call(bf16[64,128]{1,0:T(8,128)(2,1)S(1)} %get-tuple-element.19.packed_ref, bf16[640,128]{1,0:T(8,128)(2,1)S(1)} %collective-permute-done.3.other_ref, f32[1,72,128]{2,1,0:T(8,128)S(1)} %shard_map.41.own_ref, f32[16,72,128]{2,1,0:T(8,128)S(1)} %shard_map.40.local_ref), custom_call_target="tpu_custom_call" | custom-call | flops 1073741824 | bytes 2097152 | tf_op jit(solution)/shard_map/pallas_call | solution.py:427
  60.1 10.7 %all_to_all.16.in_ref = bf16[16,64,128]{2,1,0:T(8,128)(2,1)S(1)} all-to-all(bf16[16,64,128]{2,1,0:T(8,128)(2,1)S(1)} %shard_map.42), channel_id=1, replica_groups=mesh['seqhi'=32,'seqlo'=16] {'seqlo'}, dimensions={0} | all-to-all | bytes 524288 | tf_op jit(solution)/shard_map/all_to_all | solution.py:431
  70.8 0.8 %shard_map.43 = bf16[128,1024]{1,0:T(8,128)(2,1)} custom-call(bf16[16,64,128]{2,1,0:T(8,128)(2,1)S(1)} %all_to_all.16.in_ref), custom_call_target="tpu_custom_call" | custom-call | flops 4194304 | bytes 524288 | tf_op jit(solution)/shard_map/pallas_call | solution.py:432
  (2 shorter events, 0.0 us)
Async XLA Ops:
  22.6 31.9 %all-to-all-start.1 = ((bf16[16,32,128]{2,1,0:T(8,128)(2,1)}), bf16[16,32,128]{2,1,0:T(8,128)(2,1)S(1)}, u32[]{:S(2)}, u32[]{:S(2)}) async-start(bf16[16,32,128]{2,1,0:T(8,128)(2,1)} %get-tuple-element.20), calls=%async_computation.1 | async-start | bytes 262144 | tf_op jit(solution)/shard_map/all_to_all | solution.py:387
  42.5 9.9 %collective-permute-start.1 = (bf16[11,64,128]{2,1,0:T(8,128)(2,1)S(1)}, bf16[11,64,128]{2,1,0:T(8,128)(2,1)S(1)}, u32[]{:S(2)}, u32[]{:S(2)}) collective-permute-start(bf16[11,64,128]{2,1,0:T(8,128)(2,1)S(1)} %get-tuple-element.23), channel_id=1, source_target_pairs={{16,32},{32,16},{48,64},{64,48},{80,96},{96,80},{112,128},{128,112... | collective-permute-start | bytes 540680 | tf_op jit(solution)/shard_map/ppermute | solution.py:404
  48.0 6.5 %collective-permute-start.2 = (bf16[64,128]{1,0:T(8,128)(2,1)S(1)}, bf16[64,128]{1,0:T(8,128)(2,1)S(1)}, u32[]{:S(2)}, u32[]{:S(2)}) collective-permute-start(bf16[64,128]{1,0:T(8,128)(2,1)S(1)} %get-tuple-element.27.fifth_ref), channel_id=1, source_target_pairs={{0,32},{32,64},{64,96},{96,128},{128,160},{160,192},{192,224},{224... | collective-permute-start | bytes 49160 | tf_op jit(solution)/shard_map/ppermute | solution.py:409
  49.3 3.9 %collective-permute-start = (bf16[5,128,128]{2,1,0:T(8,128)(2,1)S(1)}, bf16[5,128,128]{2,1,0:T(8,128)(2,1)S(1)}, u32[]{:S(2)}, u32[]{:S(2)}) collective-permute-start(bf16[5,128,128]{2,1,0:T(8,128)(2,1)S(1)} %get-tuple-element.22), channel_id=1, source_target_pairs={{0,16},{16,0},{32,48},{48,32},{64,80},{80,64},{96,112},{112,96},{1... | collective-permute-start | bytes 491528 | tf_op jit(solution)/shard_map/ppermute | solution.py:406
  54.5 4.7 %collective-permute-start.3 = (bf16[640,128]{1,0:T(8,128)(2,1)S(1)}, bf16[640,128]{1,0:T(8,128)(2,1)S(1)}, u32[]{:S(2)}, u32[]{:S(2)}) collective-permute-start(bf16[640,128]{1,0:T(8,128)(2,1)S(1)} %pad_maximum_fusion), channel_id=1, source_target_pairs={{0,16},{16,0},{32,48},{48,32},{64,80},{80,64},{96,112},{112,96},{1... | collective-permute-start | bytes 491528 | tf_op jit(solution)/shard_map/ppermute | solution.py:422

commit v4 on v3

--- a/solution.py
+++ b/solution.py
@@ -1,4 +1,3 @@
-import functools
 import math
 
 import jax
@@ -30,23 +29,23 @@
     return jnp.dot(a, b, preferred_element_type=jnp.float32)
 
 
-def split_kernel(count, *refs):
-    sources, out_ref, held, sems = refs[:count], refs[count], refs[count + 1], refs[count + 2]
-    copies = []
-    for place in range(count):
-        for part in range(2):
-            columns = pl.ds(512 * part, 512)
-            copy = pltpu.make_async_copy(
-                sources[place].at[:, columns], held.at[place, :, columns], sems.at[place, part]
-            )
-            copy.start()
-            copies.append((place, part, copy))
-    for place, part, copy in copies:
+def split_kernel(k_ref, v_ref, q_ref, out_ref, held, turned, in_sems, out_sems):
+    copies = [pltpu.make_async_copy(ref, held.at[n], in_sems.at[n]) for n, ref in enumerate((k_ref, v_ref, q_ref))]
+    for copy in copies:
+        copy.start()
+    sent = []
+    for n, copy in enumerate(copies):
         copy.wait()
-        for pair in range(4 * part, 4 * part + 4):
-            turned = held[place, :, 128 * pair : 128 * pair + 128].T
-            out_ref[2 * pair, 64 * place : 64 * place + 64, :] = turned[:64]
-            out_ref[2 * pair + 1, 64 * place : 64 * place + 64, :] = turned[64:]
+        rows = pl.ds(64 * n, 64)
+        for pair in range(HEADS // 2):
+            both = held[n, :, 128 * pair : 128 * pair + 128].T
+            turned[2 * pair, rows, :] = both[:64]
+            turned[2 * pair + 1, rows, :] = both[64:]
+        out = pltpu.make_async_copy(turned.at[:, rows], out_ref.at[:, rows], out_sems.at[n])
+        out.start()
+        sent.append(out)
+    for out in sent:
+        out.wait()
 
 
 def join_kernel(in_ref, out_ref):
@@ -65,10 +64,8 @@
 
 
 def coarser_tiles(finer, halve):
-    count, dims = len(finer) // 2, finer[0].shape[0]
-    pairs = [jnp.concatenate([finer[2 * i], finer[2 * i + 1]], axis=1) for i in range(count)]
-    joined = mm(jnp.concatenate(pairs, axis=0), halve).astype(jnp.bfloat16)
-    return [joined[dims * i : dims * (i + 1)] for i in range(count)]
+    pairs = [jnp.concatenate([finer[i], finer[i + 1]], axis=1) for i in range(0, len(finer), 2)]
+    return [mm(pair, halve).astype(jnp.bfloat16) for pair in pairs]
 
 
 def coarse_kernel(x_ref, far_ref, fifth_ref, tiles_ref, ready_ref):
@@ -341,8 +338,9 @@
         out_ref[i] = (numer / total).astype(jnp.bfloat16)
 
 
-def call(kernel, out_shape, in_specs, flops, moved, exps=0, scratch=(), limit=24):
-    out_specs = (VMEM,) * len(out_shape) if isinstance(out_shape, tuple) else VMEM
+def call(kernel, out_shape, in_specs, flops, moved, exps=0, scratch=(), limit=24, out_specs=VMEM):
+    if isinstance(out_shape, tuple):
+        out_specs = (out_specs,) * len(out_shape)
     return pl.pallas_call(
         kernel,
         out_shape=out_shape,
@@ -354,17 +352,16 @@
     )
 
 
-def split(*arrays):
-    count = len(arrays)
-    return call(
-        functools.partial(split_kernel, count),
-        jax.ShapeDtypeStruct((HEADS, 64 * count, 128), jnp.bfloat16),
-        [pl.BlockSpec(memory_space=pltpu.HBM)] * count,
-        1 << 22,
-        count << 19,
-        scratch=[pltpu.VMEM((count, 128, HEADS * HEAD), jnp.bfloat16), pltpu.SemaphoreType.DMA((count, 2))],
-        limit=62,
-    )(*arrays)
+def split(key_rows, value_rows, queries):
+    hbm = pl.BlockSpec(memory_space=pltpu.HBM)
+    scratch = [
+        pltpu.VMEM((3, 128, HEADS * HEAD), jnp.bfloat16),
+        pltpu.VMEM((HEADS, 192, 128), jnp.bfloat16),
+        pltpu.SemaphoreType.DMA((3,)),
+        pltpu.SemaphoreType.DMA((3,)),
+    ]
+    out = jax.ShapeDtypeStruct((HEADS, 192, 128), jnp.bfloat16)
+    return call(split_kernel, out, [hbm] * 3, 1 << 22, 3 << 19, 0, scratch, 62, hbm)(key_rows, value_rows, queries)
 
 
 def body(queries, key_rows, value_rows):

time: 72 us -> 71.6 us (level)
  no operation moved by 1% of the time
where the time goes in v4:
time: 71.6 us; the launch traced here: 71.2 us
  starting transfers between devices  31 us (43%)
  blocking collectives  29 us (41%)
  Pallas kernels  9.57 us (13%)
  waiting for transfers between devices  1.55 us (2%)
    all_to_all x1, blocking collectives, body(): tokens = lax.all_to_all(split(key_rows, value_rows, queries), 'seqlo', 0, 0)  18.3 us
    all_to_all x1, starting transfers between devices, body(): own = lax.all_to_all(far, 'seqhi', 0, 0, axis_index_groups=planes)  17.6 us
    all_to_all x1, blocking collectives, body(): heads = lax.all_to_all(out, 'seqlo', 0, 0)  10.7 us
    ppermute x1, starting transfers between devices, body(): outside = lax.ppermute(outside, 'seqhi', beside)  5.44 us
    ppermute x1, starting transfers between devices, body(): lax.ppermute(jnp.concatenate([own, outside[10], beyond], axis=0), 'seqhi'...  3.73 us
    ppermute x1, starting transfers between devices, body(): inside = lax.ppermute(inside, 'seqhi', cores)  2.93 us
    pallas_call x1, Pallas kernels, body(): call(interior_kernel, (shape((STATE_TILES, ROWS, 128), f32), shape((15, 6...  2.23 us
    pallas_call x1, Pallas kernels, split(): call(split_kernel, out, [hbm] * 3, 1 << 22, 3 << 19, 0, scratch, 62, hbm)  2.09 us
  transfers between devices with their start and end apart: 5, of which 3 were waited for; matrix products, arithmetic and copies ran while one was open for 0% of the time, Pallas kernels for 6%

profile of v4, /device:TPU:1, one launch (start us, length us, event | category | flops | bytes accessed | tf_op | source)
XLA Modules:
  0.0 71.2 jit_solution(10337434903856202772)
XLA Ops:
  0.0 2.1 %shard_map.37 = bf16[16,192,128]{2,1,0:T(8,128)(2,1)} custom-call(bf16[128,1024]{1,0:T(8,128)(2,1)} %k_ref.1, bf16[128,1024]{1,0:T(8,128)(2,1)} %v_ref.1, bf16[128,1024]{1,0:T(8,128)(2,1)} %q_ref.1), custom_call_target="tpu_custom_call" | custom-call | flops 4194304 | bytes 1572864 | tf_op jit(solution)/shard_map/pallas_call | solution.py:364
  2.1 18.3 %all_to_all.15.x_ref = bf16[16,192,128]{2,1,0:T(8,128)(2,1)S(1)} all-to-all(bf16[16,192,128]{2,1,0:T(8,128)(2,1)} %shard_map.37), channel_id=1, replica_groups=mesh['seqhi'=32,'seqlo'=16] {'seqlo'}, dimensions={0} | all-to-all | bytes 1572864 | tf_op jit(solution)/shard_map/all_to_all | solution.py:372
  20.4 1.8 %shard_map.38 = (bf16[16,32,128]{2,1,0:T(8,128)(2,1)}, bf16[64,128]{1,0:T(8,128)(2,1)S(1)}, bf16[15,128,128]{2,1,0:T(8,128)(2,1)S(1)}) custom-call(bf16[16,192,128]{2,1,0:T(8,128)(2,1)S(1)} %all_to_all.15.x_ref), custom_call_target="tpu_custom_call" | custom-call | flops 134217728 | bytes 2097152 | tf_op jit(solution)/shard_map/pallas_call | solution.py:374
  22.2 17.6 %all-to-all-start.1 = ((bf16[16,32,128]{2,1,0:T(8,128)(2,1)}), bf16[16,32,128]{2,1,0:T(8,128)(2,1)S(1)}, u32[]{:S(2)}, u32[]{:S(2)}) async-start(bf16[16,32,128]{2,1,0:T(8,128)(2,1)} %get-tuple-element.20), calls=%async_computation.1 | async-start | bytes 262144 | tf_op jit(solution)/shard_map/all_to_all | solution.py:384
  39.8 2.2 %shard_map.39 = (f32[28,72,128]{2,1,0:T(8,128)S(1)}, bf16[15,64,128]{2,1,0:T(8,128)(2,1)S(1)}, bf16[64,128]{1,0:T(8,128)(2,1)S(1)}, bf16[5,128,128]{2,1,0:T(8,128)(2,1)S(1)}, bf16[11,64,128]{2,1,0:T(8,128)(2,1)S(1)}) custom-call(bf16[16,192,128]{2,1,0:T(8,128)(2,1)S(1)} %all_to_all.15.x_ref, bf16[15,128,128]{2,1,0:T(8,128)(2,1)S(1)} %get-tuple-element.17.tiles_ref, ...), custom_call_target="tpu_custom_call" | custom-call | flops 1048576 | bytes 65536 | tf_op jit(solution)/shard_map/pallas_call | solution.py:385
  42.0 5.4 %collective-permute-start.1 = (bf16[11,64,128]{2,1,0:T(8,128)(2,1)S(1)}, bf16[11,64,128]{2,1,0:T(8,128)(2,1)S(1)}, u32[]{:S(2)}, u32[]{:S(2)}) collective-permute-start(bf16[11,64,128]{2,1,0:T(8,128)(2,1)S(1)} %get-tuple-element.23), channel_id=1, source_target_pairs={{16,32},{32,16},{48,64},{64,48},{80,96},{96,80},{112,128},{128,112... | collective-permute-start | bytes 540680 | tf_op jit(solution)/shard_map/ppermute | solution.py:401
  47.5 1.3 %collective-permute-start.2 = (bf16[64,128]{1,0:T(8,128)(2,1)S(1)}, bf16[64,128]{1,0:T(8,128)(2,1)S(1)}, u32[]{:S(2)}, u32[]{:S(2)}) collective-permute-start(bf16[64,128]{1,0:T(8,128)(2,1)S(1)} %get-tuple-element.27.fifth_ref), channel_id=1, source_target_pairs={{0,32},{32,64},{64,96},{96,128},{128,160},{160,192},{192,224},{224... | collective-permute-start | bytes 49160 | tf_op jit(solution)/shard_map/ppermute | solution.py:406
  48.8 2.9 %collective-permute-start = (bf16[5,128,128]{2,1,0:T(8,128)(2,1)S(1)}, bf16[5,128,128]{2,1,0:T(8,128)(2,1)S(1)}, u32[]{:S(2)}, u32[]{:S(2)}) collective-permute-start(bf16[5,128,128]{2,1,0:T(8,128)(2,1)S(1)} %get-tuple-element.22), channel_id=1, source_target_pairs={{0,16},{16,0},{32,48},{48,32},{64,80},{80,64},{96,112},{112,96},{1... | collective-permute-start | bytes 491528 | tf_op jit(solution)/shard_map/ppermute | solution.py:403
  51.7 0.3 collective-permute-done.1.outside_ref
  52.0 0.7 collective-permute-done.inside_ref
  52.7 1.3 %shard_map.40.local_ref = f32[16,72,128]{2,1,0:T(8,128)S(1)} custom-call(bf16[15,64,128]{2,1,0:T(8,128)(2,1)S(1)} %get-tuple-element.21.coarse_q_ref, bf16[16,192,128]{2,1,0:T(8,128)(2,1)S(1)} %all_to_all.15.x_ref, bf16[15,128,128]{2,1,0:T(8,128)(2,1)S(1)} %get-tuple-element.17.tiles_ref, bf16[5,128,128]{2,1,0:T(8,128)(2,1)S(1)} %collective-permute-done.inside_ref, ...), custom_call_target="tpu_custom_call" | custom-call | flops 1048576 | bytes 65536 | tf_op jit(solution)/shard_map/pallas_call | solution.py:407
  54.0 0.0 all-to-all-done.1
  54.0 0.0 collective-permute-done.2.beyond_ref
  54.0 3.7 %collective-permute-start.3 = (bf16[640,128]{1,0:T(8,128)(2,1)S(1)}, bf16[640,128]{1,0:T(8,128)(2,1)S(1)}, u32[]{:S(2)}, u32[]{:S(2)}) collective-permute-start(bf16[640,128]{1,0:T(8,128)(2,1)S(1)} %pad_maximum_fusion), channel_id=1, source_target_pairs={{0,16},{16,0},{32,48},{48,32},{64,80},{80,64},{96,112},{112,96},{1... | collective-permute-start | bytes 491528 | tf_op jit(solution)/shard_map/ppermute | solution.py:419
  57.7 0.5 shard_map.41.own_ref
  58.2 0.5 collective-permute-done.3.other_ref
  58.7 0.9 %shard_map.42 = bf16[16,64,128]{2,1,0:T(8,128)(2,1)S(1)} custom-call(bf16[64,128]{1,0:T(8,128)(2,1)S(1)} %get-tuple-element.19.packed_ref, bf16[640,128]{1,0:T(8,128)(2,1)S(1)} %collective-permute-done.3.other_ref, f32[1,72,128]{2,1,0:T(8,128)S(1)} %shard_map.41.own_ref, f32[16,72,128]{2,1,0:T(8,128)S(1)} %shard_map.40.local_ref), custom_call_target="tpu_custom_call" | custom-call | flops 1073741824 | bytes 2097152 | tf_op jit(solution)/shard_map/pallas_call | solution.py:424
  59.7 10.7 %all_to_all.16.in_ref = bf16[16,64,128]{2,1,0:T(8,128)(2,1)S(1)} all-to-all(bf16[16,64,128]{2,1,0:T(8,128)(2,1)S(1)} %shard_map.42), channel_id=1, replica_groups=mesh['seqhi'=32,'seqlo'=16] {'seqlo'}, dimensions={0} | all-to-all | bytes 524288 | tf_op jit(solution)/shard_map/all_to_all | solution.py:428
  70.4 0.8 %shard_map.43 = bf16[128,1024]{1,0:T(8,128)(2,1)} custom-call(bf16[16,64,128]{2,1,0:T(8,128)(2,1)S(1)} %all_to_all.16.in_ref), custom_call_target="tpu_custom_call" | custom-call | flops 4194304 | bytes 524288 | tf_op jit(solution)/shard_map/pallas_call | solution.py:429
  (2 shorter events, 0.0 us)
Async XLA Ops:
  22.2 31.8 %all-to-all-start.1 = ((bf16[16,32,128]{2,1,0:T(8,128)(2,1)}), bf16[16,32,128]{2,1,0:T(8,128)(2,1)S(1)}, u32[]{:S(2)}, u32[]{:S(2)}) async-start(bf16[16,32,128]{2,1,0:T(8,128)(2,1)} %get-tuple-element.20), calls=%async_computation.1 | async-start | bytes 262144 | tf_op jit(solution)/shard_map/all_to_all | solution.py:384
  42.0 10.0 %collective-permute-start.1 = (bf16[11,64,128]{2,1,0:T(8,128)(2,1)S(1)}, bf16[11,64,128]{2,1,0:T(8,128)(2,1)S(1)}, u32[]{:S(2)}, u32[]{:S(2)}) collective-permute-start(bf16[11,64,128]{2,1,0:T(8,128)(2,1)S(1)} %get-tuple-element.23), channel_id=1, source_target_pairs={{16,32},{32,16},{48,64},{64,48},{80,96},{96,80},{112,128},{128,112... | collective-permute-start | bytes 540680 | tf_op jit(solution)/shard_map/ppermute | solution.py:401
  47.5 6.5 %collective-permute-start.2 = (bf16[64,128]{1,0:T(8,128)(2,1)S(1)}, bf16[64,128]{1,0:T(8,128)(2,1)S(1)}, u32[]{:S(2)}, u32[]{:S(2)}) collective-permute-start(bf16[64,128]{1,0:T(8,128)(2,1)S(1)} %get-tuple-element.27.fifth_ref), channel_id=1, source_target_pairs={{0,32},{32,64},{64,96},{96,128},{128,160},{160,192},{192,224},{224... | collective-permute-start | bytes 49160 | tf_op jit(solution)/shard_map/ppermute | solution.py:406
  48.8 3.9 %collective-permute-start = (bf16[5,128,128]{2,1,0:T(8,128)(2,1)S(1)}, bf16[5,128,128]{2,1,0:T(8,128)(2,1)S(1)}, u32[]{:S(2)}, u32[]{:S(2)}) collective-permute-start(bf16[5,128,128]{2,1,0:T(8,128)(2,1)S(1)} %get-tuple-element.22), channel_id=1, source_target_pairs={{0,16},{16,0},{32,48},{48,32},{64,80},{80,64},{96,112},{112,96},{1... | collective-permute-start | bytes 491528 | tf_op jit(solution)/shard_map/ppermute | solution.py:403
  54.0 4.7 %collective-permute-start.3 = (bf16[640,128]{1,0:T(8,128)(2,1)S(1)}, bf16[640,128]{1,0:T(8,128)(2,1)S(1)}, u32[]{:S(2)}, u32[]{:S(2)}) collective-permute-start(bf16[640,128]{1,0:T(8,128)(2,1)S(1)} %pad_maximum_fusion), channel_id=1, source_target_pairs={{0,16},{16,0},{32,48},{48,32},{64,80},{80,64},{96,112},{112,96},{1... | collective-permute-start | bytes 491528 | tf_op jit(solution)/shard_map/ppermute | solution.py:419

commit v5 on v4

--- a/solution.py
+++ b/solution.py
@@ -191,9 +191,7 @@
     return level_zero[i, 128:] if level == 0 else coarse[OFFSET[level] + i]
 
 
-def interior_kernel(
-    x_ref, tiles_ref, fifth_ref, state_ref, coarse_q_ref, packed_ref, inside_ref, outside_ref, score_ref, weight_ref
-):
+def prepare_kernel(x_ref, tiles_ref, fifth_ref, inside_ref, outside_ref, coarse_q_ref, packed_ref):
     first_core = (lax.axis_index("seqhi") & 1) == 0
     for level in range(5):
         first = level_tile(x_ref, tiles_ref, level, 0)[:128]
@@ -220,6 +218,8 @@
             packed = jnp.where(lanes >= PACKED[level], pltpu.roll(wide, PACKED[level], 1), packed)
     packed_ref[...] = packed.astype(jnp.bfloat16)
 
+
+def interior_kernel(x_ref, tiles_ref, coarse_q_ref, state_ref, score_ref, weight_ref):
     tasks, places = [], []
     for level in range(3):
         turned = [level_tile(x_ref, tiles_ref, level, n)[:64].T for n in range(COUNT[level])]
@@ -382,27 +382,33 @@
 
     planes = [[2 * z + core for z in range(outer // 2)] for core in range(2)]
     own = lax.all_to_all(far, "seqhi", 0, 0, axis_index_groups=planes)
-    inner, coarse_q, packed, inside, outside = call(
-        interior_kernel,
+    inside, outside, coarse_q, packed = call(
+        prepare_kernel,
         (
-            shape((STATE_TILES, ROWS, 128), f32),
+            shape((5, 128, 128), bf16),
+            shape((11, 64, 128), bf16),
             shape((15, 64, 128), bf16),
             shape((64, 128), bf16),
-            shape((5, 128, 128), bf16),
-            shape((11, 64, 128), bf16),
         ),
         [VMEM] * 3,
         1 << 20,
         1 << 16,
-        1 << 10,
-        [pltpu.VMEM((22, 384, 128), f32), pltpu.VMEM((22, 384, 128), bf16)],
     )(tokens, tiles, fifth)
     beside = [pair for i in range(1, outer - 1, 2) for pair in ((i, i + 1), (i + 1, i))]
     outside = lax.ppermute(outside, "seqhi", beside)
     cores = [(i, i ^ 1) for i in range(outer)]
     inside = lax.ppermute(inside, "seqhi", cores)
     apart = [(i, i + 2) for i in range(0, outer - 2, 2)] + [(i, i - 2) for i in range(3, outer, 2)]
-    fifth, inner = lax.optimization_barrier((fifth, inner))
+
+    inner = call(
+        interior_kernel,
+        shape((STATE_TILES, ROWS, 128), f32),
+        [VMEM] * 3,
+        1 << 20,
+        1 << 16,
+        1 << 10,
+        [pltpu.VMEM((22, 384, 128), f32), pltpu.VMEM((22, 384, 128), bf16)],
+    )(tokens, tiles, coarse_q)
     beyond = lax.ppermute(fifth, "seqhi", apart)
     local = call(
         edges_kernel,

time: 71.6 us -> 71.6 us (level)
  waiting for transfers between devices: 1.55 us -> 0.56 us
    pallas_call x1 -> x2, Pallas kernels: 2.23 us -> 2.7 us  [the longest x1 1.55 us: body(): call(interior_kernel, shape((STATE_TILES, ROWS, 128), f32), [VMEM] * 3, 1...]
  transfers between devices with their start and end apart: 5 -> 5, of which waited for: 3 -> 1; matrix products, arithmetic and copies ran while one was open for 0% -> 0% of each run, Pallas kernels for 6% -> 6%
where the time goes in v5:
time: 71.6 us; the launch traced here: 71.2 us
  starting transfers between devices  31.5 us (44%)
  blocking collectives  29 us (41%)
  Pallas kernels  10 us (14%)
    all_to_all x1, blocking collectives, body(): tokens = lax.all_to_all(split(key_rows, value_rows, queries), 'seqlo', 0, 0)  18.3 us
    all_to_all x1, starting transfers between devices, body(): own = lax.all_to_all(far, 'seqhi', 0, 0, axis_index_groups=planes)  17.6 us
    all_to_all x1, blocking collectives, body(): heads = lax.all_to_all(out, 'seqlo', 0, 0)  10.7 us
    ppermute x1, starting transfers between devices, body(): outside = lax.ppermute(outside, 'seqhi', beside)  5.45 us
    ppermute x1, starting transfers between devices, body(): lax.ppermute(jnp.concatenate([own, outside[10], beyond], axis=0), 'seqhi'...  4.23 us
    ppermute x1, starting transfers between devices, body(): inside = lax.ppermute(inside, 'seqhi', cores)  2.93 us
    pallas_call x1, Pallas kernels, split(): call(split_kernel, out, [hbm] * 3, 1 << 22, 3 << 19, 0, scratch, 62, hbm)  2.09 us
    pallas_call x1, Pallas kernels, body(): call(coarse_kernel, (shape((16, 32, 128), bf16), shape((64, 128), bf16),...  1.8 us
  transfers between devices with their start and end apart: 5, of which 1 were waited for; matrix products, arithmetic and copies ran while one was open for 0% of the time, Pallas kernels for 6%

profile of v5, /device:TPU:1, one launch (start us, length us, event | category | flops | bytes accessed | tf_op | source)
XLA Modules:
  0.0 71.2 jit_solution(14267748235619049904)
XLA Ops:
  0.0 2.1 %shard_map.37 = bf16[16,192,128]{2,1,0:T(8,128)(2,1)} custom-call(bf16[128,1024]{1,0:T(8,128)(2,1)} %k_ref.1, bf16[128,1024]{1,0:T(8,128)(2,1)} %v_ref.1, bf16[128,1024]{1,0:T(8,128)(2,1)} %q_ref.1), custom_call_target="tpu_custom_call" | custom-call | flops 4194304 | bytes 1572864 | tf_op jit(solution)/shard_map/pallas_call | solution.py:364
  2.1 18.3 %all_to_all.15.x_ref = bf16[16,192,128]{2,1,0:T(8,128)(2,1)S(1)} all-to-all(bf16[16,192,128]{2,1,0:T(8,128)(2,1)} %shard_map.37), channel_id=1, replica_groups=mesh['seqhi'=32,'seqlo'=16] {'seqlo'}, dimensions={0} | all-to-all | bytes 1572864 | tf_op jit(solution)/shard_map/all_to_all | solution.py:372
  20.4 1.8 %shard_map.38 = (bf16[16,32,128]{2,1,0:T(8,128)(2,1)}, bf16[64,128]{1,0:T(8,128)(2,1)S(1)}, bf16[15,128,128]{2,1,0:T(8,128)(2,1)S(1)}) custom-call(bf16[16,192,128]{2,1,0:T(8,128)(2,1)S(1)} %all_to_all.15.x_ref), custom_call_target="tpu_custom_call" | custom-call | flops 134217728 | bytes 2097152 | tf_op jit(solution)/shard_map/pallas_call | solution.py:374
  22.2 17.6 %all-to-all-start.1 = ((bf16[16,32,128]{2,1,0:T(8,128)(2,1)}), bf16[16,32,128]{2,1,0:T(8,128)(2,1)S(1)}, u32[]{:S(2)}, u32[]{:S(2)}) async-start(bf16[16,32,128]{2,1,0:T(8,128)(2,1)} %get-tuple-element.17), calls=%async_computation.1 | async-start | bytes 262144 | tf_op jit(solution)/shard_map/all_to_all | solution.py:384
  39.8 1.1 %shard_map.39 = (bf16[5,128,128]{2,1,0:T(8,128)(2,1)S(1)}, bf16[11,64,128]{2,1,0:T(8,128)(2,1)S(1)}, bf16[15,64,128]{2,1,0:T(8,128)(2,1)S(1)}, bf16[64,128]{1,0:T(8,128)(2,1)S(1)}) custom-call(bf16[16,192,128]{2,1,0:T(8,128)(2,1)S(1)} %all_to_all.15.x_ref, bf16[15,128,128]{2,1,0:T(8,128)(2,1)S(1)} %get-tuple-element.14.tiles_ref, ...), custom_call_target="tpu_custom_call" | custom-call | flops 1048576 | bytes 65536 | tf_op jit(solution)/shard_map/pallas_call | solution.py:385
  40.9 5.4 %collective-permute-start.1 = (bf16[11,64,128]{2,1,0:T(8,128)(2,1)S(1)}, bf16[11,64,128]{2,1,0:T(8,128)(2,1)S(1)}, u32[]{:S(2)}, u32[]{:S(2)}) collective-permute-start(bf16[11,64,128]{2,1,0:T(8,128)(2,1)S(1)} %get-tuple-element.20), channel_id=1, source_target_pairs={{16,32},{32,16},{48,64},{64,48},{80,96},{96,80},{112,128},{128,112... | collective-permute-start | bytes 540680 | tf_op jit(solution)/shard_map/ppermute | solution.py:398
  46.4 1.3 %collective-permute-start.2 = (bf16[64,128]{1,0:T(8,128)(2,1)S(1)}, bf16[64,128]{1,0:T(8,128)(2,1)S(1)}, u32[]{:S(2)}, u32[]{:S(2)}) collective-permute-start(bf16[64,128]{1,0:T(8,128)(2,1)S(1)} %get-tuple-element.15.fifth_ref), channel_id=1, source_target_pairs={{0,32},{32,64},{64,96},{96,128},{128,160},{160,192},{192,224},{224... | collective-permute-start | bytes 49160 | tf_op jit(solution)/shard_map/ppermute | solution.py:412
  47.7 2.9 %collective-permute-start = (bf16[5,128,128]{2,1,0:T(8,128)(2,1)S(1)}, bf16[5,128,128]{2,1,0:T(8,128)(2,1)S(1)}, u32[]{:S(2)}, u32[]{:S(2)}) collective-permute-start(bf16[5,128,128]{2,1,0:T(8,128)(2,1)S(1)} %get-tuple-element.19), channel_id=1, source_target_pairs={{0,16},{16,0},{32,48},{48,32},{64,80},{80,64},{96,112},{112,96},{1... | collective-permute-start | bytes 491528 | tf_op jit(solution)/shard_map/ppermute | solution.py:400
  50.6 1.6 %shard_map.40.inner_ref = f32[28,72,128]{2,1,0:T(8,128)S(1)} custom-call(bf16[16,192,128]{2,1,0:T(8,128)(2,1)S(1)} %all_to_all.15.x_ref, bf16[15,128,128]{2,1,0:T(8,128)(2,1)S(1)} %get-tuple-element.14.tiles_ref, bf16[15,64,128]{2,1,0:T(8,128)(2,1)S(1)} %get-tuple-element.18.coarse_q_ref), custom_call_target="tpu_custom_call" | custom-call | flops 1048576 | bytes 65536 | tf_op jit(solution)/shard_map/pallas_call | solution.py:403
  52.2 0.0 collective-permute-done.1.outside_ref
  52.2 0.0 collective-permute-done.inside_ref
  52.2 1.3 %shard_map.41.local_ref = f32[16,72,128]{2,1,0:T(8,128)S(1)} custom-call(bf16[15,64,128]{2,1,0:T(8,128)(2,1)S(1)} %get-tuple-element.18.coarse_q_ref, bf16[16,192,128]{2,1,0:T(8,128)(2,1)S(1)} %all_to_all.15.x_ref, bf16[15,128,128]{2,1,0:T(8,128)(2,1)S(1)} %get-tuple-element.14.tiles_ref, bf16[5,128,128]{2,1,0:T(8,128)(2,1)S(1)} %collective-permute-done.inside_ref, ...), custom_call_target="tpu_custom_call" | custom-call | flops 1048576 | bytes 65536 | tf_op jit(solution)/shard_map/pallas_call | solution.py:413
  53.5 0.0 all-to-all-done.1
  53.5 0.0 collective-permute-done.2.beyond_ref
  53.5 4.2 %collective-permute-start.3 = (bf16[640,128]{1,0:T(8,128)(2,1)S(1)}, bf16[640,128]{1,0:T(8,128)(2,1)S(1)}, u32[]{:S(2)}, u32[]{:S(2)}) collective-permute-start(bf16[640,128]{1,0:T(8,128)(2,1)S(1)} %pad_maximum_fusion), channel_id=1, source_target_pairs={{0,16},{16,0},{32,48},{48,32},{64,80},{80,64},{96,112},{112,96},{1... | collective-permute-start | bytes 491528 | tf_op jit(solution)/shard_map/ppermute | solution.py:425
  57.7 0.5 shard_map.42.own_ref
  58.2 0.5 collective-permute-done.3.other_ref
  58.7 0.9 %shard_map.43 = bf16[16,64,128]{2,1,0:T(8,128)(2,1)S(1)} custom-call(bf16[64,128]{1,0:T(8,128)(2,1)S(1)} %get-tuple-element.16.packed_ref, bf16[640,128]{1,0:T(8,128)(2,1)S(1)} %collective-permute-done.3.other_ref, f32[1,72,128]{2,1,0:T(8,128)S(1)} %shard_map.42.own_ref, f32[16,72,128]{2,1,0:T(8,128)S(1)} %shard_map.41.local_ref), custom_call_target="tpu_custom_call" | custom-call | flops 1073741824 | bytes 2097152 | tf_op jit(solution)/shard_map/pallas_call | solution.py:430
  59.7 10.7 %all_to_all.16.in_ref = bf16[16,64,128]{2,1,0:T(8,128)(2,1)S(1)} all-to-all(bf16[16,64,128]{2,1,0:T(8,128)(2,1)S(1)} %shard_map.43), channel_id=1, replica_groups=mesh['seqhi'=32,'seqlo'=16] {'seqlo'}, dimensions={0} | all-to-all | bytes 524288 | tf_op jit(solution)/shard_map/all_to_all | solution.py:434
  70.4 0.8 %shard_map.44 = bf16[128,1024]{1,0:T(8,128)(2,1)} custom-call(bf16[16,64,128]{2,1,0:T(8,128)(2,1)S(1)} %all_to_all.16.in_ref), custom_call_target="tpu_custom_call" | custom-call | flops 4194304 | bytes 524288 | tf_op jit(solution)/shard_map/pallas_call | solution.py:435
  (2 shorter events, 0.0 us)
Async XLA Ops:
  22.2 31.3 %all-to-all-start.1 = ((bf16[16,32,128]{2,1,0:T(8,128)(2,1)}), bf16[16,32,128]{2,1,0:T(8,128)(2,1)S(1)}, u32[]{:S(2)}, u32[]{:S(2)}) async-start(bf16[16,32,128]{2,1,0:T(8,128)(2,1)} %get-tuple-element.17), calls=%async_computation.1 | async-start | bytes 262144 | tf_op jit(solution)/shard_map/all_to_all | solution.py:384
  40.9 11.3 %collective-permute-start.1 = (bf16[11,64,128]{2,1,0:T(8,128)(2,1)S(1)}, bf16[11,64,128]{2,1,0:T(8,128)(2,1)S(1)}, u32[]{:S(2)}, u32[]{:S(2)}) collective-permute-start(bf16[11,64,128]{2,1,0:T(8,128)(2,1)S(1)} %get-tuple-element.20), channel_id=1, source_target_pairs={{16,32},{32,16},{48,64},{64,48},{80,96},{96,80},{112,128},{128,112... | collective-permute-start | bytes 540680 | tf_op jit(solution)/shard_map/ppermute | solution.py:398
  46.4 7.1 %collective-permute-start.2 = (bf16[64,128]{1,0:T(8,128)(2,1)S(1)}, bf16[64,128]{1,0:T(8,128)(2,1)S(1)}, u32[]{:S(2)}, u32[]{:S(2)}) collective-permute-start(bf16[64,128]{1,0:T(8,128)(2,1)S(1)} %get-tuple-element.15.fifth_ref), channel_id=1, source_target_pairs={{0,32},{32,64},{64,96},{96,128},{128,160},{160,192},{192,224},{224... | collective-permute-start | bytes 49160 | tf_op jit(solution)/shard_map/ppermute | solution.py:412
  47.7 4.5 %collective-permute-start = (bf16[5,128,128]{2,1,0:T(8,128)(2,1)S(1)}, bf16[5,128,128]{2,1,0:T(8,128)(2,1)S(1)}, u32[]{:S(2)}, u32[]{:S(2)}) collective-permute-start(bf16[5,128,128]{2,1,0:T(8,128)(2,1)S(1)} %get-tuple-element.19), channel_id=1, source_target_pairs={{0,16},{16,0},{32,48},{48,32},{64,80},{80,64},{96,112},{112,96},{1... | collective-permute-start | bytes 491528 | tf_op jit(solution)/shard_map/ppermute | solution.py:400
  53.5 5.2 %collective-permute-start.3 = (bf16[640,128]{1,0:T(8,128)(2,1)S(1)}, bf16[640,128]{1,0:T(8,128)(2,1)S(1)}, u32[]{:S(2)}, u32[]{:S(2)}) collective-permute-start(bf16[640,128]{1,0:T(8,128)(2,1)S(1)} %pad_maximum_fusion), channel_id=1, source_target_pairs={{0,16},{16,0},{32,48},{48,32},{64,80},{80,64},{96,112},{112,96},{1... | collective-permute-start | bytes 491528 | tf_op jit(solution)/shard_map/ppermute | solution.py:425

commit v6 on v5

--- a/solution.py
+++ b/solution.py
@@ -279,7 +279,7 @@
     return jnp.where(lane < 64, 5, jnp.where(lane < 96, 6, jnp.where(lane < 112, 7, 8)))
 
 
-def far_state(plane, query, chunks_ref, near, bias_ref, score_ref):
+def far_scores(plane, query, rows, near, bias_ref, score_ref):
     slot = iota((32, 128), 0)
     lane_level = lane_levels()
     bias_ref[0] = jnp.full((32, 128), NEVER, jnp.float32)
@@ -288,42 +288,49 @@
         bias_ref[level - 5] = jnp.where(held, 0.0, NEVER)
     first_lanes = jnp.where(iota((1, 128), 1) < 64, 0.0, NEVER)
     tall = jnp.concatenate([query, jnp.zeros((64, 128), jnp.bfloat16)], axis=0)
-    rows = jnp.concatenate([chunks_ref[...]] + [tile for tile, _ in near], axis=0)
-    count = rows.shape[0]
-    score_ref[:count] = mm(rows, tall)
+    scores = mm(rows, tall)
     top = None
     for n in range(16 + 2 * len(near)):
         if n < 16:
             bias = bias_ref[needed_level(plane, n) - 5]
         else:
-            bias = first_lanes + jnp.where(near[(n - 16) // 2][1], 0.0, NEVER)
-        part = score_ref[32 * n : 32 * n + 32] + bias
+            bias = first_lanes + jnp.where(near[(n - 16) // 2], 0.0, NEVER)
+        part = scores[32 * n : 32 * n + 32] + bias
         score_ref[32 * n : 32 * n + 32] = part
         high = part.max(axis=0, keepdims=True)
         top = high if top is None else jnp.maximum(top, high)
-    top = top * SCALE
-    grown = jnp.exp2(score_ref[:count] * SCALE - top)
-    total = grown.sum(axis=0, keepdims=True)
+    return top
+
+
+def far_sums(rows, scores, top):
+    grown = jnp.exp2(scores * SCALE - top)
     both = lax.dot_general(
         rows, grown.astype(jnp.bfloat16), (((0,), (0,)), ((), ())), preferred_element_type=jnp.float32
     )
-    return both[64:], top, total
-
-
-def own_kernel(packed_ref, chunks_ref, beyond_ref, state_ref, bias_ref, score_ref):
+    return both[64:], grown.sum(axis=0, keepdims=True)
+
+
+def own_kernel(packed_ref, chunks_ref, beyond_ref, score_ref, top_ref, rows_ref, bias_ref):
     place = lax.axis_index("seqhi")
     toward = jnp.where((place & 1) == 0, place - 2, place + 2)
-    near = [(beyond_ref[...], (toward >= 0) & (toward < lax.axis_size("seqhi")))]
-    put(state_ref, 0, far_state(place >> 1, packed_ref[...], chunks_ref, near, bias_ref, score_ref))
-
-
-def final_kernel(packed_ref, other_ref, own_ref, local_ref, out_ref, bias_ref, score_ref):
+    near = [(toward >= 0) & (toward < lax.axis_size("seqhi"))]
+    rows_ref[:512] = chunks_ref[...]
+    rows_ref[512:] = beyond_ref[...]
+    top = far_scores(place >> 1, packed_ref[...], rows_ref[...], near, bias_ref, score_ref)
+    top_ref[...] = jnp.broadcast_to(top, (8, 128))
+
+
+def final_kernel(
+    packed_ref, other_ref, own_score_ref, own_top_ref, own_rows_ref, local_ref, out_ref, bias_ref, score_ref
+):
     place = lax.axis_index("seqhi")
     toward = jnp.where((place & 1) == 0, place + 2, place - 2)
     here = (toward >= 0) & (toward < lax.axis_size("seqhi"))
-    near = [(other_ref[512:576], here), (other_ref[576:], here)]
-    state = far_state(place >> 1, packed_ref[...], other_ref.at[:512], near, bias_ref, score_ref)
-    numer, top, total = merge(state, get(own_ref, 0))
+    top = far_scores(place >> 1, packed_ref[...], other_ref[...], [here, here], bias_ref, score_ref)
+    top = jnp.maximum(top, own_top_ref[:1]) * SCALE
+    own_numer, own_total = far_sums(own_rows_ref[...], own_score_ref[...], top)
+    numer, total = far_sums(other_ref[...], score_ref[...], top)
+    numer, total = numer + own_numer, total + own_total
     row = lane_levels()[:1]
     times = jnp.where(row == 5, 32.0, jnp.where(row == 6, 64.0, jnp.where(row == 7, 128.0, 256.0)))
     packed = (numer * times, top, total * times)
@@ -424,12 +431,18 @@
     own = own.reshape(512, 128)
     other = lax.ppermute(jnp.concatenate([own, outside[10], beyond], axis=0), "seqhi", cores)
     scratch = [pltpu.VMEM((4, 32, 128), f32), pltpu.VMEM((640, 128), f32)]
-    own_state = call(
-        own_kernel, shape((1, ROWS, 128), f32), [VMEM] * 3, 1 << 30, 1 << 20, 1 << 17, scratch
+    own_far = call(
+        own_kernel,
+        (shape((576, 128), f32), shape((8, 128), f32), shape((576, 128), bf16)),
+        [VMEM] * 3,
+        1 << 30,
+        1 << 20,
+        1 << 17,
+        scratch[:1],
     )(packed, own, beyond)
     out = call(
-        final_kernel, shape((TILES, HEAD, 128), bf16), [VMEM] * 4, 1 << 30, 2 << 20, 1 << 17, scratch
-    )(packed, other, own_state, local)
+        final_kernel, shape((TILES, HEAD, 128), bf16), [VMEM] * 6, 1 << 30, 2 << 20, 1 << 17, scratch
+    )(packed, other, *own_far, local)
 
     heads = lax.all_to_all(out, "seqlo", 0, 0)
     return call(join_kernel, shape((128, HEADS * HEAD), bf16), [VMEM], 1 << 22, 1 << 19)(heads)

time: 71.6 us -> 71.7 us (level)
  no operation moved by 1% of the time
where the time goes in v6:
time: 71.7 us; the launch traced here: 71.3 us
  starting transfers between devices  31.5 us (44%)
  blocking collectives  29 us (40%)
  Pallas kernels  9.86 us (14%)
  waiting for transfers between devices  0.83 us (1%)
    all_to_all x1, blocking collectives, body(): tokens = lax.all_to_all(split(key_rows, value_rows, queries), 'seqlo', 0, 0)  18.3 us
    all_to_all x1, starting transfers between devices, body(): own = lax.all_to_all(far, 'seqhi', 0, 0, axis_index_groups=planes)  17.6 us
    all_to_all x1, blocking collectives, body(): heads = lax.all_to_all(out, 'seqlo', 0, 0)  10.7 us
    ppermute x1, starting transfers between devices, body(): outside = lax.ppermute(outside, 'seqhi', beside)  5.44 us
    ppermute x1, starting transfers between devices, body(): lax.ppermute(jnp.concatenate([own, outside[10], beyond], axis=0), 'seqhi'...  4.24 us
    ppermute x1, starting transfers between devices, body(): inside = lax.ppermute(inside, 'seqhi', cores)  2.93 us
    pallas_call x1, Pallas kernels, split(): call(split_kernel, out, [hbm] * 3, 1 << 22, 3 << 19, 0, scratch, 62, hbm)  2.09 us
    pallas_call x1, Pallas kernels, body(): call(coarse_kernel, (shape((16, 32, 128), bf16), shape((64, 128), bf16),...  1.81 us
  transfers between devices with their start and end apart: 5, of which 1 were waited for; matrix products, arithmetic and copies ran while one was open for 0% of the time, Pallas kernels for 6%

profile of v6, /device:TPU:1, one launch (start us, length us, event | category | flops | bytes accessed | tf_op | source)
XLA Modules:
  0.0 71.3 jit_solution(9790964765748520261)
XLA Ops:
  0.0 2.1 %shard_map.37 = bf16[16,192,128]{2,1,0:T(8,128)(2,1)} custom-call(bf16[128,1024]{1,0:T(8,128)(2,1)} %k_ref.1, bf16[128,1024]{1,0:T(8,128)(2,1)} %v_ref.1, bf16[128,1024]{1,0:T(8,128)(2,1)} %q_ref.1), custom_call_target="tpu_custom_call" | custom-call | flops 4194304 | bytes 1572864 | tf_op jit(solution)/shard_map/pallas_call | solution.py:371
  2.1 18.3 %all_to_all.15.x_ref = bf16[16,192,128]{2,1,0:T(8,128)(2,1)S(1)} all-to-all(bf16[16,192,128]{2,1,0:T(8,128)(2,1)} %shard_map.37), channel_id=1, replica_groups=mesh['seqhi'=32,'seqlo'=16] {'seqlo'}, dimensions={0} | all-to-all | bytes 1572864 | tf_op jit(solution)/shard_map/all_to_all | solution.py:379
  20.4 1.8 %shard_map.38 = (bf16[16,32,128]{2,1,0:T(8,128)(2,1)}, bf16[64,128]{1,0:T(8,128)(2,1)S(1)}, bf16[15,128,128]{2,1,0:T(8,128)(2,1)S(1)}) custom-call(bf16[16,192,128]{2,1,0:T(8,128)(2,1)S(1)} %all_to_all.15.x_ref), custom_call_target="tpu_custom_call" | custom-call | flops 134217728 | bytes 2097152 | tf_op jit(solution)/shard_map/pallas_call | solution.py:381
  22.2 17.6 %all-to-all-start.1 = ((bf16[16,32,128]{2,1,0:T(8,128)(2,1)}), bf16[16,32,128]{2,1,0:T(8,128)(2,1)S(1)}, u32[]{:S(2)}, u32[]{:S(2)}) async-start(bf16[16,32,128]{2,1,0:T(8,128)(2,1)} %get-tuple-element.20), calls=%async_computation.1 | async-start | bytes 262144 | tf_op jit(solution)/shard_map/all_to_all | solution.py:391
  39.8 1.1 %shard_map.39 = (bf16[5,128,128]{2,1,0:T(8,128)(2,1)S(1)}, bf16[11,64,128]{2,1,0:T(8,128)(2,1)S(1)}, bf16[15,64,128]{2,1,0:T(8,128)(2,1)S(1)}, bf16[64,128]{1,0:T(8,128)(2,1)S(1)}) custom-call(bf16[16,192,128]{2,1,0:T(8,128)(2,1)S(1)} %all_to_all.15.x_ref, bf16[15,128,128]{2,1,0:T(8,128)(2,1)S(1)} %get-tuple-element.17.tiles_ref, ...), custom_call_target="tpu_custom_call" | custom-call | flops 1048576 | bytes 65536 | tf_op jit(solution)/shard_map/pallas_call | solution.py:392
  40.9 5.4 %collective-permute-start.1 = (bf16[11,64,128]{2,1,0:T(8,128)(2,1)S(1)}, bf16[11,64,128]{2,1,0:T(8,128)(2,1)S(1)}, u32[]{:S(2)}, u32[]{:S(2)}) collective-permute-start(bf16[11,64,128]{2,1,0:T(8,128)(2,1)S(1)} %get-tuple-element.23), channel_id=1, source_target_pairs={{16,32},{32,16},{48,64},{64,48},{80,96},{96,80},{112,128},{128,112... | collective-permute-start | bytes 540680 | tf_op jit(solution)/shard_map/ppermute | solution.py:405
  46.4 1.3 %collective-permute-start.2 = (bf16[64,128]{1,0:T(8,128)(2,1)S(1)}, bf16[64,128]{1,0:T(8,128)(2,1)S(1)}, u32[]{:S(2)}, u32[]{:S(2)}) collective-permute-start(bf16[64,128]{1,0:T(8,128)(2,1)S(1)} %get-tuple-element.18.fifth_ref), channel_id=1, source_target_pairs={{0,32},{32,64},{64,96},{96,128},{128,160},{160,192},{192,224},{224... | collective-permute-start | bytes 49160 | tf_op jit(solution)/shard_map/ppermute | solution.py:419
  47.7 2.9 %collective-permute-start = (bf16[5,128,128]{2,1,0:T(8,128)(2,1)S(1)}, bf16[5,128,128]{2,1,0:T(8,128)(2,1)S(1)}, u32[]{:S(2)}, u32[]{:S(2)}) collective-permute-start(bf16[5,128,128]{2,1,0:T(8,128)(2,1)S(1)} %get-tuple-element.22), channel_id=1, source_target_pairs={{0,16},{16,0},{32,48},{48,32},{64,80},{80,64},{96,112},{112,96},{1... | collective-permute-start | bytes 491528 | tf_op jit(solution)/shard_map/ppermute | solution.py:407
  50.6 1.6 %shard_map.40.inner_ref = f32[28,72,128]{2,1,0:T(8,128)S(1)} custom-call(bf16[16,192,128]{2,1,0:T(8,128)(2,1)S(1)} %all_to_all.15.x_ref, bf16[15,128,128]{2,1,0:T(8,128)(2,1)S(1)} %get-tuple-element.17.tiles_ref, bf16[15,64,128]{2,1,0:T(8,128)(2,1)S(1)} %get-tuple-element.21.coarse_q_ref), custom_call_target="tpu_custom_call" | custom-call | flops 1048576 | bytes 65536 | tf_op jit(solution)/shard_map/pallas_call | solution.py:410
  52.2 0.0 collective-permute-done.1.outside_ref
  52.2 0.0 collective-permute-done.inside_ref
  52.2 1.3 %shard_map.41.local_ref = f32[16,72,128]{2,1,0:T(8,128)S(1)} custom-call(bf16[15,64,128]{2,1,0:T(8,128)(2,1)S(1)} %get-tuple-element.21.coarse_q_ref, bf16[16,192,128]{2,1,0:T(8,128)(2,1)S(1)} %all_to_all.15.x_ref, bf16[15,128,128]{2,1,0:T(8,128)(2,1)S(1)} %get-tuple-element.17.tiles_ref, bf16[5,128,128]{2,1,0:T(8,128)(2,1)S(1)} %collective-permute-done.inside_ref, ...), custom_call_target="tpu_custom_call" | custom-call | flops 1048576 | bytes 65536 | tf_op jit(solution)/shard_map/pallas_call | solution.py:420
  53.5 0.0 all-to-all-done.1
  53.5 0.0 collective-permute-done.2.beyond_ref
  53.5 4.2 %collective-permute-start.3 = (bf16[640,128]{1,0:T(8,128)(2,1)S(1)}, bf16[640,128]{1,0:T(8,128)(2,1)S(1)}, u32[]{:S(2)}, u32[]{:S(2)}) collective-permute-start(bf16[640,128]{1,0:T(8,128)(2,1)S(1)} %pad_maximum_fusion), channel_id=1, source_target_pairs={{0,16},{16,0},{32,48},{48,32},{64,80},{80,64},{96,112},{112,96},{1... | collective-permute-start | bytes 491528 | tf_op jit(solution)/shard_map/ppermute | solution.py:432
  57.7 0.2 shard_map.42
  57.9 0.8 %collective-permute-done.3.other_ref = bf16[640,128]{1,0:T(8,128)(2,1)S(1)} collective-permute-done((bf16[640,128]{1,0:T(8,128)(2,1)S(1)}, bf16[640,128]{1,0:T(8,128)(2,1)S(1)}, u32[]{:S(2)}, u32[]{:S(2)}) %collective-permute-start.3) | collective-permute-done | bytes 163872 | tf_op jit(solution)/shard_map/ppermute | solution.py:432
  58.8 1.0 %shard_map.43 = bf16[16,64,128]{2,1,0:T(8,128)(2,1)S(1)} custom-call(bf16[64,128]{1,0:T(8,128)(2,1)S(1)} %get-tuple-element.19.packed_ref, bf16[640,128]{1,0:T(8,128)(2,1)S(1)} %collective-permute-done.3.other_ref, f32[576,128]{1,0:T(8,128)S(1)} %get-tuple-element.25.own_score_ref, f32[8,128]{1,0:T(8,128)S(1)} %get-tuple-element.26.own_top_ref, ...), custom_call_target="tpu_custom_call" | custom-call | flops 1073741824 | bytes 2097152 | tf_op jit(solution)/shard_map/pallas_call | solution.py:443
  59.8 10.7 %all_to_all.16.in_ref = bf16[16,64,128]{2,1,0:T(8,128)(2,1)S(1)} all-to-all(bf16[16,64,128]{2,1,0:T(8,128)(2,1)S(1)} %shard_map.43), channel_id=1, replica_groups=mesh['seqhi'=32,'seqlo'=16] {'seqlo'}, dimensions={0} | all-to-all | bytes 524288 | tf_op jit(solution)/shard_map/all_to_all | solution.py:447
  70.5 0.8 %shard_map.44 = bf16[128,1024]{1,0:T(8,128)(2,1)} custom-call(bf16[16,64,128]{2,1,0:T(8,128)(2,1)S(1)} %all_to_all.16.in_ref), custom_call_target="tpu_custom_call" | custom-call | flops 4194304 | bytes 524288 | tf_op jit(solution)/shard_map/pallas_call | solution.py:448
  (2 shorter events, 0.0 us)
Async XLA Ops:
  22.2 31.3 %all-to-all-start.1 = ((bf16[16,32,128]{2,1,0:T(8,128)(2,1)}), bf16[16,32,128]{2,1,0:T(8,128)(2,1)S(1)}, u32[]{:S(2)}, u32[]{:S(2)}) async-start(bf16[16,32,128]{2,1,0:T(8,128)(2,1)} %get-tuple-element.20), calls=%async_computation.1 | async-start | bytes 262144 | tf_op jit(solution)/shard_map/all_to_all | solution.py:391
  40.9 11.2 %collective-permute-start.1 = (bf16[11,64,128]{2,1,0:T(8,128)(2,1)S(1)}, bf16[11,64,128]{2,1,0:T(8,128)(2,1)S(1)}, u32[]{:S(2)}, u32[]{:S(2)}) collective-permute-start(bf16[11,64,128]{2,1,0:T(8,128)(2,1)S(1)} %get-tuple-element.23), channel_id=1, source_target_pairs={{16,32},{32,16},{48,64},{64,48},{80,96},{96,80},{112,128},{128,112... | collective-permute-start | bytes 540680 | tf_op jit(solution)/shard_map/ppermute | solution.py:405
  46.4 7.1 %collective-permute-start.2 = (bf16[64,128]{1,0:T(8,128)(2,1)S(1)}, bf16[64,128]{1,0:T(8,128)(2,1)S(1)}, u32[]{:S(2)}, u32[]{:S(2)}) collective-permute-start(bf16[64,128]{1,0:T(8,128)(2,1)S(1)} %get-tuple-element.18.fifth_ref), channel_id=1, source_target_pairs={{0,32},{32,64},{64,96},{96,128},{128,160},{160,192},{192,224},{224... | collective-permute-start | bytes 49160 | tf_op jit(solution)/shard_map/ppermute | solution.py:419
  47.7 4.5 %collective-permute-start = (bf16[5,128,128]{2,1,0:T(8,128)(2,1)S(1)}, bf16[5,128,128]{2,1,0:T(8,128)(2,1)S(1)}, u32[]{:S(2)}, u32[]{:S(2)}) collective-permute-start(bf16[5,128,128]{2,1,0:T(8,128)(2,1)S(1)} %get-tuple-element.22), channel_id=1, source_target_pairs={{0,16},{16,0},{32,48},{48,32},{64,80},{80,64},{96,112},{112,96},{1... | collective-permute-start | bytes 491528 | tf_op jit(solution)/shard_map/ppermute | solution.py:407
  53.5 5.2 %collective-permute-start.3 = (bf16[640,128]{1,0:T(8,128)(2,1)S(1)}, bf16[640,128]{1,0:T(8,128)(2,1)S(1)}, u32[]{:S(2)}, u32[]{:S(2)}) collective-permute-start(bf16[640,128]{1,0:T(8,128)(2,1)S(1)} %pad_maximum_fusion), channel_id=1, source_target_pairs={{0,16},{16,0},{32,48},{48,32},{64,80},{80,64},{96,112},{112,96},{1... | collective-permute-start | bytes 491528 | tf_op jit(solution)/shard_map/ppermute | solution.py:432

commit v7 on v6

--- a/solution.py
+++ b/solution.py
@@ -48,10 +48,18 @@
         out.wait()
 
 
-def join_kernel(in_ref, out_ref):
-    for pair in range(HEADS // 2):
-        both = jnp.concatenate([in_ref[2 * pair], in_ref[2 * pair + 1]], axis=0)
-        out_ref[:, 128 * pair : 128 * pair + 128] = both.T
+def join_kernel(in_ref, out_ref, held, sems):
+    sent = []
+    for half in range(2):
+        for pair in range(4 * half, 4 * half + 4):
+            both = jnp.concatenate([in_ref[2 * pair], in_ref[2 * pair + 1]], axis=0)
+            held[:, 128 * pair : 128 * pair + 128] = both.T
+        columns = pl.ds(512 * half, 512)
+        copy = pltpu.make_async_copy(held.at[:, columns], out_ref.at[:, columns], sems.at[half])
+        copy.start()
+        sent.append(copy)
+    for copy in sent:
+        copy.wait()
 
 
 def halving():
@@ -445,7 +453,9 @@
     )(packed, other, *own_far, local)
 
     heads = lax.all_to_all(out, "seqlo", 0, 0)
-    return call(join_kernel, shape((128, HEADS * HEAD), bf16), [VMEM], 1 << 22, 1 << 19)(heads)
+    scratch = [pltpu.VMEM((128, HEADS * HEAD), bf16), pltpu.SemaphoreType.DMA((2,))]
+    hbm = pl.BlockSpec(memory_space=pltpu.HBM)
+    return call(join_kernel, shape((128, HEADS * HEAD), bf16), [VMEM], 1 << 22, 1 << 19, 0, scratch, 24, hbm)(heads)
 
 
 def solution(mesh):

time: 71.7 us -> 71.7 us (level)
  no operation moved by 1% of the time
where the time goes in v7:
time: 71.7 us; the launch traced here: 71.3 us
  starting transfers between devices  31.5 us (44%)
  blocking collectives  29 us (40%)
  Pallas kernels  9.84 us (14%)
  waiting for transfers between devices  0.83 us (1%)
    all_to_all x1, blocking collectives, body(): tokens = lax.all_to_all(split(key_rows, value_rows, queries), 'seqlo', 0, 0)  18.3 us
    all_to_all x1, starting transfers between devices, body(): own = lax.all_to_all(far, 'seqhi', 0, 0, axis_index_groups=planes)  17.6 us
    all_to_all x1, blocking collectives, body(): heads = lax.all_to_all(out, 'seqlo', 0, 0)  10.7 us
    ppermute x1, starting transfers between devices, body(): outside = lax.ppermute(outside, 'seqhi', beside)  5.44 us
    ppermute x1, starting transfers between devices, body(): lax.ppermute(jnp.concatenate([own, outside[10], beyond], axis=0), 'seqhi'...  4.24 us
    ppermute x1, starting transfers between devices, body(): inside = lax.ppermute(inside, 'seqhi', cores)  2.93 us
    pallas_call x1, Pallas kernels, split(): call(split_kernel, out, [hbm] * 3, 1 << 22, 3 << 19, 0, scratch, 62, hbm)  2.09 us
    pallas_call x1, Pallas kernels, body(): call(coarse_kernel, (shape((16, 32, 128), bf16), shape((64, 128), bf16),...  1.81 us
  transfers between devices with their start and end apart: 5, of which 1 were waited for; matrix products, arithmetic and copies ran while one was open for 0% of the time, Pallas kernels for 6%

profile of v7, /device:TPU:1, one launch (start us, length us, event | category | flops | bytes accessed | tf_op | source)
XLA Modules:
  0.0 71.3 jit_solution(15023354969102552683)
XLA Ops:
  0.0 2.1 %shard_map.37 = bf16[16,192,128]{2,1,0:T(8,128)(2,1)} custom-call(bf16[128,1024]{1,0:T(8,128)(2,1)} %k_ref.1, bf16[128,1024]{1,0:T(8,128)(2,1)} %v_ref.1, bf16[128,1024]{1,0:T(8,128)(2,1)} %q_ref.1), custom_call_target="tpu_custom_call" | custom-call | flops 4194304 | bytes 1572864 | tf_op jit(solution)/shard_map/pallas_call | solution.py:379
  2.1 18.3 %all_to_all.15.x_ref = bf16[16,192,128]{2,1,0:T(8,128)(2,1)S(1)} all-to-all(bf16[16,192,128]{2,1,0:T(8,128)(2,1)} %shard_map.37), channel_id=1, replica_groups=mesh['seqhi'=32,'seqlo'=16] {'seqlo'}, dimensions={0} | all-to-all | bytes 1572864 | tf_op jit(solution)/shard_map/all_to_all | solution.py:387
  20.4 1.8 %shard_map.38 = (bf16[16,32,128]{2,1,0:T(8,128)(2,1)}, bf16[64,128]{1,0:T(8,128)(2,1)S(1)}, bf16[15,128,128]{2,1,0:T(8,128)(2,1)S(1)}) custom-call(bf16[16,192,128]{2,1,0:T(8,128)(2,1)S(1)} %all_to_all.15.x_ref), custom_call_target="tpu_custom_call" | custom-call | flops 134217728 | bytes 2097152 | tf_op jit(solution)/shard_map/pallas_call | solution.py:389
  22.2 17.6 %all-to-all-start.1 = ((bf16[16,32,128]{2,1,0:T(8,128)(2,1)}), bf16[16,32,128]{2,1,0:T(8,128)(2,1)S(1)}, u32[]{:S(2)}, u32[]{:S(2)}) async-start(bf16[16,32,128]{2,1,0:T(8,128)(2,1)} %get-tuple-element.20), calls=%async_computation.1 | async-start | bytes 262144 | tf_op jit(solution)/shard_map/all_to_all | solution.py:399
  39.8 1.1 %shard_map.39 = (bf16[5,128,128]{2,1,0:T(8,128)(2,1)S(1)}, bf16[11,64,128]{2,1,0:T(8,128)(2,1)S(1)}, bf16[15,64,128]{2,1,0:T(8,128)(2,1)S(1)}, bf16[64,128]{1,0:T(8,128)(2,1)S(1)}) custom-call(bf16[16,192,128]{2,1,0:T(8,128)(2,1)S(1)} %all_to_all.15.x_ref, bf16[15,128,128]{2,1,0:T(8,128)(2,1)S(1)} %get-tuple-element.17.tiles_ref, ...), custom_call_target="tpu_custom_call" | custom-call | flops 1048576 | bytes 65536 | tf_op jit(solution)/shard_map/pallas_call | solution.py:400
  40.9 5.4 %collective-permute-start.1 = (bf16[11,64,128]{2,1,0:T(8,128)(2,1)S(1)}, bf16[11,64,128]{2,1,0:T(8,128)(2,1)S(1)}, u32[]{:S(2)}, u32[]{:S(2)}) collective-permute-start(bf16[11,64,128]{2,1,0:T(8,128)(2,1)S(1)} %get-tuple-element.23), channel_id=1, source_target_pairs={{16,32},{32,16},{48,64},{64,48},{80,96},{96,80},{112,128},{128,112... | collective-permute-start | bytes 540680 | tf_op jit(solution)/shard_map/ppermute | solution.py:413
  46.4 1.3 %collective-permute-start.2 = (bf16[64,128]{1,0:T(8,128)(2,1)S(1)}, bf16[64,128]{1,0:T(8,128)(2,1)S(1)}, u32[]{:S(2)}, u32[]{:S(2)}) collective-permute-start(bf16[64,128]{1,0:T(8,128)(2,1)S(1)} %get-tuple-element.18.fifth_ref), channel_id=1, source_target_pairs={{0,32},{32,64},{64,96},{96,128},{128,160},{160,192},{192,224},{224... | collective-permute-start | bytes 49160 | tf_op jit(solution)/shard_map/ppermute | solution.py:427
  47.7 2.9 %collective-permute-start = (bf16[5,128,128]{2,1,0:T(8,128)(2,1)S(1)}, bf16[5,128,128]{2,1,0:T(8,128)(2,1)S(1)}, u32[]{:S(2)}, u32[]{:S(2)}) collective-permute-start(bf16[5,128,128]{2,1,0:T(8,128)(2,1)S(1)} %get-tuple-element.22), channel_id=1, source_target_pairs={{0,16},{16,0},{32,48},{48,32},{64,80},{80,64},{96,112},{112,96},{1... | collective-permute-start | bytes 491528 | tf_op jit(solution)/shard_map/ppermute | solution.py:415
  50.6 1.6 %shard_map.40.inner_ref = f32[28,72,128]{2,1,0:T(8,128)S(1)} custom-call(bf16[16,192,128]{2,1,0:T(8,128)(2,1)S(1)} %all_to_all.15.x_ref, bf16[15,128,128]{2,1,0:T(8,128)(2,1)S(1)} %get-tuple-element.17.tiles_ref, bf16[15,64,128]{2,1,0:T(8,128)(2,1)S(1)} %get-tuple-element.21.coarse_q_ref), custom_call_target="tpu_custom_call" | custom-call | flops 1048576 | bytes 65536 | tf_op jit(solution)/shard_map/pallas_call | solution.py:418
  52.2 0.0 collective-permute-done.1.outside_ref
  52.2 0.0 collective-permute-done.inside_ref
  52.2 1.3 %shard_map.41.local_ref = f32[16,72,128]{2,1,0:T(8,128)S(1)} custom-call(bf16[15,64,128]{2,1,0:T(8,128)(2,1)S(1)} %get-tuple-element.21.coarse_q_ref, bf16[16,192,128]{2,1,0:T(8,128)(2,1)S(1)} %all_to_all.15.x_ref, bf16[15,128,128]{2,1,0:T(8,128)(2,1)S(1)} %get-tuple-element.17.tiles_ref, bf16[5,128,128]{2,1,0:T(8,128)(2,1)S(1)} %collective-permute-done.inside_ref, ...), custom_call_target="tpu_custom_call" | custom-call | flops 1048576 | bytes 65536 | tf_op jit(solution)/shard_map/pallas_call | solution.py:428
  53.5 0.0 all-to-all-done.1
  53.5 0.0 collective-permute-done.2.beyond_ref
  53.5 4.2 %collective-permute-start.3 = (bf16[640,128]{1,0:T(8,128)(2,1)S(1)}, bf16[640,128]{1,0:T(8,128)(2,1)S(1)}, u32[]{:S(2)}, u32[]{:S(2)}) collective-permute-start(bf16[640,128]{1,0:T(8,128)(2,1)S(1)} %pad_maximum_fusion), channel_id=1, source_target_pairs={{0,16},{16,0},{32,48},{48,32},{64,80},{80,64},{96,112},{112,96},{1... | collective-permute-start | bytes 491528 | tf_op jit(solution)/shard_map/ppermute | solution.py:440
  57.7 0.2 shard_map.42
  57.9 0.8 %collective-permute-done.3.other_ref = bf16[640,128]{1,0:T(8,128)(2,1)S(1)} collective-permute-done((bf16[640,128]{1,0:T(8,128)(2,1)S(1)}, bf16[640,128]{1,0:T(8,128)(2,1)S(1)}, u32[]{:S(2)}, u32[]{:S(2)}) %collective-permute-start.3) | collective-permute-done | bytes 163872 | tf_op jit(solution)/shard_map/ppermute | solution.py:440
  58.8 1.0 %shard_map.43 = bf16[16,64,128]{2,1,0:T(8,128)(2,1)S(1)} custom-call(bf16[64,128]{1,0:T(8,128)(2,1)S(1)} %get-tuple-element.19.packed_ref, bf16[640,128]{1,0:T(8,128)(2,1)S(1)} %collective-permute-done.3.other_ref, f32[576,128]{1,0:T(8,128)S(1)} %get-tuple-element.25.own_score_ref, f32[8,128]{1,0:T(8,128)S(1)} %get-tuple-element.26.own_top_ref, ...), custom_call_target="tpu_custom_call" | custom-call | flops 1073741824 | bytes 2097152 | tf_op jit(solution)/shard_map/pallas_call | solution.py:451
  59.8 10.7 %all_to_all.16.in_ref = bf16[16,64,128]{2,1,0:T(8,128)(2,1)S(1)} all-to-all(bf16[16,64,128]{2,1,0:T(8,128)(2,1)S(1)} %shard_map.43), channel_id=1, replica_groups=mesh['seqhi'=32,'seqlo'=16] {'seqlo'}, dimensions={0} | all-to-all | bytes 524288 | tf_op jit(solution)/shard_map/all_to_all | solution.py:455
  70.5 0.8 %shard_map.44 = bf16[128,1024]{1,0:T(8,128)(2,1)} custom-call(bf16[16,64,128]{2,1,0:T(8,128)(2,1)S(1)} %all_to_all.16.in_ref), custom_call_target="tpu_custom_call" | custom-call | flops 4194304 | bytes 524288 | tf_op jit(solution)/shard_map/pallas_call | solution.py:458
  (2 shorter events, 0.0 us)
Async XLA Ops:
  22.2 31.3 %all-to-all-start.1 = ((bf16[16,32,128]{2,1,0:T(8,128)(2,1)}), bf16[16,32,128]{2,1,0:T(8,128)(2,1)S(1)}, u32[]{:S(2)}, u32[]{:S(2)}) async-start(bf16[16,32,128]{2,1,0:T(8,128)(2,1)} %get-tuple-element.20), calls=%async_computation.1 | async-start | bytes 262144 | tf_op jit(solution)/shard_map/all_to_all | solution.py:399
  40.9 11.2 %collective-permute-start.1 = (bf16[11,64,128]{2,1,0:T(8,128)(2,1)S(1)}, bf16[11,64,128]{2,1,0:T(8,128)(2,1)S(1)}, u32[]{:S(2)}, u32[]{:S(2)}) collective-permute-start(bf16[11,64,128]{2,1,0:T(8,128)(2,1)S(1)} %get-tuple-element.23), channel_id=1, source_target_pairs={{16,32},{32,16},{48,64},{64,48},{80,96},{96,80},{112,128},{128,112... | collective-permute-start | bytes 540680 | tf_op jit(solution)/shard_map/ppermute | solution.py:413
  46.4 7.1 %collective-permute-start.2 = (bf16[64,128]{1,0:T(8,128)(2,1)S(1)}, bf16[64,128]{1,0:T(8,128)(2,1)S(1)}, u32[]{:S(2)}, u32[]{:S(2)}) collective-permute-start(bf16[64,128]{1,0:T(8,128)(2,1)S(1)} %get-tuple-element.18.fifth_ref), channel_id=1, source_target_pairs={{0,32},{32,64},{64,96},{96,128},{128,160},{160,192},{192,224},{224... | collective-permute-start | bytes 49160 | tf_op jit(solution)/shard_map/ppermute | solution.py:427
  47.7 4.5 %collective-permute-start = (bf16[5,128,128]{2,1,0:T(8,128)(2,1)S(1)}, bf16[5,128,128]{2,1,0:T(8,128)(2,1)S(1)}, u32[]{:S(2)}, u32[]{:S(2)}) collective-permute-start(bf16[5,128,128]{2,1,0:T(8,128)(2,1)S(1)} %get-tuple-element.22), channel_id=1, source_target_pairs={{0,16},{16,0},{32,48},{48,32},{64,80},{80,64},{96,112},{112,96},{1... | collective-permute-start | bytes 491528 | tf_op jit(solution)/shard_map/ppermute | solution.py:415
  53.5 5.2 %collective-permute-start.3 = (bf16[640,128]{1,0:T(8,128)(2,1)S(1)}, bf16[640,128]{1,0:T(8,128)(2,1)S(1)}, u32[]{:S(2)}, u32[]{:S(2)}) collective-permute-start(bf16[640,128]{1,0:T(8,128)(2,1)S(1)} %pad_maximum_fusion), channel_id=1, source_target_pairs={{0,16},{16,0},{32,48},{48,32},{64,80},{80,64},{96,112},{112,96},{1... | collective-permute-start | bytes 491528 | tf_op jit(solution)/shard_map/ppermute | solution.py:440
